TPU v7x, 32 devices: a whole 2x2x4 slice. The times are simulated.
32 devices in a mesh: seq: 8 (over z, x), head: 4 (over y, core).
Axes of the slice: x: 2, y: 2, z: 4, core: 2. Of those that a mesh axis runs over, the one named last changes fastest.
Arguments:
- hidden_states: bfloat16 [4096, 2048], P('seq', 'head'), may hold values from -7 to 7
- proj_ba: bfloat16 [2048, 64], P('head'), may hold values from -0.125 to 0.125
- query_in: bfloat16 [4096, 2048], P('seq', 'head'), may hold values from -6 to 6
- key_in: bfloat16 [4096, 2048], P('seq', 'head'), may hold values from -6 to 6
- value_in: bfloat16 [4096, 4096], P('seq', 'head'), may hold values from -6 to 6
- conv_query: bfloat16 [4, 2048], P(None, 'head'), may hold values from -2 to 2
- conv_key: bfloat16 [4, 2048], P(None, 'head'), may hold values from -2 to 2
- convolution_value_taps: bfloat16 [4, 4096], P(None, 'head'), may hold values from -2.5 to 2.5
- decay_scale: float32 [32], P('head'), may hold values from 1 to 16
- dt_bias: float32 [32], P('head'), may hold values from -30 to -2
Outputs:
- layer_output: float32 [4096, 4096], P('seq', 'head')
All inputs are finite; a program needn't handle non-finite values.
Results may differ from a plain program's by a relative error of at most 0.0003.
Values may be sent and summed in bfloat16 or wider, within the bound.
No kernel may reach another device: no remote copies, remote signals or barrier semaphores. Data moves between devices by JAX's collectives and lax.ppermute only.
A program may use at most 128 MiB of HBM per device.

v0:
```python
import math

import jax
import jax.numpy as jnp
from jax import lax
from jax.sharding import PartitionSpec as P

DK = 128
DV = 128
KCONV = 4
BLOCK = 128


highest = lax.Precision.HIGHEST


def passed_along(block, axis, distance):
    devices = range(lax.axis_size(axis))
    route = [(i - distance, i) for i in devices if i - distance in devices]
    return lax.ppermute(block, axis, route)


def carried_in(array, axis, combine, identity):
    count, place = (lax.axis_size(axis), lax.axis_index(axis))
    everything = jax.tree.map(lambda part: lax.all_gather(part, axis), array)
    start = jax.tree.map(
        lambda part, zero: jnp.broadcast_to(jnp.asarray(zero, part.dtype), part.shape),
        array,
        identity,
    )

    def lap(k, before):
        reached = k < place
        new = combine(before, jax.tree.map(lambda part: part[k], everything))
        return jax.tree.map(lambda a, b: jnp.where(reached, a, b), new, before)

    return lax.fori_loop(0, count, lap, start)


def causal_conv(previous, current, weights):
    padded = jnp.concatenate([previous, current], axis=0).astype(jnp.float32)
    length = current.shape[0]
    kernel = weights.astype(jnp.float32)
    summed = jnp.zeros(current.shape, jnp.float32)
    for offset in range(weights.shape[0]):
        summed = summed + kernel[offset][None, :] * lax.slice_in_dim(
            padded, offset, offset + length, axis=0
        )
    return jax.nn.silu(summed)


def unit_rows(features, head_count, factor):
    reshaped_array = features.reshape(features.shape[0], head_count, -1)
    normed = (
        reshaped_array
        * lax.rsqrt(jnp.sum(reshaped_array * reshaped_array, axis=-1, keepdims=True) + 1e-06)
        * factor
    )
    return jnp.transpose(normed, (1, 0, 2))


def block_terms(queries, key_rows, values, log_decay, write_rate):
    block_length = queries.shape[-2]
    cumulative = jnp.cumsum(log_decay, axis=-1)
    row_index = lax.broadcasted_iota(jnp.int32, (block_length, block_length), 0)
    column_index = lax.broadcasted_iota(jnp.int32, (block_length, block_length), 1)
    causal = row_index >= column_index
    strict = row_index > column_index
    spread = cumulative[..., :, None] - cumulative[..., None, :]
    decay_table = jnp.where(causal, jnp.exp(jnp.where(causal, spread, 0.0)), 0.0)
    key_dots = jnp.einsum("...td,...sd->...ts", key_rows, key_rows, precision=highest)
    lower_part = jnp.where(strict, write_rate[..., :, None] * decay_table * key_dots, 0.0)
    system = lower_part + jnp.eye(block_length, dtype=jnp.float32)
    growth = jnp.exp(cumulative)
    stacked = jnp.concatenate(
        [write_rate[..., None] * values, (write_rate * growth)[..., None] * key_rows], axis=-1
    )
    solved = jax.scipy.linalg.solve_triangular(system, stacked, lower=True, unit_diagonal=True)
    value_width = values.shape[-1]
    update_value = solved[..., :value_width]
    update_key = solved[..., value_width:]
    query_dots = jnp.einsum("...td,...sd->...ts", queries, key_rows, precision=highest)
    attend = jnp.where(causal, query_dots * decay_table, 0.0)
    scaled_query = growth[..., None] * queries
    tail_keys = jnp.exp(cumulative[..., -1:] - cumulative)[..., None] * key_rows
    end_decay = growth[..., -1]
    return (scaled_query, attend, update_value, update_key, tail_keys, end_decay)


def to_front(source):
    return jnp.moveaxis(source, 1, 0)


def apply_move(move_matrix, state_now):
    return jnp.einsum("hdf,hfe->hde", move_matrix, state_now, precision=highest)


def per_device(
    hidden_states,
    proj_ba,
    query_in,
    key_in,
    value_in,
    conv_query,
    conv_key,
    convolution_value_taps,
    decay_scale,
    dt_bias,
):
    heads_here = decay_scale.shape[0]
    local_tokens = hidden_states.shape[0]
    key_count = query_in.shape[1] // DK
    group_size = heads_here // key_count
    block_count = local_tokens // BLOCK
    query_scale = 1.0 / math.sqrt(DK)
    logits = lax.psum_scatter(
        lax.dot_general(
            proj_ba, hidden_states, (((0,), (1,)), ((), ())), preferred_element_type=jnp.float32
        ),
        "head",
        scatter_dimension=0,
        tiled=True,
    )
    log_decay = -decay_scale[:, None] * jax.nn.softplus(logits[0::2] + dt_bias[:, None])
    write_rate = jax.nn.sigmoid(logits[1::2])
    margin = KCONV - 1
    tail_rows = (
        query_in[local_tokens - margin :],
        key_in[local_tokens - margin :],
        value_in[local_tokens - margin :],
    )
    before_query, before_key, before_value = passed_along(
        (tail_rows[0], tail_rows[1], tail_rows[2]), "seq", 1
    )
    unit_query = jnp.repeat(
        unit_rows(causal_conv(before_query, query_in, conv_query), key_count, query_scale),
        group_size,
        axis=0,
    )
    unit_keys = jnp.repeat(
        unit_rows(causal_conv(before_key, key_in, conv_key), key_count, 1.0), group_size, axis=0
    )
    mixed_values = jnp.transpose(
        causal_conv(before_value, value_in, convolution_value_taps).reshape(
            local_tokens, heads_here, DV
        ),
        (1, 0, 2),
    )

    def blocks(source):
        return source.reshape(heads_here, block_count, BLOCK, source.shape[-1])

    scaled_query, attend, update_value, update_key, tail_keys, end_decay = block_terms(
        blocks(unit_query),
        blocks(unit_keys),
        blocks(mixed_values),
        log_decay.reshape(heads_here, block_count, BLOCK),
        write_rate.reshape(heads_here, block_count, BLOCK),
    )
    identity_key = jnp.eye(DK, dtype=jnp.float32)

    def local_step(carried_pair, pieces):
        state_now, transit = carried_pair
        value_part, key_part, tail_part, end_part = pieces
        errors = value_part - jnp.einsum("hcd,hde->hce", key_part, state_now, precision=highest)
        next_state = end_part[:, None, None] * state_now + jnp.einsum(
            "hcd,hce->hde", tail_part, errors, precision=highest
        )
        block_move = end_part[:, None, None] * identity_key - jnp.einsum(
            "hcd,hcf->hdf", tail_part, key_part, precision=highest
        )
        next_transit = apply_move(block_move, transit)
        return ((next_state, next_transit), (state_now, transit))

    start_pair = (
        jnp.zeros((heads_here, DK, DV), jnp.float32),
        jnp.broadcast_to(identity_key, (heads_here, DK, DK)),
    )
    (dev_state, dev_move), (start_states, start_moves) = lax.scan(
        local_step,
        start_pair,
        (to_front(update_value), to_front(update_key), to_front(tail_keys), to_front(end_decay)),
    )

    def combine(first_pair, second_pair):
        return (
            apply_move(second_pair[0], first_pair[0]),
            apply_move(second_pair[0], first_pair[1]) + second_pair[1],
        )

    neutral = (jnp.broadcast_to(identity_key, dev_move.shape), jnp.zeros_like(dev_state))
    unused, entering = carried_in((dev_move, dev_state), "seq", combine, neutral)

    def final_step(state_now, pieces):
        query_part, attend_part, value_part, key_part, tail_part, end_part = pieces
        errors = value_part - jnp.einsum("hcd,hde->hce", key_part, state_now, precision=highest)
        produced = jnp.einsum(
            "hcd,hde->hce", query_part, state_now, precision=highest
        ) + jnp.einsum("hcs,hse->hce", attend_part, errors, precision=highest)
        next_state = end_part[:, None, None] * state_now + jnp.einsum(
            "hcd,hce->hde", tail_part, errors, precision=highest
        )
        return (next_state, produced)

    unused_state, produced = lax.scan(
        final_step,
        entering,
        (
            to_front(scaled_query),
            to_front(attend),
            to_front(update_value),
            to_front(update_key),
            to_front(tail_keys),
            to_front(end_decay),
        ),
    )
    outputs = jnp.moveaxis(produced, 0, 1)
    return jnp.transpose(outputs.reshape(heads_here, local_tokens, DV), (1, 0, 2)).reshape(
        local_tokens, heads_here * DV
    )


def solution(mesh):
    placed = (
        P("seq", "head"),
        P("head", None),
        P("seq", "head"),
        P("seq", "head"),
        P("seq", "head"),
        P(None, "head"),
        P(None, "head"),
        P(None, "head"),
        P("head"),
        P("head"),
    )
    return jax.shard_map(
        per_device, mesh=mesh, in_specs=placed, out_specs=P("seq", "head"), check_vma=False
    )
```

profile of v0, /device:TPU:0, one launch (start us, length us, event | category | flops | bytes accessed | tf_op | source)
XLA Modules:
  0.0 595.9 jit_solution(8965543544239724335)
XLA Ops:
  7.3 4.8 collective-permute-start
  14.7 3.4 collective-permute-start.1
  25.6 2.6 copy_bitcast_fusion
  28.2 5.8 reduce-scatter.2.cloned.1.call-done
  38.6 6.0 %add_bitcast_fusion = f32[8,4,1,128,128]{4,3,2,1,0:T(8,128)} fusion(f32[8,4,128,128]{3,2,1,0:T(8,128)S(1)} %bitcast.183, f32[128,128]{1,0:T(8,128)S(1)} %fusion.59, f32[128,128]{1,0:T(8,128)S(1)} %get-tuple-element.365, f32[8,4,128]{2,1,0:T(4,128)S(1)} %copy.82, f32[8,4,128]{2,1,0:T(4,128)S(1)} %copy.81, pred[128,128]{1,0:T(8,128)(4,1)S(1)} %get-tuple-element.362, ...), kind=kOutput, calls=%fused_computation.71 | convolution fusion | flops 810024960 | bytes 4407296 | tf_op jit(solution)/shard_map/...td,...sd->...ts/dot_general | solution.py:71
  44.6 315.8 %custom-call.4 = f32[8,4,1,128,128]{3,4,2,1,0:T(8,128)} custom-call(f32[8,4,1,128,128]{4,3,2,1,0:T(8,128)} %add_bitcast_fusion), custom_call_target="InvertDiagBlocksLowerTriangular" | custom-call | tf_op jit(solution)/shard_map/jit(_solve_triangular)/vmap(vmap())/triangular_solve | solution.py:78
  360.5 2.2 broadcast_multiply_fusion.1
  362.7 2.2 broadcast_multiply_fusion
  364.9 3.8 fusion.43
  370.9 3.0 copy.87
  374.1 16.3 %while.43 = (s32[]{:T(128)}, f32[8,128,128]{2,1,0:T(8,128)S(1)}, f32[8,128,128]{2,1,0:T(8,128)S(1)}, f32[4,8]{1,0:T(4,128)S(1)}, f32[4,8,128,128]{2,3,1,0:T(8,12...) while((s32[]{:T(128)}, f32[8,128,128]{2,1,0:T(8,128)S(1)}, ...), condition=%wide.region_4.5_spmd.clone.clone, body=%wide.region_3.4_spmd.clone.sunk.clone | while | flops 806256640 | bytes 16911548 | solution.py:179
  392.7 3.4 collective-permute-start.2
  400.3 2.5 reshape.77
  402.8 1.9 multiply_reduce_fusion
  405.8 2.0 multiply_bitcast_fusion
  407.7 5.8 fusion.50
  413.6 51.2 %all-gather.5.cloned.1.call-done = f32[64,128,128]{2,1,0:T(8,128)} async-done(((f32[8,128,128]{2,1,0:T(8,128)}), f32[64,128,128]{2,1,0:T(8,128)}) %all-gather.5.cloned.1.call-update) | async-done | bytes 4194320 | tf_op jit(solution)/shard_map/all_gather | solution.py:25
  464.8 74.0 %all-gather.7.cloned.1.call-done = f32[64,128,128]{2,1,0:T(8,128)} async-done(((f32[8,128,128]{2,1,0:T(8,128)}), f32[64,128,128]{2,1,0:T(8,128)}) %all-gather.7.cloned.1.call-update) | async-done | bytes 4194320 | tf_op jit(solution)/shard_map/all_gather | solution.py:25
  538.8 15.5 %while.44 = (s32[]{:T(128)}, f32[8,128,128]{2,1,0:T(8,128)S(1)}, s32[]{:T(128)}, f32[8,8,128,128]{3,2,1,0:T(8,128)}, f32[8,8,128,128]{3,2,1,0:T(8,128)}) while((s32[]{:T(128)}, f32[8,128,128]{2,1,0:T(8,128)S(1)}, s32[]{:T(128)}, f32[8,8,128,128]{3,2,1,0:T(8,128)}, f32[8,8,128,128]{3,2,1,0:T(8,128)}) %tuple.113), condition=%wide.region_6.7_spmd.clone.clone, body=%wide.region_5.6_spmd.clone.sunk.clone | while | flops 201850880 | bytes 3672655 | solution.py:37
  538.9 1.9 fusion.155
  540.8 1.9 fusion.155
  544.7 1.9 fusion.155
  546.7 1.9 fusion.155
  548.6 1.9 fusion.155
  550.6 1.9 fusion.155
  552.5 1.9 fusion.155
  554.4 31.1 %while.42 = (s32[]{:T(128)}, f32[8,128,128]{2,1,0:T(8,128)S(1)}, f32[4,8,128,128]{3,2,0,1:T(8,128)}, f32[4,8]{1,0:T(4,128)S(1)}, f32[4,8,128,128]{2,3,1,0:T(8,12...) while((s32[]{:T(128)}, f32[8,128,128]{2,1,0:T(8,128)S(1)}, ...), condition=%wide.region_9.10_spmd.clone, body=%wide.region_8.9_spmd.sunk.clone | while | flops 805830656 | bytes 7867585 | solution.py:205
  557.8 2.5 fusion.141
  565.6 2.5 fusion.141
  573.4 2.5 fusion.141
  581.2 2.5 fusion.141
  585.6 1.9 copy.101
  (141 shorter events, 65.8 us)
Async XLA Ops:
  6.5 5.6 copy-start
  6.5 27.5 %reduce-scatter.2.cloned.1.call-start = ((), (), s32[]{:S(2)}) async-start(), calls=%async_computation.1 | async-start | bytes 163840 | tf_op jit(solution)/shard_map/reduce_scatter | solution.py:116
  7.3 13.4 %collective-permute-start = (bf16[3,512]{1,0:T(4,128)(2,1)S(1)}, bf16[3,512]{1,0:T(4,128)(2,1)S(1)}, u32[]{:S(2)}, u32[]{:S(2)}) collective-permute-start(bf16[3,512]{1,0:T(4,128)(2,1)S(1)} %slice.109), channel_id=1, source_target_pairs={{0,4},{4,8},{8,12},{12,16},{16,20},{20,24},{24,28},{1,5},{5,9},{9,... | collective-permute-start | bytes 9224 | tf_op jit(solution)/shard_map/ppermute | solution.py:20
  14.0 450.9 %all-gather.5.cloned.1.call-start = ((), (), s32[]{:S(2)}) async-start(), calls=%async_computation.2 | async-start | bytes 4718592 | tf_op jit(solution)/shard_map/all_gather | solution.py:25
  14.7 10.5 %collective-permute-start.1 = (bf16[3,1024]{1,0:T(4,128)(2,1)S(1)}, bf16[3,1024]{1,0:T(4,128)(2,1)S(1)}, u32[]{:S(2)}, u32[]{:S(2)}) collective-permute-start(bf16[3,1024]{1,0:T(4,128)(2,1)S(1)} %slice.119), channel_id=1, source_target_pairs={{0,4},{4,8},{8,12},{12,16},{16,20},{20,24},{24,28},{1,5},{5,9},{9,... | collective-permute-start | bytes 18440 | tf_op jit(solution)/shard_map/ppermute | solution.py:20
  23.6 1.7 copy-start.9
  25.6 9.2 %copy-start.11 = (f32[8]{0:T(128)S(1)}, f32[8]{0:T(128)}, u32[]{:S(2)}) copy-start(f32[8]{0:T(128)} %param.25) | copy-start | bytes 100
  38.6 324.0 %copy-start.5 = (f32[4,2,512,128]{3,2,1,0:T(8,128)}, f32[4,2,512,128]{3,2,1,0:T(8,128)S(1)}, u32[]{:S(2)}) copy-start(f32[4,2,512,128]{3,2,1,0:T(8,128)S(1)} %broadcast_in_dim.55) | copy-start | bytes 6291460
  362.7 2.2 copy-start.8
  374.1 22.0 %copy-start.10 = (bf16[4,512]{1,0:T(4,128)(2,1)S(1)}, bf16[4,512]{1,0:T(4,128)(2,1)}, u32[]{:S(2)}) copy-start(bf16[4,512]{1,0:T(4,128)(2,1)} %param.21) | copy-start | bytes 12292
  374.3 1.9 copy-start.3
  378.4 1.9 copy-start.3
  382.4 1.9 copy-start.3
  386.4 1.9 copy-start.3
  390.4 0.8 copy-start.4
  390.4 1.0 copy-start.2
  391.2 147.6 %all-gather.7.cloned.1.call-start = ((), (), s32[]{:S(2)}) async-start(), calls=%async_computation.3 | async-start | bytes 4718592 | tf_op jit(solution)/shard_map/all_gather | solution.py:25
  392.7 4.7 collective-permute-start.2
  402.8 2.0 copy-start.7
  405.8 2.0 copy-start.6
  587.5 1.8 copy-start.1
Sparse Core Ops, SparseCore 0:
  14.1 19.8 reduce-scatter.1
  391.4 73.3 all-gather.4
  467.2 71.6 all-gather.6
where the time goes:
time: 598 us; the launch traced here: 596 us
  other arithmetic  336 us (56%)
  waiting for transfers between devices  133 us (22%)
  matrix products  78.9 us (13%)
  local copies, waits for them, and re-layouts  21.7 us (4%)
  between operations  13.5 us (2%)
  starting transfers between devices  11.7 us (2%)
    another operation x4, other arithmetic, block_terms(): jax.scipy.linalg.solve_triangular(system, stacked, lower=True, unit_diago...  316 us
    all_gather x2, waiting for transfers between devices, carried_in(): everything = jax.tree.map(lambda part: lax.all_gather(part, axis), array)  125 us
    dot_general x12, matrix products, apply_move(): return jnp.einsum('hdf,hfe->hde', move_matrix, state_now, precision=highest)  17.7 us
  transfers between devices with their start and end apart: 6, of which 4 were waited for; matrix products, arithmetic and copies ran while one was open for 5% of the time, Pallas kernels for 0%

commit v1 on v0

v1 whole, which is shorter than its diff:
```python
import functools
import math

import jax
import jax.numpy as jnp
from jax import lax
from jax.experimental import pallas as pl
from jax.experimental.pallas import tpu as pltpu
from jax.sharding import PartitionSpec as P

DK = 128
DV = 128
KCONV = 4
BLOCK = 128
SUB = 16
EDGE = 16

f32 = jnp.float32
bf16 = jnp.bfloat16
VMEM = pltpu.VMEM
FAR = -1e30


def split(x):
    hi = x.astype(bf16)
    return hi, (x - hi.astype(f32)).astype(bf16)


def dot_split(a, b, contract=((1,), (0,))):
    (ah, al), (bh, bl) = a, b
    (ca,), (cb,) = contract
    left = jnp.concatenate([ah, al, ah], axis=ca)
    right = jnp.concatenate([bh, bh, bl], axis=cb)
    return lax.dot_general(left, right, (contract, ((), ())), preferred_element_type=f32)


NN = ((1,), (0,))
NT = ((1,), (1,))
TN = ((0,), (0,))


def silu(x):
    return x / (1.0 + jnp.exp(-x))


def unit(x, factor=1.0):
    return x * (lax.rsqrt(jnp.sum(x * x, axis=-1, keepdims=True) + 1e-6) * factor)


def conv_rows(padded_ref, taps, rows, columns):
    total = taps[0:1] * padded_ref[pl.ds(8 - KCONV + 1, rows), columns]
    for j in range(1, KCONV):
        total = total + taps[j : j + 1] * padded_ref[pl.ds(8 - KCONV + 1 + j, rows), columns]
    return silu(total)


def iotas(rows=BLOCK, columns=BLOCK):
    return (
        lax.broadcasted_iota(jnp.int32, (rows, columns), 0),
        lax.broadcasted_iota(jnp.int32, (rows, columns), 1),
    )


def lanes(start, size):
    return pl.ds(pl.multiple_of(start, 128), size)


def logits_kernel(head_count, hidden_ref, proj_ref, q_ref, k_ref, v_ref, *refs):
    outs, tail_ref, held = refs[:head_count], refs[head_count], refs[head_count + 1]
    rows = proj_ref.shape[1] // head_count
    everything = lax.dot_general(
        proj_ref[...], hidden_ref[...], (((0,), (1,)), ((), ())), preferred_element_type=f32
    )
    for m in range(head_count):
        held[m] = everything[m * rows : (m + 1) * rows]
    me = lax.axis_index("head")
    for d in range(head_count):
        outs[d][...] = held[me ^ d]
    dk = q_ref.shape[1]
    tail_ref[:, 0:dk] = q_ref[...]
    tail_ref[:, dk : 2 * dk] = k_ref[...]
    tail_ref[:, 2 * dk :] = v_ref[...]


def mix_kernel(k_ref, v_ref, kt_ref, vt_ref, unit_ref, dots_ref, mixed_ref, padded):
    tokens = k_ref.shape[0]
    padded[0:8] = jnp.zeros((8, padded.shape[1]), f32)
    padded[8:, 0:DK] = k_ref[...].astype(f32)
    padded[8:, DK:] = v_ref[...].astype(f32)
    key_taps = kt_ref[...].astype(f32)
    value_taps = vt_ref[...].astype(f32)
    keys = unit(conv_rows(padded, key_taps, tokens, slice(0, DK)))
    unit_ref[0] = keys
    for c in range(tokens // BLOCK):
        part = split(keys[c * BLOCK : (c + 1) * BLOCK])
        dots_ref[0, c] = dot_split(part, part, NT)
    mixed_ref[0] = conv_rows(padded, value_taps, tokens, slice(DK, None))


def softplus(u):
    e = jnp.exp(-jnp.abs(u))
    small = e * (1.0 - e * (0.5 - e * (1.0 / 3.0 - e * (0.25 - e * 0.2))))
    return jnp.maximum(u, 0.0) + jnp.where(e < 0.03, small, jnp.log(1.0 + e))


def invert_all(lowers):
    count = len(lowers)
    row, column = iotas()
    blocks = (row // SUB) == (column // SUB)
    folded = []
    for lower in lowers:
        kept = jnp.where(blocks, lower, 0.0)
        total = kept[0:SUB]
        for b in range(1, BLOCK // SUB):
            total = total + kept[b * SUB : (b + 1) * SUB]
        folded.append(total)
    spread = jnp.concatenate(split(jnp.concatenate(folded, axis=0)), axis=1)
    pick = [
        jnp.where(row == (column // SUB) * SUB + j, 1.0, 0.0).astype(bf16) for j in range(SUB - 1)
    ]
    pick = jnp.concatenate(pick, axis=1)
    pick = jnp.concatenate([pick, pick], axis=0)
    wide = jnp.dot(spread, pick, preferred_element_type=f32).reshape(
        count, SUB, (SUB - 1) * BLOCK
    )
    srow, scolumn = iotas(SUB, BLOCK)
    inverse = jnp.broadcast_to(
        jnp.where(srow == scolumn % SUB, 1.0, 0.0)[None], (count, SUB, BLOCK)
    )
    for j in range(SUB - 1):
        inverse = inverse - wide[:, :, j * BLOCK : (j + 1) * BLOCK] * inverse[:, j : j + 1, :]
    full = [
        jnp.where(blocks, jnp.concatenate([inverse[i]] * (BLOCK // SUB), axis=0), 0.0)
        for i in range(count)
    ]
    size = SUB
    while size < BLOCK:
        across = ((row // (2 * size)) == (column // (2 * size))) & ((row // size) > (column // size))
        halves = [split(x) for x in full]
        first = [
            dot_split(halves[i], split(jnp.where(across, lowers[i], 0.0))) for i in range(count)
        ]
        full = [full[i] - dot_split(split(first[i]), halves[i]) for i in range(count)]
        size *= 2
    return full


def solve_kernel(
    slots,
    group,
    pieces,
    scale_ref,
    bias_ref,
    *refs,
):
    logit_refs, refs = refs[:pieces], refs[pieces:]
    (unit_ref, dots_ref, mixed_ref, k_ref, v_ref, before_ref, kt_ref, vt_ref), refs = (
        refs[:8],
        refs[8:],
    )
    count = len(slots)
    message_refs, refs = refs[:count], refs[count:]
    solved_ref, moves_ref, cumulative_ref, first_ref, padded = refs
    tokens = unit_ref.shape[1]
    blocks = tokens // BLOCK
    key_width = kt_ref.shape[1]
    place = lax.axis_index("seq") % group
    row, column = iotas()
    upper = jnp.where(row <= column, 1.0, 0.0)
    identity = row == column
    strict = row > column

    systems, rights, tails, ends, key_parts = [], [], [], [], []
    for at, s in enumerate(slots):
        p = place ^ (group - 1 - s)
        kcol, vcol = p * DK, p * 2 * DV
        padded[0:8, 0:DK] = before_ref[:, lanes(key_width + kcol, DK)].astype(f32)[EDGE - 8 :]
        padded[0:8, DK:] = before_ref[:, lanes(2 * key_width + vcol, 2 * DV)].astype(f32)[EDGE - 8 :]
        padded[8:, 0:DK] = k_ref[:, lanes(kcol, DK)].astype(f32)
        padded[8:, DK:] = v_ref[:, lanes(vcol, 2 * DV)].astype(f32)
        key_taps = kt_ref[:, lanes(kcol, DK)].astype(f32)
        value_taps = vt_ref[:, lanes(vcol, 2 * DV)].astype(f32)
        edge_keys = unit(conv_rows(padded, key_taps, EDGE, slice(0, DK)))
        edge_values = conv_rows(padded, value_taps, EDGE, slice(DK, None))
        decays, rates = [], []
        for b in range(2):
            h = 2 * p + b
            u = logit_refs[0][pl.ds(2 * h, 1), :]
            w = logit_refs[0][pl.ds(2 * h + 1, 1), :]
            for ref in logit_refs[1:]:
                u = u + ref[pl.ds(2 * h, 1), :]
                w = w + ref[pl.ds(2 * h + 1, 1), :]
            decays.append(-scale_ref[h] * softplus(u + bias_ref[h]))
            rates.append(1.0 / (1.0 + jnp.exp(-w)))
        decay_rows = jnp.concatenate(
            [d[:, c * BLOCK : (c + 1) * BLOCK] for d in decays for c in range(blocks)], axis=0
        )
        rate_rows = jnp.concatenate(
            [r[:, c * BLOCK : (c + 1) * BLOCK] for r in rates for c in range(blocks)], axis=0
        )
        sums = jnp.dot(
            decay_rows, upper, precision=lax.Precision.HIGHEST, preferred_element_type=f32
        )
        cumulative_ref[at] = sums
        cum_columns = jnp.transpose(sums)
        rate_columns = jnp.transpose(rate_rows)
        growth_columns = jnp.exp(cum_columns)
        last = sums[:, BLOCK - 1 : BLOCK]
        tail_columns = jnp.exp(jnp.transpose(last - sums))
        end_values = jnp.exp(last)
        for c in range(blocks):
            keys = unit_ref[p, pl.ds(c * BLOCK, BLOCK), :]
            values = mixed_ref[p, pl.ds(c * BLOCK, BLOCK), :]
            if c == 0:
                keys = jnp.concatenate([edge_keys, keys[EDGE:]], axis=0)
                values = jnp.concatenate([edge_values, values[EDGE:]], axis=0)
                first_ref[at] = keys
            parts = split(keys)
            key_parts.append(parts)
            dots = dot_split(parts, parts, NT) if c == 0 else dots_ref[p, c]
            for b in range(2):
                r = b * blocks + c
                rate = rate_columns[:, r : r + 1]
                spread = cum_columns[:, r : r + 1] - sums[r : r + 1, :]
                table = jnp.exp(jnp.where(strict, spread, FAR))
                systems.append(rate * table * dots)
                rights.append(
                    jnp.concatenate(
                        [
                            rate * values[:, b * DV : (b + 1) * DV],
                            (rate * growth_columns[:, r : r + 1]) * keys,
                        ],
                        axis=1,
                    )
                )
                tails.append(tail_columns[:, r : r + 1])
                ends.append(end_values[r : r + 1, :])

    inverses = invert_all(systems)
    solved = [dot_split(split(x), split(r)) for x, r in zip(inverses, rights)]
    for at in range(count):
        moves = {}
        for c in range(blocks):
            i = (at * blocks + c) * 2
            both = jnp.concatenate([tails[i] * solved[i], tails[i + 1] * solved[i + 1]], axis=1)
            grown = dot_split(key_parts[at * blocks + c], split(both), TN)
            for b in range(2):
                solved_ref[at, b, pl.ds(c * BLOCK, BLOCK), :] = solved[i + b]
                added = grown[:, b * 2 * DK : b * 2 * DK + DV]
                move = (
                    jnp.where(identity, ends[i + b], 0.0)
                    - grown[:, b * 2 * DK + DV : (b + 1) * 2 * DK]
                )
                moves[b, c] = (added, move)
                if c < blocks - 1:
                    moves_ref[at, b, c, :, 0:DV] = added
                    moves_ref[at, b, c, :, DV:] = move
        for b in range(2):
            added, move = moves[b, 0]
            both = jnp.concatenate([added, move], axis=1)
            for c in range(1, blocks):
                added, move = moves[b, c]
                both = dot_split(split(move), split(both))
                both = jnp.concatenate([both[:, :DV] + added, both[:, DV:]], axis=1)
            message_refs[at][b] = both


def query_kernel(
    group, q_ref, before_ref, qt_ref, unit_ref, first_ref, cumulative_ref, solved_ref, out_ref, padded
):
    s = pl.program_id(0)
    place = lax.axis_index("seq") % group
    p = place ^ (group - 1 - s)
    tokens = q_ref.shape[0]
    blocks = tokens // BLOCK
    columns = lanes(p * DK, DK)
    padded[0:8] = before_ref[:, columns].astype(f32)[EDGE - 8 :]
    padded[8:] = q_ref[:, columns].astype(f32)
    taps = qt_ref[:, columns].astype(f32)
    queries = unit(conv_rows(padded, taps, tokens, slice(None)), 1.0 / math.sqrt(DK))
    row, column = iotas()
    causal = row >= column
    sums = cumulative_ref[0]
    cum_columns = jnp.transpose(sums)
    growth_columns = jnp.exp(cum_columns)
    for c in range(blocks):
        here = queries[c * BLOCK : (c + 1) * BLOCK]
        keys = first_ref[0] if c == 0 else unit_ref[p, pl.ds(c * BLOCK, BLOCK), :]
        dots = dot_split(split(here), split(keys), NT)
        for b in range(2):
            r = b * blocks + c
            spread = cum_columns[:, r : r + 1] - sums[r : r + 1, :]
            attend = dots * jnp.exp(jnp.where(causal, spread, FAR))
            seen = dot_split(split(attend), split(solved_ref[0, b, pl.ds(c * BLOCK, BLOCK), :]))
            out_ref[0, b, pl.ds(c * BLOCK, BLOCK), 0:DV] = seen[:, :DV]
            out_ref[0, b, pl.ds(c * BLOCK, BLOCK), DV:] = (
                growth_columns[:, r : r + 1] * here - seen[:, DV:]
            )


def prefix_kernel(group, entering_ref, *refs):
    messages, refs = refs[:group], refs[group:]
    outs, refs = refs[: group + 1], refs[group + 1 :]
    held, sems = refs
    place = lax.axis_index("seq") % group
    copies = [
        pltpu.make_async_copy(messages[d], held.at[place ^ d], sems.at[d]) for d in range(group)
    ]
    for copy in copies:
        copy.start()
    for copy in copies:
        copy.wait()
    heads = entering_ref.shape[0]
    states = [entering_ref[b] for b in range(heads)]
    chain = []
    for i in range(group):
        chain.append(states)
        states = [
            held[i, b, :, 0:DV] + dot_split(split(held[i, b, :, DV:]), split(states[b]))
            for b in range(heads)
        ]
    for b in range(heads):
        outs[group][b] = states[b]
    for j in range(group):

        @pl.when(place == j)
        def _():
            for i in range(group):
                for b in range(heads):
                    outs[j ^ i][b] = chain[i][b]


def output_kernel(group, reads_ref, moves_ref, *refs):
    entering, (out_ref,) = refs[:group], refs[group:]
    place = lax.axis_index("seq") % group
    tokens = out_ref.shape[0]
    blocks = tokens // BLOCK
    for s in range(group):
        p = place ^ (group - 1 - s)
        for b in range(2):
            state = entering[group - 1 - s][b]
            for c in range(blocks):
                reads = reads_ref[s, b, pl.ds(c * BLOCK, BLOCK), DV:]
                if c < blocks - 1:
                    reads = jnp.concatenate([reads, moves_ref[s, b, c, :, DV:]], axis=0)
                product = dot_split(split(reads), split(state))
                out_ref[pl.ds(c * BLOCK, BLOCK), lanes(p * 2 * DV + b * DV, DV)] = (
                    reads_ref[s, b, pl.ds(c * BLOCK, BLOCK), 0:DV] + product[:BLOCK]
                )
                if c < blocks - 1:
                    state = moves_ref[s, b, c, :, 0:DV] + product[BLOCK:]


def shape(*dims, dtype=f32):
    return jax.ShapeDtypeStruct(dims, dtype)


def params(mib=56):
    return pltpu.CompilerParams(vmem_limit_bytes=mib << 20)


def whole(space=VMEM):
    return pl.BlockSpec(memory_space=space)


def per_device(
    hidden_states,
    proj_ba,
    query_in,
    key_in,
    value_in,
    conv_query,
    conv_key,
    convolution_value_taps,
    decay_scale,
    dt_bias,
):
    tokens = hidden_states.shape[0]
    heads = decay_scale.shape[0]
    pairs = key_in.shape[1] // DK
    blocks = tokens // BLOCK
    key_width, value_width = key_in.shape[1], value_in.shape[1]
    seq, head_count = lax.axis_size("seq"), lax.axis_size("head")
    group = pairs

    def full(block):
        return pl.BlockSpec(block, lambda i: (0,) * len(block))

    last_rows = tokens // EDGE - 1
    *partial, tail = pl.pallas_call(
        functools.partial(logits_kernel, head_count),
        grid=(1,),
        in_specs=[
            full(hidden_states.shape),
            full(proj_ba.shape),
            pl.BlockSpec((EDGE, key_width), lambda i: (last_rows, 0)),
            pl.BlockSpec((EDGE, key_width), lambda i: (last_rows, 0)),
            pl.BlockSpec((EDGE, value_width), lambda i: (last_rows, 0)),
        ],
        out_specs=[full((2 * heads, tokens))] * head_count
        + [full((EDGE, 2 * key_width + value_width))],
        out_shape=[shape(2 * heads, tokens)] * head_count
        + [shape(EDGE, 2 * key_width + value_width, dtype=bf16)],
        scratch_shapes=[VMEM((head_count, 2 * heads, tokens), f32)],
        compiler_params=params(),
        name="logits",
    )(hidden_states, proj_ba, query_in, key_in, value_in)

    logits = [partial[0]] + [
        lax.ppermute(partial[d], "head", [(i, i ^ d) for i in range(head_count)])
        for d in range(1, head_count)
    ]
    before = lax.ppermute(tail, "seq", [(i, i + 1) for i in range(seq - 1)])

    unit_keys, key_dots, mixed = pl.pallas_call(
        mix_kernel,
        grid=(pairs,),
        in_specs=[
            pl.BlockSpec((tokens, DK), lambda i: (0, i)),
            pl.BlockSpec((tokens, 2 * DV), lambda i: (0, i)),
            pl.BlockSpec((KCONV, DK), lambda i: (0, i)),
            pl.BlockSpec((KCONV, 2 * DV), lambda i: (0, i)),
        ],
        out_specs=[
            pl.BlockSpec((1, tokens, DK), lambda i: (i, 0, 0)),
            pl.BlockSpec((1, blocks, BLOCK, BLOCK), lambda i: (i, 0, 0, 0)),
            pl.BlockSpec((1, tokens, 2 * DV), lambda i: (i, 0, 0)),
        ],
        out_shape=[
            shape(pairs, tokens, DK),
            shape(pairs, blocks, BLOCK, BLOCK),
            shape(pairs, tokens, 2 * DV),
        ],
        scratch_shapes=[VMEM((tokens + 8, DK + 2 * DV), f32)],
        compiler_params=params(),
        cost_estimate=pl.CostEstimate(
            flops=4_000_000_000, bytes_accessed=6_000_000, transcendentals=0
        ),
        name="mix",
    )(key_in, value_in, conv_key, convolution_value_taps)

    def solve(slots):
        count = len(slots)
        return pl.pallas_call(
            functools.partial(solve_kernel, slots, group, head_count),
            grid=(1,),
            in_specs=[whole(pltpu.SMEM)] * 2
            + [whole()] * (head_count + 3)
            + [
                pl.BlockSpec((EDGE, key_width), lambda i: (0, 0)),
                pl.BlockSpec((EDGE, value_width), lambda i: (0, 0)),
            ]
            + [whole()] * 3,
            out_specs=[whole()] * (count + 4),
            out_shape=[shape(2, DK, 2 * DK)] * count
            + [
                shape(count, 2, tokens, 2 * DK),
                shape(count, 2, blocks - 1, DK, 2 * DK),
                shape(count, 2 * blocks, BLOCK),
                shape(count, BLOCK, DK),
            ],
            scratch_shapes=[VMEM((EDGE + 8, DK + 2 * DV), f32)],
            compiler_params=params(),
            cost_estimate=pl.CostEstimate(
                flops=4_000_000_000 * count, bytes_accessed=4_000_000 * count, transcendentals=0
            ),
            name="solve",
        )(
            decay_scale,
            dt_bias,
            *logits,
            unit_keys,
            key_dots,
            mixed,
            key_in,
            value_in,
            before,
            conv_key,
            convolution_value_taps,
        )

    *messages, solved, moves, cumulative, first_keys = solve(tuple(range(group)))

    arrived = [messages[group - 1]]
    for d in range(1, group):
        arrived.append(
            lax.ppermute(messages[group - 1 - d], "seq", [(i, i ^ d) for i in range(seq)])
        )

    reads = pl.pallas_call(
        functools.partial(query_kernel, group),
        grid=(pairs,),
        in_specs=[
            full(query_in.shape),
            full(tail.shape),
            full(conv_query.shape),
            full(unit_keys.shape),
            pl.BlockSpec((1, BLOCK, DK), lambda i: (i, 0, 0)),
            pl.BlockSpec((1, 2 * blocks, BLOCK), lambda i: (i, 0, 0)),
            pl.BlockSpec((1, 2, tokens, 2 * DK), lambda i: (i, 0, 0, 0)),
        ],
        out_specs=pl.BlockSpec((1, 2, tokens, 2 * DK), lambda i: (i, 0, 0, 0)),
        out_shape=shape(pairs, 2, tokens, 2 * DK),
        scratch_shapes=[VMEM((tokens + 8, DK), f32)],
        compiler_params=params(),
        cost_estimate=pl.CostEstimate(
            flops=4_000_000_000, bytes_accessed=8_000_000, transcendentals=0
        ),
        name="query",
    )(query_in, before, conv_query, unit_keys, first_keys, cumulative, solved)

    prefix = pl.pallas_call(
        functools.partial(prefix_kernel, group),
        in_specs=[whole()] + [whole(pl.ANY)] * group,
        out_specs=[whole()] * (group + 1),
        out_shape=[shape(2, DK, DV)] * (group + 1),
        scratch_shapes=[VMEM((group, 2, DK, 2 * DK), f32), pltpu.SemaphoreType.DMA((group,))],
        compiler_params=params(),
        name="prefix",
    )
    *entering, leaving = prefix(jnp.zeros((2, DK, DV), f32), *arrived)
    for _ in range(seq // group - 1):
        received = lax.ppermute(leaving, "seq", [(i, i + group) for i in range(seq - group)])
        *entering, leaving = prefix(received, *arrived)

    states = [entering[0]] + [
        lax.ppermute(entering[d], "seq", [(i, i ^ d) for i in range(seq)]) for d in range(1, group)
    ]
    return pl.pallas_call(
        functools.partial(output_kernel, group),
        in_specs=[whole()] * (2 + group),
        out_specs=whole(),
        out_shape=shape(tokens, value_width),
        compiler_params=params(),
        name="outputs",
    )(reads, moves, *states)


def solution(mesh):
    placed = (
        P("seq", "head"),
        P("head", None),
        P("seq", "head"),
        P("seq", "head"),
        P("seq", "head"),
        P(None, "head"),
        P(None, "head"),
        P(None, "head"),
        P("head"),
        P("head"),
    )
    return jax.shard_map(
        per_device, mesh=mesh, in_specs=placed, out_specs=P("seq", "head"), check_vma=False
    )
```

time: 598 us -> 92.3 us (0.15)
  other arithmetic: 336 us -> 0 us
  waiting for transfers between devices: 133 us -> 14.9 us
  matrix products: 78.9 us -> 0 us
  Pallas kernels: 0 us -> 52.1 us
  local copies, waits for them, and re-layouts: 21.7 us -> 4.37 us
  between operations: 13.5 us -> 0.15 us
  starting transfers between devices: 11.7 us -> 20.3 us
    another operation x5 -> x0, other arithmetic: 317 us -> none  [the longest x4 316 us: block_terms(): jax.scipy.linalg.solve_triangular(system, stacked, lower=True, unit_diago...]
    all_gather x2 -> x0, waiting for transfers between devices: 125 us -> none  [carried_in(): everything = jax.tree.map(lambda part: lax.all_gather(part, axis), array)]
    dot_general x43 -> x0, matrix products: 75.1 us -> none  [the longest x12 17.7 us: apply_move(): return jnp.einsum('hdf,hfe->hde', move_matrix, state_now, precision=highest)]
    pallas_call x0 -> x7, Pallas kernels: none -> 52.1 us  [the longest x1 17.9 us: solve(): pl.pallas_call(functools.partial(solve_kernel, slots, group, head_count),...]
    ppermute x3 -> x11, waiting for transfers between devices: 1.26 us -> 14.9 us  [the longest x3 12.1 us: per_device(): lax.ppermute(messages[group - 1 - d], 'seq', [(i, i ^ d) for i in range(s...]
    ppermute x3 -> x11, starting transfers between devices: 11.6 us -> 20.3 us  [the longest x3 5.43 us: per_device(): lax.ppermute(entering[d], 'seq', [(i, i ^ d) for i in range(seq)])]
    mul x6 -> x0, other arithmetic: 6.78 us -> none  [the longest x2 2.29 us: causal_conv(): return jax.nn.silu(summed)]
  transfers between devices with their start and end apart: 6 -> 11, of which waited for: 4 -> 4; matrix products, arithmetic and copies ran while one was open for 5% -> 0% of each run, Pallas kernels for 0% -> 16%
where the time goes in v1:
time: 92.3 us; the launch traced here: 91.8 us
  Pallas kernels  52.1 us (56%)
  starting transfers between devices  20.3 us (22%)
  waiting for transfers between devices  14.9 us (16%)
  local copies, waits for them, and re-layouts  4.37 us (5%)
    pallas_call x1, Pallas kernels, solve(): pl.pallas_call(functools.partial(solve_kernel, slots, group, head_count),...  17.9 us
    ppermute x3, waiting for transfers between devices, per_device(): lax.ppermute(messages[group - 1 - d], 'seq', [(i, i ^ d) for i in range(s...  12.1 us
    pallas_call x1, Pallas kernels, per_device(): pl.pallas_call(functools.partial(output_kernel, group), in_specs=[whole()...  9.77 us
    pallas_call x1, Pallas kernels, per_device(): pl.pallas_call(functools.partial(query_kernel, group), grid=(pairs,), in_...  8.26 us
    pallas_call x1, Pallas kernels, per_device(): pl.pallas_call(mix_kernel, grid=(pairs,), in_specs=[pl.BlockSpec((tokens,...  6.51 us
    ppermute x3, starting transfers between devices, per_device(): lax.ppermute(entering[d], 'seq', [(i, i ^ d) for i in range(seq)])  5.43 us
    ppermute x1, starting transfers between devices, per_device(): before = lax.ppermute(tail, 'seq', [(i, i + 1) for i in range(seq - 1)])  4.83 us
    ppermute x1, starting transfers between devices, per_device(): lax.ppermute(leaving, 'seq', [(i, i + group) for i in range(seq - group)])  4.5 us
  transfers between devices with their start and end apart: 11, of which 4 were waited for; matrix products, arithmetic and copies ran while one was open for 0% of the time, Pallas kernels for 16%

profile of v1, /device:TPU:0, one launch (start us, length us, event | category | flops | bytes accessed | tf_op | source)
XLA Modules:
  0.0 91.8 jit_solution(995163667533057114)
XLA Ops:
  0.0 1.6 %copy.11.proj_ref = bf16[512,64]{1,0:T(8,128)(2,1)} copy(bf16[512,64]{0,1:T(8,128)(2,1)} %param.11) | data formatting | bytes 131072 | tf_op args[1]
  1.6 2.1 %logits.1 = (f32[16,512]{1,0:T(8,128)}, f32[16,512]{1,0:T(8,128)}, f32[16,512]{1,0:T(8,128)}, f32[16,512]{1,0:T(8,128)}, bf16[16,2048]{1,0:T(8,128)(2,1)}) custom-call(bf16[512,512]{1,0:T(8,128)(2,1)} %hidden_ref.1, bf16[512,64]{1,0:T(8,128)(2,1)} %copy.11.proj_ref, bf16[512,512]{1,0:T(8,128)(2,1)} %q_ref.3, bf16[512,512]{1,0:T(8,128)(2,1)} %refs_7_.1, ...), custom_call_target="tpu_custom_call" | custom-call | tf_op jit(solution)/shard_map/logits/pallas_call | solution.py:390
  3.7 4.8 %collective-permute-start = (bf16[16,2048]{1,0:T(8,128)(2,1)}, bf16[16,2048]{1,0:T(8,128)(2,1)S(1)}, u32[]{:S(2)}, u32[]{:S(2)}) collective-permute-start(bf16[16,2048]{1,0:T(8,128)(2,1)} %get-tuple-element.26), channel_id=1, source_target_pairs={{0,4},{4,8},{8,12},{12,16},{16,20},{20,24},{24,28},{1,5},{5,9},{9,... | collective-permute-start | bytes 196616 | tf_op jit(solution)/shard_map/ppermute | solution.py:413
  8.6 0.1 collective-permute-start.1
  8.6 1.6 %collective-permute-start.2 = (f32[16,512]{1,0:T(8,128)}, f32[16,512]{1,0:T(8,128)S(1)}, u32[]{:S(2)}, u32[]{:S(2)}) collective-permute-start(f32[16,512]{1,0:T(8,128)} %get-tuple-element.30), channel_id=1, source_target_pairs={{0,2},{1,3},{2,0},{3,1},{4,6},{5,7},{6,4},{7,5},{8,10},{9,11},{10,... | collective-permute-start | bytes 98312 | tf_op jit(solution)/shard_map/ppermute | solution.py:410
  10.2 0.3 collective-permute-start.3
  10.5 6.5 %mix.1 = (f32[4,512,128]{2,1,0:T(8,128)}, f32[4,4,128,128]{3,2,1,0:T(8,128)}, f32[4,512,256]{2,1,0:T(8,128)}) custom-call(bf16[512,512]{1,0:T(8,128)(2,1)} %refs_7_.1, bf16[512,1024]{1,0:T(8,128)(2,1)} %refs_8_.1, bf16[4,512]{1,0:T(4,128)(2,1)} %refs_10_.1, bf16[4,1024]{1,0:T(4,128)(2,1)} %refs_11_.1), custom_call_target="tpu_custom_call" | custom-call | flops 4000000000 | bytes 6000000 | tf_op jit(solution)/shard_map/mix/pallas_call | solution.py:415
  17.1 0.5 copy-done.8
  17.6 0.0 copy-done.9
  17.6 0.0 copy-done.10
  17.7 0.1 copy-done.7
  17.7 17.9 %solve.1 = (f32[2,128,256]{2,1,0:T(8,128)}, f32[2,128,256]{2,1,0:T(8,128)}, f32[2,128,256]{2,1,0:T(8,128)}, f32[2,128,256]{2,1,0:T(8,128)}, f32[4,2,512,256]{3,2...) custom-call(f32[8]{0:T(128)} %scale_ref.1, f32[8]{0:T(128)} %bias_ref.1, ...), custom_call_target="tpu_custom_call" | custom-call | flops 16000000000 | bytes 16000000 | tf_op jit(solution)/shard_map/solve/pallas_call | solution.py:444
  35.7 1.6 %collective-permute-start.4 = (f32[2,128,256]{2,1,0:T(8,128)}, f32[2,128,256]{2,1,0:T(8,128)S(1)}, u32[]{:S(2)}, u32[]{:S(2)}) collective-permute-start(f32[2,128,256]{2,1,0:T(8,128)} %get-tuple-element.39), channel_id=1, source_target_pairs={{0,4},{4,0},{8,12},{12,8},{16,20},{20,16},{24,28},{28,24},{1,5},{5... | collective-permute-start | bytes 786440 | tf_op jit(solution)/shard_map/ppermute | solution.py:487
  37.3 1.6 %collective-permute-start.5 = (f32[2,128,256]{2,1,0:T(8,128)}, f32[2,128,256]{2,1,0:T(8,128)S(1)}, u32[]{:S(2)}, u32[]{:S(2)}) collective-permute-start(f32[2,128,256]{2,1,0:T(8,128)} %get-tuple-element.40), channel_id=1, source_target_pairs={{0,8},{4,12},{8,0},{12,4},{16,24},{20,28},{24,16},{28,20},{1,9},{5... | collective-permute-start | bytes 786440 | tf_op jit(solution)/shard_map/ppermute | solution.py:487
  38.9 0.4 collective-permute-start.6
  39.2 5.3 %collective-permute-done.4.refs_1_ = f32[2,128,256]{2,1,0:T(8,128)S(1)} collective-permute-done((f32[2,128,256]{2,1,0:T(8,128)}, f32[2,128,256]{2,1,0:T(8,128)S(1)}, u32[]{:S(2)}, u32[]{:S(2)}) %collective-permute-start.4) | collective-permute-done | bytes 262176 | tf_op jit(solution)/shard_map/ppermute | solution.py:487
  44.5 2.2 %collective-permute-done.5.refs_2_ = f32[2,128,256]{2,1,0:T(8,128)S(1)} collective-permute-done((f32[2,128,256]{2,1,0:T(8,128)}, f32[2,128,256]{2,1,0:T(8,128)S(1)}, u32[]{:S(2)}, u32[]{:S(2)}) %collective-permute-start.5) | collective-permute-done | bytes 262176 | tf_op jit(solution)/shard_map/ppermute | solution.py:487
  46.7 4.6 %collective-permute-done.6.refs_3_ = f32[2,128,256]{2,1,0:T(8,128)S(1)} collective-permute-done((f32[2,128,256]{2,1,0:T(8,128)}, f32[2,128,256]{2,1,0:T(8,128)S(1)}, u32[]{:S(2)}, u32[]{:S(2)}) %collective-permute-start.6) | collective-permute-done | bytes 262176 | tf_op jit(solution)/shard_map/ppermute | solution.py:487
  51.3 0.7 broadcast_in_dim.3.entering_ref
  52.0 0.0 copy-done.2
  52.1 3.8 %prefix.2 = (f32[2,128,128]{2,1,0:T(8,128)}, f32[2,128,128]{2,1,0:T(8,128)}, f32[2,128,128]{2,1,0:T(8,128)}, f32[2,128,128]{2,1,0:T(8,128)}, f32[2,128,128]{2,1,0:T(8,128)}) custom-call(f32[2,128,128]{2,1,0:T(8,128)} %broadcast_in_dim.3.entering_ref, f32[2,128,256]{2,1,0:T(8,128)} %get-tuple-element.38.refs_0_, f32[2,128,256]{2,1,0:T(8,128)} %copy-done, ...), custom_call_target="tpu_custom_call" | custom-call | tf_op jit(solution)/shard_map/prefix/pallas_call | solution.py:521
  55.8 4.5 %collective-permute-start.7 = (f32[2,128,128]{2,1,0:T(8,128)}, f32[2,128,128]{2,1,0:T(8,128)S(1)}, u32[]{:S(2)}, u32[]{:S(2)}) collective-permute-start(f32[2,128,128]{2,1,0:T(8,128)} %get-tuple-element.42), channel_id=1, source_target_pairs={{0,16},{4,20},{8,24},{12,28},{1,17},{5,21},{9,25},{13,29},{2,18},{... | collective-permute-start | bytes 393224 | tf_op jit(solution)/shard_map/ppermute | solution.py:523
  60.4 2.8 %collective-permute-done.7.entering_ref = f32[2,128,128]{2,1,0:T(8,128)S(1)} collective-permute-done((f32[2,128,128]{2,1,0:T(8,128)}, f32[2,128,128]{2,1,0:T(8,128)S(1)}, u32[]{:S(2)}, u32[]{:S(2)}) %collective-permute-start.7) | collective-permute-done | bytes 131104 | tf_op jit(solution)/shard_map/ppermute | solution.py:523
  63.2 0.6 copy-done.6
  63.8 3.8 %prefix.3 = (f32[2,128,128]{2,1,0:T(8,128)}, f32[2,128,128]{2,1,0:T(8,128)}, f32[2,128,128]{2,1,0:T(8,128)}, f32[2,128,128]{2,1,0:T(8,128)}, f32[2,128,128]{2,1,0:T(8,128)}) custom-call(f32[2,128,128]{2,1,0:T(8,128)} %copy-done.6, f32[2,128,256]{2,1,0:T(8,128)} %get-tuple-element.38.refs_0_, f32[2,128,256]{2,1,0:T(8,128)} %copy-done, ...), custom_call_target="tpu_custom_call" | custom-call | tf_op jit(solution)/shard_map/prefix/pallas_call | solution.py:524
  67.6 4.2 %collective-permute-start.10 = (f32[2,128,128]{2,1,0:T(8,128)}, f32[2,128,128]{2,1,0:T(8,128)S(1)}, u32[]{:S(2)}, u32[]{:S(2)}) collective-permute-start(f32[2,128,128]{2,1,0:T(8,128)} %get-tuple-element.46), channel_id=1, source_target_pairs={{0,12},{4,8},{8,4},{12,0},{16,28},{20,24},{24,20},{28,16},{1,13},{... | collective-permute-start | bytes 393224 | tf_op jit(solution)/shard_map/ppermute | solution.py:527
  71.8 1.2 %collective-permute-start.8 = (f32[2,128,128]{2,1,0:T(8,128)}, f32[2,128,128]{2,1,0:T(8,128)S(1)}, u32[]{:S(2)}, u32[]{:S(2)}) collective-permute-start(f32[2,128,128]{2,1,0:T(8,128)} %get-tuple-element.44), channel_id=1, source_target_pairs={{0,4},{4,0},{8,12},{12,8},{16,20},{20,16},{24,28},{28,24},{1,5},{5... | collective-permute-start | bytes 393224 | tf_op jit(solution)/shard_map/ppermute | solution.py:527
  73.0 8.3 %query.1.reads_ref = f32[4,2,512,256]{3,2,1,0:T(8,128)} custom-call(bf16[512,512]{1,0:T(8,128)(2,1)} %q_ref.3, bf16[16,2048]{1,0:T(8,128)(2,1)} %copy-done.7, bf16[4,512]{1,0:T(4,128)(2,1)} %qt_ref.1, f32[4,512,128]{2,1,0:T(8,128)} %get-tuple-element.27.refs_4_.unit_ref, f32[4,128,128]{2,1,0:T(8,128)} %get-tuple-element.34.first_ref, ...), custom_call_target="tpu_custom_call" | custom-call | flops 4000000000 | bytes 8000000 | tf_op jit(solution)/shard_map/query/pallas_call | solution.py:490
  81.3 0.6 copy-done.3
  81.9 0.0 copy-done.4
  82.0 0.0 copy-done.5
  82.0 9.8 %outputs.1 = f32[512,1024]{1,0:T(8,128)} custom-call(f32[4,2,512,256]{3,2,1,0:T(8,128)} %query.1.reads_ref, f32[4,2,3,128,256]{4,3,2,1,0:T(8,128)} %get-tuple-element.37.moves_ref, f32[2,128,128]{2,1,0:T(8,128)} %get-tuple-element.43.refs_0_, f32[2,128,128]{2,1,0:T(8,128)} %copy-done.4, f32[2,128,128]{2,1,0:T(8,128)} %copy-done.5, f32[2,128,128]{2,1,0:T(8,128)} %copy-done.3), custom_call_target="tpu_custom_call" | custom-call | tf_op jit(solution)/shard_map/outputs/pallas_call | solution.py:529
  (21 shorter events, 0.0 us)
Async XLA Ops:
  3.7 13.3 %collective-permute-start = (bf16[16,2048]{1,0:T(8,128)(2,1)}, bf16[16,2048]{1,0:T(8,128)(2,1)S(1)}, u32[]{:S(2)}, u32[]{:S(2)}) collective-permute-start(bf16[16,2048]{1,0:T(8,128)(2,1)} %get-tuple-element.26), channel_id=1, source_target_pairs={{0,4},{4,8},{8,12},{12,16},{16,20},{20,24},{24,28},{1,5},{5,9},{9,... | collective-permute-start | bytes 196616 | tf_op jit(solution)/shard_map/ppermute | solution.py:413
  8.6 8.5 %collective-permute-start.1 = (f32[16,512]{1,0:T(8,128)}, f32[16,512]{1,0:T(8,128)S(1)}, u32[]{:S(2)}, u32[]{:S(2)}) collective-permute-start(f32[16,512]{1,0:T(8,128)} %get-tuple-element.29), channel_id=1, source_target_pairs={{0,1},{1,0},{2,3},{3,2},{4,5},{5,4},{6,7},{7,6},{8,9},{9,8},{10,11... | collective-permute-start | bytes 98312 | tf_op jit(solution)/shard_map/ppermute | solution.py:410
  8.6 8.4 %collective-permute-start.2 = (f32[16,512]{1,0:T(8,128)}, f32[16,512]{1,0:T(8,128)S(1)}, u32[]{:S(2)}, u32[]{:S(2)}) collective-permute-start(f32[16,512]{1,0:T(8,128)} %get-tuple-element.30), channel_id=1, source_target_pairs={{0,2},{1,3},{2,0},{3,1},{4,6},{5,7},{6,4},{7,5},{8,10},{9,11},{10,... | collective-permute-start | bytes 98312 | tf_op jit(solution)/shard_map/ppermute | solution.py:410
  10.2 6.8 %collective-permute-start.3 = (f32[16,512]{1,0:T(8,128)}, f32[16,512]{1,0:T(8,128)S(1)}, u32[]{:S(2)}, u32[]{:S(2)}) collective-permute-start(f32[16,512]{1,0:T(8,128)} %get-tuple-element.31), channel_id=1, source_target_pairs={{0,3},{1,2},{2,1},{3,0},{4,7},{5,6},{6,5},{7,4},{8,11},{9,10},{10,... | collective-permute-start | bytes 98312 | tf_op jit(solution)/shard_map/ppermute | solution.py:410
  17.0 0.6 copy-start.8
  17.0 0.6 copy-start.9
  17.0 0.6 copy-start.10
  17.1 0.6 copy-start.7
  35.7 8.8 %collective-permute-start.4 = (f32[2,128,256]{2,1,0:T(8,128)}, f32[2,128,256]{2,1,0:T(8,128)S(1)}, u32[]{:S(2)}, u32[]{:S(2)}) collective-permute-start(f32[2,128,256]{2,1,0:T(8,128)} %get-tuple-element.39), channel_id=1, source_target_pairs={{0,4},{4,0},{8,12},{12,8},{16,20},{20,16},{24,28},{28,24},{1,5},{5... | collective-permute-start | bytes 786440 | tf_op jit(solution)/shard_map/ppermute | solution.py:487
  37.3 9.4 %collective-permute-start.5 = (f32[2,128,256]{2,1,0:T(8,128)}, f32[2,128,256]{2,1,0:T(8,128)S(1)}, u32[]{:S(2)}, u32[]{:S(2)}) collective-permute-start(f32[2,128,256]{2,1,0:T(8,128)} %get-tuple-element.40), channel_id=1, source_target_pairs={{0,8},{4,12},{8,0},{12,4},{16,24},{20,28},{24,16},{28,20},{1,9},{5... | collective-permute-start | bytes 786440 | tf_op jit(solution)/shard_map/ppermute | solution.py:487
  38.9 12.4 %collective-permute-start.6 = (f32[2,128,256]{2,1,0:T(8,128)}, f32[2,128,256]{2,1,0:T(8,128)S(1)}, u32[]{:S(2)}, u32[]{:S(2)}) collective-permute-start(f32[2,128,256]{2,1,0:T(8,128)} %get-tuple-element.41), channel_id=1, source_target_pairs={{0,12},{4,8},{8,4},{12,0},{16,28},{20,24},{24,20},{28,16},{1,13},{... | collective-permute-start | bytes 786440 | tf_op jit(solution)/shard_map/ppermute | solution.py:487
  44.5 7.5 %copy-start = (f32[2,128,256]{2,1,0:T(8,128)}, f32[2,128,256]{2,1,0:T(8,128)S(1)}, u32[]{:S(2)}) copy-start(f32[2,128,256]{2,1,0:T(8,128)S(1)} %collective-permute-done.4.refs_1_) | copy-start | bytes 786436
  46.7 5.4 %copy-start.1 = (f32[2,128,256]{2,1,0:T(8,128)}, f32[2,128,256]{2,1,0:T(8,128)S(1)}, u32[]{:S(2)}) copy-start(f32[2,128,256]{2,1,0:T(8,128)S(1)} %collective-permute-done.5.refs_2_) | copy-start | bytes 786436
  51.3 0.8 copy-start.2
  55.8 7.3 %collective-permute-start.7 = (f32[2,128,128]{2,1,0:T(8,128)}, f32[2,128,128]{2,1,0:T(8,128)S(1)}, u32[]{:S(2)}, u32[]{:S(2)}) collective-permute-start(f32[2,128,128]{2,1,0:T(8,128)} %get-tuple-element.42), channel_id=1, source_target_pairs={{0,16},{4,20},{8,24},{12,28},{1,17},{5,21},{9,25},{13,29},{2,18},{... | collective-permute-start | bytes 393224 | tf_op jit(solution)/shard_map/ppermute | solution.py:523
  63.2 0.7 copy-start.6
  67.6 13.7 %collective-permute-start.10 = (f32[2,128,128]{2,1,0:T(8,128)}, f32[2,128,128]{2,1,0:T(8,128)S(1)}, u32[]{:S(2)}, u32[]{:S(2)}) collective-permute-start(f32[2,128,128]{2,1,0:T(8,128)} %get-tuple-element.46), channel_id=1, source_target_pairs={{0,12},{4,8},{8,4},{12,0},{16,28},{20,24},{24,20},{28,16},{1,13},{... | collective-permute-start | bytes 393224 | tf_op jit(solution)/shard_map/ppermute | solution.py:527
  71.8 9.5 %collective-permute-start.8 = (f32[2,128,128]{2,1,0:T(8,128)}, f32[2,128,128]{2,1,0:T(8,128)S(1)}, u32[]{:S(2)}, u32[]{:S(2)}) collective-permute-start(f32[2,128,128]{2,1,0:T(8,128)} %get-tuple-element.44), channel_id=1, source_target_pairs={{0,4},{4,0},{8,12},{12,8},{16,20},{20,16},{24,28},{28,24},{1,5},{5... | collective-permute-start | bytes 393224 | tf_op jit(solution)/shard_map/ppermute | solution.py:527
  73.0 8.3 %collective-permute-start.9 = (f32[2,128,128]{2,1,0:T(8,128)}, f32[2,128,128]{2,1,0:T(8,128)S(1)}, u32[]{:S(2)}, u32[]{:S(2)}) collective-permute-start(f32[2,128,128]{2,1,0:T(8,128)} %get-tuple-element.45), channel_id=1, source_target_pairs={{0,8},{4,12},{8,0},{12,4},{16,24},{20,28},{24,16},{28,20},{1,9},{5... | collective-permute-start | bytes 393224 | tf_op jit(solution)/shard_map/ppermute | solution.py:527
  81.3 0.7 copy-start.3
  81.3 0.7 copy-start.4
  81.3 0.7 copy-start.5

commit v2 on v1

--- a/solution.py
+++ b/solution.py
@@ -61,15 +61,31 @@
     )
 
 
+def slot_partner(group, slot):
+    order = [d for d in range(group - 1, 0, -1) if d % 2] + [
+        d for d in range(group - 1, 0, -1) if d % 2 == 0
+    ]
+    return (order + [0])[slot]
+
+
+def solve_calls(group):
+    half = group // 2
+    return [tuple(range(half))] + [(s,) for s in range(half, group)]
+
+
+def in_hbm(x):
+    return pltpu.with_memory_space_constraint(x, pltpu.HBM)
+
+
 def lanes(start, size):
     return pl.ds(pl.multiple_of(start, 128), size)
 
 
 def logits_kernel(head_count, hidden_ref, proj_ref, q_ref, k_ref, v_ref, *refs):
     outs, tail_ref, held = refs[:head_count], refs[head_count], refs[head_count + 1]
-    rows = proj_ref.shape[1] // head_count
+    rows = proj_ref.shape[0] // head_count
     everything = lax.dot_general(
-        proj_ref[...], hidden_ref[...], (((0,), (1,)), ((), ())), preferred_element_type=f32
+        proj_ref[...], hidden_ref[...], (NT, ((), ())), preferred_element_type=f32
     )
     for m in range(head_count):
         held[m] = everything[m * rows : (m + 1) * rows]
@@ -160,7 +176,7 @@
     )
     count = len(slots)
     message_refs, refs = refs[:count], refs[count:]
-    solved_ref, moves_ref, cumulative_ref, first_ref, padded = refs
+    solved_ref, starts_ref, cumulative_ref, first_ref, padded = refs
     tokens = unit_ref.shape[1]
     blocks = tokens // BLOCK
     key_width = kt_ref.shape[1]
@@ -172,7 +188,7 @@
 
     systems, rights, tails, ends, key_parts = [], [], [], [], []
     for at, s in enumerate(slots):
-        p = place ^ (group - 1 - s)
+        p = place ^ slot_partner(group, s)
         kcol, vcol = p * DK, p * 2 * DV
         padded[0:8, 0:DK] = before_ref[:, lanes(key_width + kcol, DK)].astype(f32)[EDGE - 8 :]
         padded[0:8, DK:] = before_ref[:, lanes(2 * key_width + vcol, 2 * DV)].astype(f32)[EDGE - 8 :]
@@ -252,13 +268,10 @@
                     - grown[:, b * 2 * DK + DV : (b + 1) * 2 * DK]
                 )
                 moves[b, c] = (added, move)
-                if c < blocks - 1:
-                    moves_ref[at, b, c, :, 0:DV] = added
-                    moves_ref[at, b, c, :, DV:] = move
         for b in range(2):
-            added, move = moves[b, 0]
-            both = jnp.concatenate([added, move], axis=1)
+            both = jnp.concatenate(moves[b, 0], axis=1)
             for c in range(1, blocks):
+                starts_ref[at, b, c - 1] = both
                 added, move = moves[b, c]
                 both = dot_split(split(move), split(both))
                 both = jnp.concatenate([both[:, :DV] + added, both[:, DV:]], axis=1)
@@ -266,42 +279,64 @@
 
 
 def query_kernel(
-    group, q_ref, before_ref, qt_ref, unit_ref, first_ref, cumulative_ref, solved_ref, out_ref, padded
+    slots,
+    group,
+    q_ref,
+    before_ref,
+    qt_ref,
+    unit_ref,
+    first_ref,
+    cumulative_ref,
+    solved_ref,
+    starts_ref,
+    own_ref,
+    high_ref,
+    low_ref,
+    padded,
 ):
-    s = pl.program_id(0)
     place = lax.axis_index("seq") % group
-    p = place ^ (group - 1 - s)
     tokens = q_ref.shape[0]
     blocks = tokens // BLOCK
-    columns = lanes(p * DK, DK)
-    padded[0:8] = before_ref[:, columns].astype(f32)[EDGE - 8 :]
-    padded[8:] = q_ref[:, columns].astype(f32)
-    taps = qt_ref[:, columns].astype(f32)
-    queries = unit(conv_rows(padded, taps, tokens, slice(None)), 1.0 / math.sqrt(DK))
     row, column = iotas()
     causal = row >= column
-    sums = cumulative_ref[0]
-    cum_columns = jnp.transpose(sums)
-    growth_columns = jnp.exp(cum_columns)
-    for c in range(blocks):
-        here = queries[c * BLOCK : (c + 1) * BLOCK]
-        keys = first_ref[0] if c == 0 else unit_ref[p, pl.ds(c * BLOCK, BLOCK), :]
-        dots = dot_split(split(here), split(keys), NT)
-        for b in range(2):
-            r = b * blocks + c
-            spread = cum_columns[:, r : r + 1] - sums[r : r + 1, :]
-            attend = dots * jnp.exp(jnp.where(causal, spread, FAR))
-            seen = dot_split(split(attend), split(solved_ref[0, b, pl.ds(c * BLOCK, BLOCK), :]))
-            out_ref[0, b, pl.ds(c * BLOCK, BLOCK), 0:DV] = seen[:, :DV]
-            out_ref[0, b, pl.ds(c * BLOCK, BLOCK), DV:] = (
-                growth_columns[:, r : r + 1] * here - seen[:, DV:]
-            )
-
-
-def prefix_kernel(group, entering_ref, *refs):
+    work = []
+    for at, s in enumerate(slots):
+        p = place ^ slot_partner(group, s)
+        columns = lanes(p * DK, DK)
+        padded[0:8] = before_ref[:, columns].astype(f32)[EDGE - 8 :]
+        padded[8:] = q_ref[:, columns].astype(f32)
+        taps = qt_ref[:, columns].astype(f32)
+        queries = unit(conv_rows(padded, taps, tokens, slice(None)), 1.0 / math.sqrt(DK))
+        sums = cumulative_ref[at]
+        cum_columns = jnp.transpose(sums)
+        growth_columns = jnp.exp(cum_columns)
+        for c in range(blocks):
+            here = queries[c * BLOCK : (c + 1) * BLOCK]
+            keys = first_ref[at] if c == 0 else unit_ref[p, pl.ds(c * BLOCK, BLOCK), :]
+            dots = dot_split(split(here), split(keys), NT)
+            for b in range(2):
+                r = b * blocks + c
+                spread = cum_columns[:, r : r + 1] - sums[r : r + 1, :]
+                attend = dots * jnp.exp(jnp.where(causal, spread, FAR))
+                grown = growth_columns[:, r : r + 1] * here
+                work.append((at, b, c, split(attend), grown))
+    seen = [
+        dot_split(attend, split(solved_ref[at, b, pl.ds(c * BLOCK, BLOCK), :]))
+        for at, b, c, attend, grown in work
+    ]
+    for (at, b, c, attend, grown), one in zip(work, seen):
+        own, reads = one[:, :DV], grown - one[:, DV:]
+        if c > 0:
+            through = dot_split(split(reads), split(starts_ref[at, b, c - 1]))
+            own, reads = own + through[:, :DV], through[:, DV:]
+        here = pl.ds(c * BLOCK, BLOCK)
+        own_ref[at, b, here, :] = own
+        high_ref[at, b, here, :], low_ref[at, b, here, :] = split(reads)
+
+
+def prefix_kernel(group, *refs):
     messages, refs = refs[:group], refs[group:]
-    outs, refs = refs[: group + 1], refs[group + 1 :]
-    held, sems = refs
+    chain_ref, leaving_ref, held, sems = refs
     place = lax.axis_index("seq") % group
     copies = [
         pltpu.make_async_copy(messages[d], held.at[place ^ d], sems.at[d]) for d in range(group)
@@ -310,52 +345,62 @@
         copy.start()
     for copy in copies:
         copy.wait()
-    heads = entering_ref.shape[0]
-    states = [entering_ref[b] for b in range(heads)]
-    chain = []
-    for i in range(group):
-        chain.append(states)
-        states = [
-            held[i, b, :, 0:DV] + dot_split(split(held[i, b, :, DV:]), split(states[b]))
+    heads = leaving_ref.shape[0]
+    chain = [held[0, b] for b in range(heads)]
+    for i in range(1, group):
+        for b in range(heads):
+            chain_ref[i - 1, b] = chain[b]
+        chain = [
+            dot_split(split(held[i, b, :, DV:]), split(chain[b])) for b in range(heads)
+        ]
+        chain = [
+            jnp.concatenate([chain[b][:, :DV] + held[i, b, :, 0:DV], chain[b][:, DV:]], axis=1)
             for b in range(heads)
         ]
     for b in range(heads):
-        outs[group][b] = states[b]
+        chain_ref[group - 1, b] = chain[b]
+        leaving_ref[b] = chain[b][:, :DV]
+
+
+def enter_kernel(group, entering_ref, chain_ref, *refs):
+    *outs, leaving_ref = refs
+    place = lax.axis_index("seq") % group
+    heads = entering_ref.shape[0]
+    states = [[entering_ref[b] for b in range(heads)]] + [[] for i in range(group)]
+    for b in range(heads):
+        moves = jnp.concatenate([chain_ref[i, b, :, DV:] for i in range(group)], axis=0)
+        moved = dot_split(split(moves), split(states[0][b]))
+        for i in range(group):
+            states[i + 1].append(chain_ref[i, b, :, 0:DV] + moved[i * DK : (i + 1) * DK])
+    for b in range(heads):
+        leaving_ref[b] = states[group][b]
     for j in range(group):
 
         @pl.when(place == j)
         def _():
             for i in range(group):
                 for b in range(heads):
-                    outs[j ^ i][b] = chain[i][b]
-
-
-def output_kernel(group, reads_ref, moves_ref, *refs):
-    entering, (out_ref,) = refs[:group], refs[group:]
+                    outs[j ^ i][b] = states[i][b]
+
+
+def output_kernel(group, calls, *refs):
+    reads, entering, (out_ref,) = refs[: 3 * len(calls)], refs[3 * len(calls) : -1], refs[-1:]
     place = lax.axis_index("seq") % group
-    tokens = out_ref.shape[0]
-    blocks = tokens // BLOCK
-    for s in range(group):
-        p = place ^ (group - 1 - s)
-        for b in range(2):
-            state = entering[group - 1 - s][b]
-            for c in range(blocks):
-                reads = reads_ref[s, b, pl.ds(c * BLOCK, BLOCK), DV:]
-                if c < blocks - 1:
-                    reads = jnp.concatenate([reads, moves_ref[s, b, c, :, DV:]], axis=0)
-                product = dot_split(split(reads), split(state))
-                out_ref[pl.ds(c * BLOCK, BLOCK), lanes(p * 2 * DV + b * DV, DV)] = (
-                    reads_ref[s, b, pl.ds(c * BLOCK, BLOCK), 0:DV] + product[:BLOCK]
-                )
-                if c < blocks - 1:
-                    state = moves_ref[s, b, c, :, 0:DV] + product[BLOCK:]
+    for k, slots in enumerate(calls):
+        own_ref, high_ref, low_ref = reads[3 * k : 3 * k + 3]
+        for at, s in enumerate(slots):
+            d = slot_partner(group, s)
+            p = place ^ d
+            for b in range(2):
+                product = dot_split((high_ref[at, b], low_ref[at, b]), split(entering[d][b]))
+                out_ref[:, lanes(p * 2 * DV + b * DV, DV)] = own_ref[at, b] + product
 
 
 def shape(*dims, dtype=f32):
     return jax.ShapeDtypeStruct(dims, dtype)
 
 
-def params(mib=56):
+def params(mib=24):
     return pltpu.CompilerParams(vmem_limit_bytes=mib << 20)
 
 
@@ -392,7 +437,7 @@
         grid=(1,),
         in_specs=[
             full(hidden_states.shape),
-            full(proj_ba.shape),
+            full(proj_ba.shape[::-1]),
             pl.BlockSpec((EDGE, key_width), lambda i: (last_rows, 0)),
             pl.BlockSpec((EDGE, key_width), lambda i: (last_rows, 0)),
             pl.BlockSpec((EDGE, value_width), lambda i: (last_rows, 0)),
@@ -404,7 +449,7 @@
         scratch_shapes=[VMEM((head_count, 2 * heads, tokens), f32)],
         compiler_params=params(),
         name="logits",
-    )(hidden_states, proj_ba, query_in, key_in, value_in)
+    )(in_hbm(hidden_states), in_hbm(proj_ba.T), in_hbm(query_in), in_hbm(key_in), in_hbm(value_in))
 
     logits = [partial[0]] + [
         lax.ppermute(partial[d], "head", [(i, i ^ d) for i in range(head_count)])
@@ -437,7 +482,7 @@
             flops=4_000_000_000, bytes_accessed=6_000_000, transcendentals=0
         ),
         name="mix",
-    )(key_in, value_in, conv_key, convolution_value_taps)
+    )(in_hbm(key_in), in_hbm(value_in), in_hbm(conv_key), in_hbm(convolution_value_taps))
 
     def solve(slots):
         count = len(slots)
@@ -462,7 +507,7 @@
             scratch_shapes=[VMEM((EDGE + 8, DK + 2 * DV), f32)],
             compiler_params=params(),
             cost_estimate=pl.CostEstimate(
-                flops=4_000_000_000 * count, bytes_accessed=4_000_000 * count, transcendentals=0
+                flops=4_000_000_000 * count, bytes_accessed=2_000_000 * count, transcendentals=0
             ),
             name="solve",
         )(
@@ -472,68 +517,81 @@
             unit_keys,
             key_dots,
             mixed,
-            key_in,
-            value_in,
+            in_hbm(key_in),
+            in_hbm(value_in),
             before,
-            conv_key,
-            convolution_value_taps,
+            in_hbm(conv_key),
+            in_hbm(convolution_value_taps),
         )
 
-    *messages, solved, moves, cumulative, first_keys = solve(tuple(range(group)))
-
-    arrived = [messages[group - 1]]
-    for d in range(1, group):
-        arrived.append(
-            lax.ppermute(messages[group - 1 - d], "seq", [(i, i ^ d) for i in range(seq)])
+    def query(slots, solved, starts, cumulative, first_keys):
+        count = len(slots)
+        return pl.pallas_call(
+            functools.partial(query_kernel, slots, group),
+            in_specs=[whole()] * 8,
+            out_specs=[whole()] * 3,
+            out_shape=[shape(count, 2, tokens, DV)]
+            + [shape(count, 2, tokens, DK, dtype=bf16)] * 2,
+            scratch_shapes=[VMEM((tokens + 8, DK), f32)],
+            compiler_params=params(),
+            cost_estimate=pl.CostEstimate(
+                flops=2_000_000_000 * count, bytes_accessed=2_000_000 * count, transcendentals=0
+            ),
+            name="query",
+        )(in_hbm(query_in), before, in_hbm(conv_query), unit_keys, first_keys, cumulative, solved, starts)
+
+    calls = solve_calls(group)
+    messages, rest = [], []
+    for slots in calls:
+        results = solve(slots)
+        messages += results[: len(slots)]
+        rest.append(results[len(slots) :])
+
+    arrived = [None] * group
+    for s in range(group):
+        d = slot_partner(group, s)
+        arrived[d] = (
+            lax.ppermute(messages[s], "seq", [(i, i ^ d) for i in range(seq)]) if d else messages[s]
         )
 
-    reads = pl.pallas_call(
-        functools.partial(query_kernel, group),
-        grid=(pairs,),
-        in_specs=[
-            full(query_in.shape),
-            full(tail.shape),
-            full(conv_query.shape),
-            full(unit_keys.shape),
-            pl.BlockSpec((1, BLOCK, DK), lambda i: (i, 0, 0)),
-            pl.BlockSpec((1, 2 * blocks, BLOCK), lambda i: (i, 0, 0)),
-            pl.BlockSpec((1, 2, tokens, 2 * DK), lambda i: (i, 0, 0, 0)),
-        ],
-        out_specs=pl.BlockSpec((1, 2, tokens, 2 * DK), lambda i: (i, 0, 0, 0)),
-        out_shape=shape(pairs, 2, tokens, 2 * DK),
-        scratch_shapes=[VMEM((tokens + 8, DK), f32)],
-        compiler_params=params(),
-        cost_estimate=pl.CostEstimate(
-            flops=4_000_000_000, bytes_accessed=8_000_000, transcendentals=0
-        ),
-        name="query",
-    )(query_in, before, conv_query, unit_keys, first_keys, cumulative, solved)
-
-    prefix = pl.pallas_call(
+    reads = [query(calls[0], *rest[0])]
+    arrived, reads[0] = lax.optimization_barrier((arrived, reads[0]))
+    chain, leaving = pl.pallas_call(
         functools.partial(prefix_kernel, group),
-        in_specs=[whole()] + [whole(pl.ANY)] * group,
-        out_specs=[whole()] * (group + 1),
-        out_shape=[shape(2, DK, DV)] * (group + 1),
+        in_specs=[whole(pl.ANY)] * group,
+        out_specs=[whole()] * 2,
+        out_shape=[shape(group, 2, DK, 2 * DK), shape(2, DK, DV)],
         scratch_shapes=[VMEM((group, 2, DK, 2 * DK), f32), pltpu.SemaphoreType.DMA((group,))],
         compiler_params=params(),
         name="prefix",
-    )
-    *entering, leaving = prefix(jnp.zeros((2, DK, DV), f32), *arrived)
-    for _ in range(seq // group - 1):
+    )(*arrived)
+    enter = pl.pallas_call(
+        functools.partial(enter_kernel, group),
+        in_specs=[whole()] * 2,
+        out_specs=[whole()] * (group + 1),
+        out_shape=[shape(2, DK, DV)] * (group + 1),
+        compiler_params=params(),
+        name="enter",
+    )
+    for hop in range(seq // group - 1):
         received = lax.ppermute(leaving, "seq", [(i, i + group) for i in range(seq - group)])
-        *entering, leaving = prefix(received, *arrived)
+        if hop == 0:
+            reads += [query(slots, *outs) for slots, outs in zip(calls[1:-1], rest[1:-1])]
+            received, reads = lax.optimization_barrier((received, reads))
+        *entering, leaving = enter(received, chain)
 
     states = [entering[0]] + [
         lax.ppermute(entering[d], "seq", [(i, i ^ d) for i in range(seq)]) for d in range(1, group)
     ]
+    reads.append(query(calls[-1], *rest[-1]))
     return pl.pallas_call(
-        functools.partial(output_kernel, group),
-        in_specs=[whole()] * (2 + group),
+        functools.partial(output_kernel, group, calls),
+        in_specs=[whole()] * (3 * len(calls) + group),
         out_specs=whole(),
         out_shape=shape(tokens, value_width),
         compiler_params=params(),
         name="outputs",
-    )(reads, moves, *states)
+    )(*[x for three in reads for x in three], *states)
 
 
 def solution(mesh):

time: 92.3 us -> 63.1 us (0.68)
  Pallas kernels: 52.1 us -> 35.5 us
  waiting for transfers between devices: 14.9 us -> 7.82 us
  local copies, waits for them, and re-layouts: 4.37 us -> 0.01 us
  starting transfers between devices: 20.3 us -> 19.2 us
    pallas_call x4 -> x6, Pallas kernels: 25.5 us -> 11.5 us  [the longest x3 7.37 us: query(): pl.pallas_call(functools.partial(query_kernel, slots, group), in_specs=[w...]
    ppermute x3, waiting for transfers between devices: 12.1 us -> 3.76 us  [per_device(): lax.ppermute(messages[s], 'seq', [(i, i ^ d) for i in range(seq)])]
    ppermute x3, waiting for transfers between devices: 0.01 us -> 3.7 us  [per_device(): lax.ppermute(entering[d], 'seq', [(i, i ^ d) for i in range(seq)])]
    unnamed x23 -> x4, local copies, waits for them, and re-layouts: 3.65 us -> 0.01 us
    ppermute x1, waiting for transfers between devices: 2.81 us -> 0.35 us  [per_device(): lax.ppermute(leaving, 'seq', [(i, i + group) for i in range(seq - group)])]
    ppermute x3, starting transfers between devices: 5.43 us -> 4.14 us  [per_device(): lax.ppermute(entering[d], 'seq', [(i, i ^ d) for i in range(seq)])]
    ppermute x3, starting transfers between devices: 1.93 us -> 3.18 us  [per_device(): lax.ppermute(partial[d], 'head', [(i, i ^ d) for i in range(head_count)])]
    ppermute x1, starting transfers between devices: 4.83 us -> 3.72 us  [per_device(): before = lax.ppermute(tail, 'seq', [(i, i + 1) for i in range(seq - 1)])]
  transfers between devices with their start and end apart: 11 -> 11, of which waited for: 4 -> 4; matrix products, arithmetic and copies ran while one was open for 0% -> 0% of each run, Pallas kernels for 16% -> 40%
where the time goes in v2:
time: 63.1 us; the launch traced here: 62.7 us
  Pallas kernels  35.5 us (56%)
  starting transfers between devices  19.2 us (30%)
  waiting for transfers between devices  7.82 us (12%)
    pallas_call x3, Pallas kernels, solve(): pl.pallas_call(functools.partial(solve_kernel, slots, group, head_count),...  17.1 us
    pallas_call x3, Pallas kernels, query(): pl.pallas_call(functools.partial(query_kernel, slots, group), in_specs=[w...  7.37 us
    pallas_call x1, Pallas kernels, per_device(): pl.pallas_call(mix_kernel, grid=(pairs,), in_specs=[pl.BlockSpec((tokens,...  5.49 us
    ppermute x1, starting transfers between devices, per_device(): lax.ppermute(leaving, 'seq', [(i, i + group) for i in range(seq - group)])  4.5 us
    ppermute x3, starting transfers between devices, per_device(): lax.ppermute(entering[d], 'seq', [(i, i ^ d) for i in range(seq)])  4.14 us
    ppermute x3, waiting for transfers between devices, per_device(): lax.ppermute(messages[s], 'seq', [(i, i ^ d) for i in range(seq)])  3.76 us
    ppermute x1, starting transfers between devices, per_device(): before = lax.ppermute(tail, 'seq', [(i, i + 1) for i in range(seq - 1)])  3.72 us
    ppermute x3, waiting for transfers between devices, per_device(): lax.ppermute(entering[d], 'seq', [(i, i ^ d) for i in range(seq)])  3.7 us
  transfers between devices with their start and end apart: 11, of which 4 were waited for; matrix products, arithmetic and copies ran while one was open for 0% of the time, Pallas kernels for 40%

profile of v2, /device:TPU:0, one launch (start us, length us, event | category | flops | bytes accessed | tf_op | source)
XLA Modules:
  0.0 62.7 jit_solution(2649658562313083533)
XLA Ops:
  0.0 1.4 %logits.1 = (f32[16,512]{1,0:T(8,128)S(1)}, f32[16,512]{1,0:T(8,128)S(1)}, f32[16,512]{1,0:T(8,128)S(1)}, f32[16,512]{1,0:T(8,128)S(1)}, bf16[16,2048]{1,0:T(8,128)(2,1)S(1)}) custom-call(bf16[512,512]{1,0:T(8,128)(2,1)} %hidden_ref.1, bf16[64,512]{1,0:T(8,128)(2,1)} %bitcast.1, bf16[512,512]{1,0:T(8,128)(2,1)} %q_ref.7, bf16[512,512]{1,0:T(8,128)(2,1)} %refs_7_.5, ...), custom_call_target="tpu_custom_call" | custom-call | tf_op jit(solution)/shard_map/logits/pallas_call | solution.py:435
  1.4 0.5 collective-permute-start
  1.9 2.6 %collective-permute-start.1 = (f32[16,512]{1,0:T(8,128)S(1)}, f32[16,512]{1,0:T(8,128)S(1)}, u32[]{:S(2)}, u32[]{:S(2)}) collective-permute-start(f32[16,512]{1,0:T(8,128)S(1)} %get-tuple-element.60), channel_id=1, source_target_pairs={{0,2},{1,3},{2,0},{3,1},{4,6},{5,7},{6,4},{7,5},{8,10},{9,11},{10,... | collective-permute-start | bytes 98312 | tf_op jit(solution)/shard_map/ppermute | solution.py:455
  4.5 0.1 collective-permute-start.2
  4.6 3.7 %collective-permute-start.3 = (bf16[16,2048]{1,0:T(8,128)(2,1)S(1)}, bf16[16,2048]{1,0:T(8,128)(2,1)S(1)}, u32[]{:S(2)}, u32[]{:S(2)}) collective-permute-start(bf16[16,2048]{1,0:T(8,128)(2,1)S(1)} %get-tuple-element.65), channel_id=1, source_target_pairs={{0,4},{4,8},{8,12},{12,16},{16,20},{20,24},{24,28},{1,5},{5,9},{9,... | collective-permute-start | bytes 196616 | tf_op jit(solution)/shard_map/ppermute | solution.py:458
  8.3 5.5 %mix.1 = (f32[4,512,128]{2,1,0:T(8,128)S(1)}, f32[4,4,128,128]{3,2,1,0:T(8,128)S(1)}, f32[4,512,256]{2,1,0:T(8,128)S(1)}) custom-call(bf16[512,512]{1,0:T(8,128)(2,1)} %refs_7_.5, bf16[512,1024]{1,0:T(8,128)(2,1)} %refs_8_.5, bf16[4,512]{1,0:T(4,128)(2,1)} %refs_10_.5, bf16[4,1024]{1,0:T(4,128)(2,1)} %refs_11_.5), custom_call_target="tpu_custom_call" | custom-call | flops 4000000000 | bytes 6000000 | tf_op jit(solution)/shard_map/mix/pallas_call | solution.py:460
  13.8 0.0 collective-permute-done.refs_1_
  13.8 0.0 collective-permute-done.1.refs_2_
  13.8 0.0 collective-permute-done.2.refs_3_
  13.9 0.0 collective-permute-done.3.refs_9_.before_ref
  13.9 4.7 %solve.5 = (f32[2,128,256]{2,1,0:T(8,128)S(1)}, f32[1,2,512,256]{3,2,1,0:T(8,128)S(1)}, f32[1,2,3,128,256]{4,3,2,1,0:T(8,128)S(1)}, f32[1,8,128]{2,1,0:T(8,128)S(1)}, f32[1,128,128]{2,1,0:T(8,128)S(1)}) custom-call(f32[8]{0:T(128)S(1)} %copy-done, f32[8]{0:T(128)S(1)} %copy-done.1, f32[16,512]{1,0:T(8,128)S(1)} %get-tuple-element.58.refs_0_, ...), custom_call_target="tpu_custom_call" | custom-call | flops 4000000000 | bytes 2000000 | tf_op jit(solution)/shard_map/solve/pallas_call | solution.py:489
  18.6 1.6 %collective-permute-start.5 = (f32[2,128,256]{2,1,0:T(8,128)S(1)}, f32[2,128,256]{2,1,0:T(8,128)S(1)}, u32[]{:S(2)}, u32[]{:S(2)}) collective-permute-start(f32[2,128,256]{2,1,0:T(8,128)S(1)} %get-tuple-element.68), channel_id=1, source_target_pairs={{0,8},{4,12},{8,0},{12,4},{16,24},{20,28},{24,16},{28,20},{1,9},{5... | collective-permute-start | bytes 786440 | tf_op jit(solution)/shard_map/ppermute | solution.py:554
  20.2 7.6 %solve.4 = (f32[2,128,256]{2,1,0:T(8,128)S(1)}, f32[2,128,256]{2,1,0:T(8,128)S(1)}, f32[2,2,512,256]{3,2,1,0:T(8,128)S(1)}, f32[2,2,3,128,256]{4,3,2,1,0:T(8,128...) custom-call(f32[8]{0:T(128)S(1)} %copy-done, f32[8]{0:T(128)S(1)} %copy-done.1, ...), custom_call_target="tpu_custom_call" | custom-call | flops 8000000000 | bytes 4000000 | tf_op jit(solution)/shard_map/solve/pallas_call | solution.py:489
  27.8 1.6 %collective-permute-start.4 = (f32[2,128,256]{2,1,0:T(8,128)S(1)}, f32[2,128,256]{2,1,0:T(8,128)S(1)}, u32[]{:S(2)}, u32[]{:S(2)}) collective-permute-start(f32[2,128,256]{2,1,0:T(8,128)S(1)} %get-tuple-element.67), channel_id=1, source_target_pairs={{0,4},{4,0},{8,12},{12,8},{16,20},{20,16},{24,28},{28,24},{1,5},{5... | collective-permute-start | bytes 786440 | tf_op jit(solution)/shard_map/ppermute | solution.py:554
  29.4 0.4 collective-permute-start.6
  29.8 4.9 %solve.3 = (f32[2,128,256]{2,1,0:T(8,128)S(1)}, f32[1,2,512,256]{3,2,1,0:T(8,128)S(1)}, f32[1,2,3,128,256]{4,3,2,1,0:T(8,128)S(1)}, f32[1,8,128]{2,1,0:T(8,128)S(1)}, f32[1,128,128]{2,1,0:T(8,128)S(1)}) custom-call(f32[8]{0:T(128)S(1)} %copy-done, f32[8]{0:T(128)S(1)} %copy-done.1, f32[16,512]{1,0:T(8,128)S(1)} %get-tuple-element.58.refs_0_, ...), custom_call_target="tpu_custom_call" | custom-call | flops 4000000000 | bytes 2000000 | tf_op jit(solution)/shard_map/solve/pallas_call | solution.py:489
  34.7 3.1 %query.3 = (f32[2,2,512,128]{3,2,1,0:T(8,128)S(1)}, bf16[2,2,512,128]{3,2,1,0:T(8,128)(2,1)S(1)}, bf16[2,2,512,128]{3,2,1,0:T(8,128)(2,1)S(1)}) custom-call(bf16[512,512]{1,0:T(8,128)(2,1)} %q_ref.7, bf16[16,2048]{1,0:T(8,128)(2,1)S(1)} %collective-permute-done.3.refs_9_.before_ref, bf16[4,512]{1,0:T(4,128)(2,1)} %qt_ref.5, ...), custom_call_target="tpu_custom_call" | custom-call | flops 4000000000 | bytes 4000000 | tf_op jit(solution)/shard_map/query/pallas_call | solution.py:529
  37.7 0.0 collective-permute-done.5.refs_2_
  37.7 3.8 %collective-permute-done.4.refs_1_ = f32[2,128,256]{2,1,0:T(8,128)S(1)} collective-permute-done((f32[2,128,256]{2,1,0:T(8,128)S(1)}, f32[2,128,256]{2,1,0:T(8,128)S(1)}, u32[]{:S(2)}, u32[]{:S(2)}) %collective-permute-start.4) | collective-permute-done | bytes 262176 | tf_op jit(solution)/shard_map/ppermute | solution.py:554
  41.5 0.8 %prefix.1 = (f32[4,2,128,256]{3,2,1,0:T(8,128)S(1)}, f32[2,128,128]{2,1,0:T(8,128)S(1)}) custom-call(f32[2,128,256]{2,1,0:T(8,128)S(1)} %get-tuple-element.77.refs_0_, f32[2,128,256]{2,1,0:T(8,128)S(1)} %collective-permute-done.4.refs_1_, f32[2,128,256]{2,1,0:T(8,128)S(1)} %collective-permute-done.5.refs_2_, f32[2,128,256]{2,1,0:T(8,128)S(1)} %collective-permute-done.6.refs_3_), custom_call_target="tpu_custom_call" | custom-call | tf_op jit(solution)/shard_map/prefix/pallas_call | solution.py:559
  42.3 4.5 %collective-permute-start.7 = (f32[2,128,128]{2,1,0:T(8,128)S(1)}, f32[2,128,128]{2,1,0:T(8,128)S(1)}, u32[]{:S(2)}, u32[]{:S(2)}) collective-permute-start(f32[2,128,128]{2,1,0:T(8,128)S(1)} %get-tuple-element.81), channel_id=1, source_target_pairs={{0,16},{4,20},{8,24},{12,28},{1,17},{5,21},{9,25},{13,29},{2,18},{... | collective-permute-start | bytes 393224 | tf_op jit(solution)/shard_map/ppermute | solution.py:577
  46.8 2.2 %query.4 = (f32[1,2,512,128]{3,2,1,0:T(8,128)S(1)}, bf16[1,2,512,128]{3,2,1,0:T(8,128)(2,1)S(1)}, bf16[1,2,512,128]{3,2,1,0:T(8,128)(2,1)S(1)}) custom-call(bf16[512,512]{1,0:T(8,128)(2,1)} %q_ref.7, bf16[16,2048]{1,0:T(8,128)(2,1)S(1)} %collective-permute-done.3.refs_9_.before_ref, bf16[4,512]{1,0:T(4,128)(2,1)} %qt_ref.5, ...), custom_call_target="tpu_custom_call" | custom-call | flops 2000000000 | bytes 2000000 | tf_op jit(solution)/shard_map/query/pallas_call | solution.py:529
  49.0 0.3 collective-permute-done.7.entering_ref
  49.3 1.0 %enter.1 = (f32[2,128,128]{2,1,0:T(8,128)S(1)}, f32[2,128,128]{2,1,0:T(8,128)S(1)}, f32[2,128,128]{2,1,0:T(8,128)S(1)}, f32[2,128,128]{2,1,0:T(8,128)S(1)}, f32[2,128,128]{2,1,0:T(8,128)}) custom-call(f32[2,128,128]{2,1,0:T(8,128)S(1)} %collective-permute-done.7.entering_ref, f32[4,2,128,256]{3,2,1,0:T(8,128)S(1)} %get-tuple-element.106.chain_ref), custom_call_target="tpu_custom_call" | custom-call | tf_op jit(solution)/shard_map/enter/pallas_call | solution.py:581
  50.4 0.3 collective-permute-start.8
  50.7 3.9 %collective-permute-start.9 = (f32[2,128,128]{2,1,0:T(8,128)S(1)}, f32[2,128,128]{2,1,0:T(8,128)S(1)}, u32[]{:S(2)}, u32[]{:S(2)}) collective-permute-start(f32[2,128,128]{2,1,0:T(8,128)S(1)} %get-tuple-element.109), channel_id=1, source_target_pairs={{0,8},{4,12},{8,0},{12,4},{16,24},{20,28},{24,16},{28,20},{1,9},{5... | collective-permute-start | bytes 393224 | tf_op jit(solution)/shard_map/ppermute | solution.py:584
  54.5 0.0 collective-permute-start.10
  54.5 2.2 %query.5 = (f32[1,2,512,128]{3,2,1,0:T(8,128)S(1)}, bf16[1,2,512,128]{3,2,1,0:T(8,128)(2,1)S(1)}, bf16[1,2,512,128]{3,2,1,0:T(8,128)(2,1)S(1)}) custom-call(bf16[512,512]{1,0:T(8,128)(2,1)} %q_ref.7, bf16[16,2048]{1,0:T(8,128)(2,1)S(1)} %collective-permute-done.3.refs_9_.before_ref, bf16[4,512]{1,0:T(4,128)(2,1)} %qt_ref.5, ...), custom_call_target="tpu_custom_call" | custom-call | flops 2000000000 | bytes 2000000 | tf_op jit(solution)/shard_map/query/pallas_call | solution.py:529
  56.7 0.0 collective-permute-done.8.refs_10_
  56.7 2.2 %collective-permute-done.9.refs_11_ = f32[2,128,128]{2,1,0:T(8,128)S(1)} collective-permute-done((f32[2,128,128]{2,1,0:T(8,128)S(1)}, f32[2,128,128]{2,1,0:T(8,128)S(1)}, u32[]{:S(2)}, u32[]{:S(2)}) %collective-permute-start.9) | collective-permute-done | bytes 131104 | tf_op jit(solution)/shard_map/ppermute | solution.py:584
  58.9 1.5 %collective-permute-done.10.refs_12_ = f32[2,128,128]{2,1,0:T(8,128)S(1)} collective-permute-done((f32[2,128,128]{2,1,0:T(8,128)S(1)}, f32[2,128,128]{2,1,0:T(8,128)S(1)}, u32[]{:S(2)}, u32[]{:S(2)}) %collective-permute-start.10) | collective-permute-done | bytes 131104 | tf_op jit(solution)/shard_map/ppermute | solution.py:584
  60.4 2.3 %outputs.1 = f32[512,1024]{1,0:T(8,128)} custom-call(f32[2,2,512,128]{3,2,1,0:T(8,128)S(1)} %get-tuple-element.92.refs_0_, bf16[2,2,512,128]{3,2,1,0:T(8,128)(2,1)S(1)} %get-tuple-element.93.refs_1_, bf16[2,2,512,128]{3,2,1,0:T(8,128)(2,1)S(1)} %get-tuple-element.94.refs_2_, f32[1,2,512,128]{3,2,1,0:T(8,128)S(1)} %get-tuple-element.95.refs_3_, ...), custom_call_target="tpu_custom_call" | custom-call | tf_op jit(solution)/shard_map/outputs/pallas_call | solution.py:587
  (5 shorter events, 0.0 us)
Async XLA Ops:
  1.4 12.4 %collective-permute-start = (f32[16,512]{1,0:T(8,128)S(1)}, f32[16,512]{1,0:T(8,128)S(1)}, u32[]{:S(2)}, u32[]{:S(2)}) collective-permute-start(f32[16,512]{1,0:T(8,128)S(1)} %get-tuple-element.59), channel_id=1, source_target_pairs={{0,1},{1,0},{2,3},{3,2},{4,5},{5,4},{6,7},{7,6},{8,9},{9,8},{10,11... | collective-permute-start | bytes 98312 | tf_op jit(solution)/shard_map/ppermute | solution.py:455
  1.9 11.9 %collective-permute-start.1 = (f32[16,512]{1,0:T(8,128)S(1)}, f32[16,512]{1,0:T(8,128)S(1)}, u32[]{:S(2)}, u32[]{:S(2)}) collective-permute-start(f32[16,512]{1,0:T(8,128)S(1)} %get-tuple-element.60), channel_id=1, source_target_pairs={{0,2},{1,3},{2,0},{3,1},{4,6},{5,7},{6,4},{7,5},{8,10},{9,11},{10,... | collective-permute-start | bytes 98312 | tf_op jit(solution)/shard_map/ppermute | solution.py:455
  4.5 9.3 %collective-permute-start.2 = (f32[16,512]{1,0:T(8,128)S(1)}, f32[16,512]{1,0:T(8,128)S(1)}, u32[]{:S(2)}, u32[]{:S(2)}) collective-permute-start(f32[16,512]{1,0:T(8,128)S(1)} %get-tuple-element.61), channel_id=1, source_target_pairs={{0,3},{1,2},{2,1},{3,0},{4,7},{5,6},{6,5},{7,4},{8,11},{9,10},{10,... | collective-permute-start | bytes 98312 | tf_op jit(solution)/shard_map/ppermute | solution.py:455
  4.6 9.3 %copy-start = (f32[8]{0:T(128)S(1)}, f32[8]{0:T(128)}, u32[]{:S(2)}) copy-start(f32[8]{0:T(128)} %scale_ref.5) | copy-start | bytes 100
  4.6 9.3 %copy-start.1 = (f32[8]{0:T(128)S(1)}, f32[8]{0:T(128)}, u32[]{:S(2)}) copy-start(f32[8]{0:T(128)} %bias_ref.5) | copy-start | bytes 100
  4.6 9.3 %collective-permute-start.3 = (bf16[16,2048]{1,0:T(8,128)(2,1)S(1)}, bf16[16,2048]{1,0:T(8,128)(2,1)S(1)}, u32[]{:S(2)}, u32[]{:S(2)}) collective-permute-start(bf16[16,2048]{1,0:T(8,128)(2,1)S(1)} %get-tuple-element.65), channel_id=1, source_target_pairs={{0,4},{4,8},{8,12},{12,16},{16,20},{20,24},{24,28},{1,5},{5,9},{9,... | collective-permute-start | bytes 196616 | tf_op jit(solution)/shard_map/ppermute | solution.py:458
  18.6 19.2 %collective-permute-start.5 = (f32[2,128,256]{2,1,0:T(8,128)S(1)}, f32[2,128,256]{2,1,0:T(8,128)S(1)}, u32[]{:S(2)}, u32[]{:S(2)}) collective-permute-start(f32[2,128,256]{2,1,0:T(8,128)S(1)} %get-tuple-element.68), channel_id=1, source_target_pairs={{0,8},{4,12},{8,0},{12,4},{16,24},{20,28},{24,16},{28,20},{1,9},{5... | collective-permute-start | bytes 786440 | tf_op jit(solution)/shard_map/ppermute | solution.py:554
  27.8 13.7 %collective-permute-start.4 = (f32[2,128,256]{2,1,0:T(8,128)S(1)}, f32[2,128,256]{2,1,0:T(8,128)S(1)}, u32[]{:S(2)}, u32[]{:S(2)}) collective-permute-start(f32[2,128,256]{2,1,0:T(8,128)S(1)} %get-tuple-element.67), channel_id=1, source_target_pairs={{0,4},{4,0},{8,12},{12,8},{16,20},{20,16},{24,28},{28,24},{1,5},{5... | collective-permute-start | bytes 786440 | tf_op jit(solution)/shard_map/ppermute | solution.py:554
  29.4 12.1 %collective-permute-start.6 = (f32[2,128,256]{2,1,0:T(8,128)S(1)}, f32[2,128,256]{2,1,0:T(8,128)S(1)}, u32[]{:S(2)}, u32[]{:S(2)}) collective-permute-start(f32[2,128,256]{2,1,0:T(8,128)S(1)} %get-tuple-element.69), channel_id=1, source_target_pairs={{0,12},{4,8},{8,4},{12,0},{16,28},{20,24},{24,20},{28,16},{1,13},{... | collective-permute-start | bytes 786440 | tf_op jit(solution)/shard_map/ppermute | solution.py:554
  42.3 7.0 %collective-permute-start.7 = (f32[2,128,128]{2,1,0:T(8,128)S(1)}, f32[2,128,128]{2,1,0:T(8,128)S(1)}, u32[]{:S(2)}, u32[]{:S(2)}) collective-permute-start(f32[2,128,128]{2,1,0:T(8,128)S(1)} %get-tuple-element.81), channel_id=1, source_target_pairs={{0,16},{4,20},{8,24},{12,28},{1,17},{5,21},{9,25},{13,29},{2,18},{... | collective-permute-start | bytes 393224 | tf_op jit(solution)/shard_map/ppermute | solution.py:577
  50.4 6.3 %collective-permute-start.8 = (f32[2,128,128]{2,1,0:T(8,128)S(1)}, f32[2,128,128]{2,1,0:T(8,128)S(1)}, u32[]{:S(2)}, u32[]{:S(2)}) collective-permute-start(f32[2,128,128]{2,1,0:T(8,128)S(1)} %get-tuple-element.108), channel_id=1, source_target_pairs={{0,4},{4,0},{8,12},{12,8},{16,20},{20,16},{24,28},{28,24},{1,5},{5... | collective-permute-start | bytes 393224 | tf_op jit(solution)/shard_map/ppermute | solution.py:584
  50.7 8.2 %collective-permute-start.9 = (f32[2,128,128]{2,1,0:T(8,128)S(1)}, f32[2,128,128]{2,1,0:T(8,128)S(1)}, u32[]{:S(2)}, u32[]{:S(2)}) collective-permute-start(f32[2,128,128]{2,1,0:T(8,128)S(1)} %get-tuple-element.109), channel_id=1, source_target_pairs={{0,8},{4,12},{8,0},{12,4},{16,24},{20,28},{24,16},{28,20},{1,9},{5... | collective-permute-start | bytes 393224 | tf_op jit(solution)/shard_map/ppermute | solution.py:584
  54.5 5.9 %collective-permute-start.10 = (f32[2,128,128]{2,1,0:T(8,128)S(1)}, f32[2,128,128]{2,1,0:T(8,128)S(1)}, u32[]{:S(2)}, u32[]{:S(2)}) collective-permute-start(f32[2,128,128]{2,1,0:T(8,128)S(1)} %get-tuple-element.110), channel_id=1, source_target_pairs={{0,12},{4,8},{8,4},{12,0},{16,28},{20,24},{24,20},{28,16},{1,13},{... | collective-permute-start | bytes 393224 | tf_op jit(solution)/shard_map/ppermute | solution.py:584

commit v3 on v2

--- a/solution.py
+++ b/solution.py
@@ -3,6 +3,7 @@
 
 import jax
 import jax.numpy as jnp
+import numpy as np
 from jax import lax
 from jax.experimental import pallas as pl
 from jax.experimental.pallas import tpu as pltpu
@@ -70,19 +71,44 @@
 
 def solve_calls(group):
     half = group // 2
-    return [tuple(range(half))] + [(s,) for s in range(half, group)]
+    return [(s,) for s in range(group)]
 
 
 def in_hbm(x):
     return pltpu.with_memory_space_constraint(x, pltpu.HBM)
 
 
+def rows_before(before_ref, columns):
+    rows = before_ref[:, columns].astype(f32)[EDGE - 8 :]
+    return jnp.where(lax.axis_index("seq") > 0, rows, 0.0)
+
+
 def lanes(start, size):
     return pl.ds(pl.multiple_of(start, 128), size)
 
 
-def logits_kernel(head_count, hidden_ref, proj_ref, q_ref, k_ref, v_ref, *refs):
-    outs, tail_ref, held = refs[:head_count], refs[head_count], refs[head_count + 1]
+def logits_kernel(
+    head_count,
+    scale_ref,
+    bias_ref,
+    hidden_ref,
+    proj_ref,
+    q_first,
+    k_first,
+    v_first,
+    q_last,
+    k_last,
+    v_last,
+    q_taps,
+    k_taps,
+    v_taps,
+    kept_ref,
+    given_ref,
+    tail_ref,
+    edge_ref,
+    scales_ref,
+    held,
+):
     rows = proj_ref.shape[0] // head_count
     everything = lax.dot_general(
         proj_ref[...], hidden_ref[...], (NT, ((), ())), preferred_element_type=f32
@@ -90,27 +116,60 @@
     for m in range(head_count):
         held[m] = everything[m * rows : (m + 1) * rows]
     me = lax.axis_index("head")
-    for d in range(head_count):
-        outs[d][...] = held[me ^ d]
-    dk = q_ref.shape[1]
-    tail_ref[:, 0:dk] = q_ref[...]
-    tail_ref[:, dk : 2 * dk] = k_ref[...]
-    tail_ref[:, 2 * dk :] = v_ref[...]
-
-
-def mix_kernel(k_ref, v_ref, kt_ref, vt_ref, unit_ref, dots_ref, mixed_ref, padded):
+    for n in range(head_count // 2):
+        kept_ref[n] = held[me ^ (2 * n)]
+        given_ref[n] = held[me ^ (2 * n + 1)]
+    heads = rows // 2
+    row, column = iotas(heads, heads)
+    scale, bias = (
+        jnp.sum(jnp.where(row == column, ref[...], 0.0), axis=1, keepdims=True)
+        for ref in (scale_ref, bias_ref)
+    )
+    scales_ref[...] = jnp.broadcast_to(scale, scales_ref.shape)
+    for h in range(heads):
+        kept_ref[0, 2 * h : 2 * h + 1, :] = kept_ref[0, 2 * h : 2 * h + 1, :] + bias[h : h + 1]
+    edge_ref[...] = jnp.zeros_like(edge_ref)
+    start = 0
+    for first, last, taps in ((q_first, q_last, q_taps), (k_first, k_last, k_taps), (v_first, v_last, v_taps)):
+        here = slice(start, start + first.shape[1])
+        tail_ref[:, here] = last[...]
+        edge_ref[0:EDGE, here] = first[...].astype(f32)
+        edge_ref[EDGE : EDGE + KCONV, here] = taps[...].astype(f32)
+        start += first.shape[1]
+
+
+def mix_kernel(slots, group, key_width, edge_ref, k_ref, v_ref, unit_ref, dots_ref, mixed_ref, k_held, v_held, padded, sems):
     tokens = k_ref.shape[0]
-    padded[0:8] = jnp.zeros((8, padded.shape[1]), f32)
-    padded[8:, 0:DK] = k_ref[...].astype(f32)
-    padded[8:, DK:] = v_ref[...].astype(f32)
-    key_taps = kt_ref[...].astype(f32)
-    value_taps = vt_ref[...].astype(f32)
-    keys = unit(conv_rows(padded, key_taps, tokens, slice(0, DK)))
-    unit_ref[0] = keys
-    for c in range(tokens // BLOCK):
-        part = split(keys[c * BLOCK : (c + 1) * BLOCK])
-        dots_ref[0, c] = dot_split(part, part, NT)
-    mixed_ref[0] = conv_rows(padded, value_taps, tokens, slice(DK, None))
+    place = lax.axis_index("seq") % group
+    copies = []
+    for at, s in enumerate(slots):
+        p = place ^ slot_partner(group, s)
+        copies.append(
+            (
+                pltpu.make_async_copy(k_ref.at[:, lanes(p * DK, DK)], k_held.at[at], sems.at[at, 0]),
+                pltpu.make_async_copy(
+                    v_ref.at[:, lanes(p * 2 * DV, 2 * DV)], v_held.at[at], sems.at[at, 1]
+                ),
+            )
+        )
+    for both in copies:
+        for copy in both:
+            copy.start()
+    for at, s in enumerate(slots):
+        p = place ^ slot_partner(group, s)
+        key_taps = edge_ref[EDGE : EDGE + KCONV, lanes(key_width + p * DK, DK)]
+        value_taps = edge_ref[EDGE : EDGE + KCONV, lanes(2 * key_width + p * 2 * DV, 2 * DV)]
+        padded[at, 0:8] = jnp.zeros((8, padded.shape[2]), f32)
+        copies[at][0].wait()
+        padded[at, 8:, 0:DK] = k_held[at].astype(f32)
+        copies[at][1].wait()
+        padded[at, 8:, DK:] = v_held[at].astype(f32)
+        keys = unit(conv_rows(padded.at[at], key_taps, tokens, slice(0, DK)))
+        unit_ref[at] = keys
+        for c in range(tokens // BLOCK):
+            part = split(keys[c * BLOCK : (c + 1) * BLOCK])
+            dots_ref[at, c] = dot_split(part, part, NT)
+        mixed_ref[at] = conv_rows(padded.at[at], value_taps, tokens, slice(DK, None))
 
 
 def softplus(u):
@@ -119,7 +178,21 @@
     return jnp.maximum(u, 0.0) + jnp.where(e < 0.03, small, jnp.log(1.0 + e))
 
 
-def invert_all(lowers):
+def dot_wide(a, b):
+    rows, columns = a[0].shape[0], b[0].shape[1]
+    four = jnp.dot(
+        jnp.concatenate(a, axis=0), jnp.concatenate(b, axis=1), preferred_element_type=f32
+    )
+    return four[:rows, :columns] + (four[:rows, columns:] + four[rows:, :columns])
+
+
+def pick_matrix():
+    row, column = np.arange(BLOCK)[:, None], np.arange((SUB - 1) * BLOCK)[None, :]
+    pick = row == (column % BLOCK) // SUB * SUB + column // BLOCK
+    return np.concatenate([pick, pick], axis=0).astype(bf16)
+
+
+def invert_all(lowers, pick):
     count = len(lowers)
     row, column = iotas()
     blocks = (row // SUB) == (column // SUB)
@@ -131,11 +204,6 @@
             total = total + kept[b * SUB : (b + 1) * SUB]
         folded.append(total)
     spread = jnp.concatenate(split(jnp.concatenate(folded, axis=0)), axis=1)
-    pick = [
-        jnp.where(row == (column // SUB) * SUB + j, 1.0, 0.0).astype(bf16) for j in range(SUB - 1)
-    ]
-    pick = jnp.concatenate(pick, axis=1)
-    pick = jnp.concatenate([pick, pick], axis=0)
     wide = jnp.dot(spread, pick, preferred_element_type=f32).reshape(
         count, SUB, (SUB - 1) * BLOCK
     )
@@ -145,41 +213,51 @@
     )
     for j in range(SUB - 1):
         inverse = inverse - wide[:, :, j * BLOCK : (j + 1) * BLOCK] * inverse[:, j : j + 1, :]
-    full = [
-        jnp.where(blocks, jnp.concatenate([inverse[i]] * (BLOCK // SUB), axis=0), 0.0)
-        for i in range(count)
-    ]
+    inverses = [inverse[i] for i in range(count)]
+    halves = [split(x) for x in lowers]
     size = SUB
     while size < BLOCK:
+        same = (row // size) == (column // size)
         across = ((row // (2 * size)) == (column // (2 * size))) & ((row // size) > (column // size))
-        halves = [split(x) for x in full]
-        first = [
-            dot_split(halves[i], split(jnp.where(across, lowers[i], 0.0))) for i in range(count)
+        same, across = (jnp.where(m, 1.0, 0.0).astype(bf16) for m in (same, across))
+        odd = iotas(size, BLOCK)[1] // size % 2 == 1
+        dot = dot_wide if size < 64 else dot_split
+        parts = [split(x) for x in inverses]
+        first = [dot(x, tuple(h * across for h in low)) for x, low in zip(parts, halves)]
+        spread = [
+            tuple(jnp.concatenate([h] * (BLOCK // size), axis=0) * same for h in x) for x in parts
         ]
-        full = [full[i] - dot_split(split(first[i]), halves[i]) for i in range(count)]
+        second = [dot(split(x), y) for x, y in zip(first, spread)]
+        inverses = [
+            jnp.concatenate([jnp.where(odd, 0.0, x), jnp.where(odd, x, -y)], axis=0)
+            for x, y in zip(inverses, second)
+        ]
         size *= 2
-    return full
+    return inverses
+
+
+def followed(later, both):
+    added, move = later
+    both = dot_split(split(move), split(both))
+    return jnp.concatenate([both[:, :DV] + added, both[:, DV:]], axis=1)
 
 
 def solve_kernel(
     slots,
+    start,
     group,
+    key_width,
     pieces,
-    scale_ref,
-    bias_ref,
+    scales_ref,
     *refs,
 ):
     logit_refs, refs = refs[:pieces], refs[pieces:]
-    (unit_ref, dots_ref, mixed_ref, k_ref, v_ref, before_ref, kt_ref, vt_ref), refs = (
-        refs[:8],
-        refs[8:],
-    )
+    (unit_ref, dots_ref, mixed_ref, before_ref, edge_ref, pick_ref), refs = refs[:6], refs[6:]
     count = len(slots)
     message_refs, refs = refs[:count], refs[count:]
     solved_ref, starts_ref, cumulative_ref, first_ref, padded = refs
     tokens = unit_ref.shape[1]
     blocks = tokens // BLOCK
-    key_width = kt_ref.shape[1]
     place = lax.axis_index("seq") % group
     row, column = iotas()
     upper = jnp.where(row <= column, 1.0, 0.0)
@@ -189,24 +267,24 @@
     systems, rights, tails, ends, key_parts = [], [], [], [], []
     for at, s in enumerate(slots):
         p = place ^ slot_partner(group, s)
-        kcol, vcol = p * DK, p * 2 * DV
-        padded[0:8, 0:DK] = before_ref[:, lanes(key_width + kcol, DK)].astype(f32)[EDGE - 8 :]
-        padded[0:8, DK:] = before_ref[:, lanes(2 * key_width + vcol, 2 * DV)].astype(f32)[EDGE - 8 :]
-        padded[8:, 0:DK] = k_ref[:, lanes(kcol, DK)].astype(f32)
-        padded[8:, DK:] = v_ref[:, lanes(vcol, 2 * DV)].astype(f32)
-        key_taps = kt_ref[:, lanes(kcol, DK)].astype(f32)
-        value_taps = vt_ref[:, lanes(vcol, 2 * DV)].astype(f32)
+        kcol, vcol = lanes(key_width + p * DK, DK), lanes(2 * key_width + p * 2 * DV, 2 * DV)
+        padded[0:8, 0:DK] = rows_before(before_ref, kcol)
+        padded[0:8, DK:] = rows_before(before_ref, vcol)
+        padded[8:, 0:DK] = edge_ref[0:EDGE, kcol]
+        padded[8:, DK:] = edge_ref[0:EDGE, vcol]
+        key_taps = edge_ref[EDGE : EDGE + KCONV, kcol]
+        value_taps = edge_ref[EDGE : EDGE + KCONV, vcol]
         edge_keys = unit(conv_rows(padded, key_taps, EDGE, slice(0, DK)))
         edge_values = conv_rows(padded, value_taps, EDGE, slice(DK, None))
         decays, rates = [], []
         for b in range(2):
             h = 2 * p + b
-            u = logit_refs[0][pl.ds(2 * h, 1), :]
-            w = logit_refs[0][pl.ds(2 * h + 1, 1), :]
-            for ref in logit_refs[1:]:
+            u = logit_refs[0][0, pl.ds(2 * h, 1), :] + logit_refs[1][0, pl.ds(2 * h, 1), :]
+            w = logit_refs[0][0, pl.ds(2 * h + 1, 1), :] + logit_refs[1][0, pl.ds(2 * h + 1, 1), :]
+            for ref in logit_refs[2:]:
                 u = u + ref[pl.ds(2 * h, 1), :]
                 w = w + ref[pl.ds(2 * h + 1, 1), :]
-            decays.append(-scale_ref[h] * softplus(u + bias_ref[h]))
+            decays.append(-scales_ref[pl.ds(h, 1), :] * softplus(u))
             rates.append(1.0 / (1.0 + jnp.exp(-w)))
         decay_rows = jnp.concatenate(
             [d[:, c * BLOCK : (c + 1) * BLOCK] for d in decays for c in range(blocks)], axis=0
@@ -225,15 +303,15 @@
         tail_columns = jnp.exp(jnp.transpose(last - sums))
         end_values = jnp.exp(last)
         for c in range(blocks):
-            keys = unit_ref[p, pl.ds(c * BLOCK, BLOCK), :]
-            values = mixed_ref[p, pl.ds(c * BLOCK, BLOCK), :]
+            keys = unit_ref[start + at, pl.ds(c * BLOCK, BLOCK), :]
+            values = mixed_ref[start + at, pl.ds(c * BLOCK, BLOCK), :]
             if c == 0:
                 keys = jnp.concatenate([edge_keys, keys[EDGE:]], axis=0)
                 values = jnp.concatenate([edge_values, values[EDGE:]], axis=0)
                 first_ref[at] = keys
             parts = split(keys)
             key_parts.append(parts)
-            dots = dot_split(parts, parts, NT) if c == 0 else dots_ref[p, c]
+            dots = dot_split(parts, parts, NT) if c == 0 else dots_ref[start + at, c]
             for b in range(2):
                 r = b * blocks + c
                 rate = rate_columns[:, r : r + 1]
@@ -252,7 +330,7 @@
                 tails.append(tail_columns[:, r : r + 1])
                 ends.append(end_values[r : r + 1, :])
 
-    inverses = invert_all(systems)
+    inverses = invert_all(systems, pick_ref[...])
     solved = [dot_split(split(x), split(r)) for x, r in zip(inverses, rights)]
     for at in range(count):
         moves = {}
@@ -269,21 +347,59 @@
                 )
                 moves[b, c] = (added, move)
         for b in range(2):
-            both = jnp.concatenate(moves[b, 0], axis=1)
-            for c in range(1, blocks):
+            half = blocks // 2
+            parts = []
+            for begin in (0, half):
+                both = jnp.concatenate(moves[b, begin], axis=1)
+                for c in range(begin + 1, begin + half):
+                    if begin == 0:
+                        starts_ref[at, b, c - 1] = both
+                    both = followed(moves[b, c], both)
+                parts.append(both)
+            both = parts[0]
+            for c in range(half, blocks):
                 starts_ref[at, b, c - 1] = both
-                added, move = moves[b, c]
-                both = dot_split(split(move), split(both))
-                both = jnp.concatenate([both[:, :DV] + added, both[:, DV:]], axis=1)
+                if c < blocks - 1:
+                    both = followed(moves[b, c], both)
+            both = followed((parts[1][:, :DV], parts[1][:, DV:]), parts[0])
             message_refs[at][b] = both
+
+
+def mix_and_solve_kernel(slots, group, key_width, pieces, *refs):
+    count = len(slots)
+    (scales_ref, *logit_refs), refs = refs[: 1 + pieces], refs[1 + pieces :]
+    (before_ref, edge_ref, pick_ref, k_ref, v_ref), refs = refs[:5], refs[5:]
+    outs, refs = refs[: count + 4], refs[count + 4 :]
+    unit_ref, dots_ref, mixed_ref, k_held, v_held, padded, sems, few = refs
+    mix_kernel(
+        slots, group, key_width, edge_ref, k_ref, v_ref, unit_ref, dots_ref, mixed_ref, k_held, v_held, padded, sems
+    )
+    solve_kernel(
+        slots,
+        0,
+        group,
+        key_width,
+        pieces,
+        scales_ref,
+        *logit_refs,
+        unit_ref,
+        dots_ref,
+        mixed_ref,
+        before_ref,
+        edge_ref,
+        pick_ref,
+        *outs,
+        few,
+    )
 
 
 def query_kernel(
     slots,
+    start,
     group,
     q_ref,
     before_ref,
-    qt_ref,
+    edge_ref,
     unit_ref,
     first_ref,
     cumulative_ref,
@@ -303,16 +419,16 @@
     for at, s in enumerate(slots):
         p = place ^ slot_partner(group, s)
         columns = lanes(p * DK, DK)
-        padded[0:8] = before_ref[:, columns].astype(f32)[EDGE - 8 :]
+        padded[0:8] = rows_before(before_ref, columns)
         padded[8:] = q_ref[:, columns].astype(f32)
-        taps = qt_ref[:, columns].astype(f32)
+        taps = edge_ref[EDGE : EDGE + KCONV, columns]
         queries = unit(conv_rows(padded, taps, tokens, slice(None)), 1.0 / math.sqrt(DK))
         sums = cumulative_ref[at]
         cum_columns = jnp.transpose(sums)
         growth_columns = jnp.exp(cum_columns)
         for c in range(blocks):
             here = queries[c * BLOCK : (c + 1) * BLOCK]
-            keys = first_ref[at] if c == 0 else unit_ref[p, pl.ds(c * BLOCK, BLOCK), :]
+            keys = first_ref[at] if c == 0 else unit_ref[start + at, pl.ds(c * BLOCK, BLOCK), :]
             dots = dot_split(split(here), split(keys), NT)
             for b in range(2):
                 r = b * blocks + c
@@ -432,102 +548,98 @@
         return pl.BlockSpec(block, lambda i: (0,) * len(block))
 
     last_rows = tokens // EDGE - 1
-    *partial, tail = pl.pallas_call(
+    width = 2 * key_width + value_width
+    inputs = (query_in, key_in, value_in)
+    taps = (conv_query, conv_key, convolution_value_taps)
+    kept, given, tail, edge, scales = pl.pallas_call(
         functools.partial(logits_kernel, head_count),
         grid=(1,),
-        in_specs=[
-            full(hidden_states.shape),
-            full(proj_ba.shape[::-1]),
-            pl.BlockSpec((EDGE, key_width), lambda i: (last_rows, 0)),
-            pl.BlockSpec((EDGE, key_width), lambda i: (last_rows, 0)),
-            pl.BlockSpec((EDGE, value_width), lambda i: (last_rows, 0)),
-        ],
-        out_specs=[full((2 * heads, tokens))] * head_count
-        + [full((EDGE, 2 * key_width + value_width))],
-        out_shape=[shape(2 * heads, tokens)] * head_count
-        + [shape(EDGE, 2 * key_width + value_width, dtype=bf16)],
+        in_specs=[full((1, heads))] * 2 + [full(hidden_states.shape), full(proj_ba.shape[::-1])]
+        + [pl.BlockSpec((EDGE, x.shape[1]), lambda i: (0, 0)) for x in inputs]
+        + [pl.BlockSpec((EDGE, x.shape[1]), lambda i: (last_rows, 0)) for x in inputs]
+        + [full(x.shape) for x in taps],
+        out_specs=[whole()] * 5,
+        out_shape=[shape(head_count // 2, 2 * heads, tokens)] * 2
+        + [shape(EDGE, width, dtype=bf16), shape(EDGE + 8, width), shape(heads, tokens)],
         scratch_shapes=[VMEM((head_count, 2 * heads, tokens), f32)],
         compiler_params=params(),
         name="logits",
-    )(in_hbm(hidden_states), in_hbm(proj_ba.T), in_hbm(query_in), in_hbm(key_in), in_hbm(value_in))
-
-    logits = [partial[0]] + [
-        lax.ppermute(partial[d], "head", [(i, i ^ d) for i in range(head_count)])
-        for d in range(1, head_count)
+    )(
+        *[in_hbm(x.reshape(1, heads)) for x in (decay_scale, dt_bias)],
+        *[in_hbm(x) for x in (hidden_states, proj_ba.T, *inputs, *inputs, *taps)],
+    )
+
+    taken = lax.ppermute(given, "head", [(i, i ^ 1) for i in range(head_count)])
+    logits = [kept, taken] + [
+        lax.ppermute(kept[n] + taken[n], "head", [(i, i ^ (2 * n)) for i in range(head_count)])
+        for n in range(1, head_count // 2)
     ]
-    before = lax.ppermute(tail, "seq", [(i, i + 1) for i in range(seq - 1)])
-
-    unit_keys, key_dots, mixed = pl.pallas_call(
-        mix_kernel,
-        grid=(pairs,),
-        in_specs=[
-            pl.BlockSpec((tokens, DK), lambda i: (0, i)),
-            pl.BlockSpec((tokens, 2 * DV), lambda i: (0, i)),
-            pl.BlockSpec((KCONV, DK), lambda i: (0, i)),
-            pl.BlockSpec((KCONV, 2 * DV), lambda i: (0, i)),
-        ],
-        out_specs=[
-            pl.BlockSpec((1, tokens, DK), lambda i: (i, 0, 0)),
-            pl.BlockSpec((1, blocks, BLOCK, BLOCK), lambda i: (i, 0, 0, 0)),
-            pl.BlockSpec((1, tokens, 2 * DV), lambda i: (i, 0, 0)),
-        ],
-        out_shape=[
-            shape(pairs, tokens, DK),
-            shape(pairs, blocks, BLOCK, BLOCK),
-            shape(pairs, tokens, 2 * DV),
-        ],
-        scratch_shapes=[VMEM((tokens + 8, DK + 2 * DV), f32)],
-        compiler_params=params(),
-        cost_estimate=pl.CostEstimate(
-            flops=4_000_000_000, bytes_accessed=6_000_000, transcendentals=0
-        ),
-        name="mix",
-    )(in_hbm(key_in), in_hbm(value_in), in_hbm(conv_key), in_hbm(convolution_value_taps))
-
-    def solve(slots):
+    before = lax.ppermute(tail, "seq", [(i, (i + 1) % seq) for i in range(seq)])
+
+    pick = jnp.asarray(pick_matrix())
+
+    def mix_shapes(count):
+        return [(count, tokens, DK), (count, blocks, BLOCK, BLOCK), (count, tokens, 2 * DV)]
+
+    def mix_scratch(count):
+        return [
+            VMEM((count, tokens, DK), bf16),
+            VMEM((count, tokens, 2 * DV), bf16),
+            VMEM((count, tokens + 8, DK + 2 * DV), f32),
+            pltpu.SemaphoreType.DMA((count, 2)),
+        ]
+
+    def solve_shapes(count):
+        return [shape(2, DK, 2 * DK)] * count + [
+            shape(count, 2, tokens, 2 * DK),
+            shape(count, 2, blocks - 1, DK, 2 * DK),
+            shape(count, 2 * blocks, BLOCK),
+            shape(count, BLOCK, DK),
+        ]
+
+    def mix(slots):
         count = len(slots)
         return pl.pallas_call(
-            functools.partial(solve_kernel, slots, group, head_count),
-            grid=(1,),
-            in_specs=[whole(pltpu.SMEM)] * 2
-            + [whole()] * (head_count + 3)
-            + [
-                pl.BlockSpec((EDGE, key_width), lambda i: (0, 0)),
-                pl.BlockSpec((EDGE, value_width), lambda i: (0, 0)),
-            ]
-            + [whole()] * 3,
+            functools.partial(mix_kernel, slots, group, key_width),
+            in_specs=[whole(), whole(pl.ANY), whole(pl.ANY)],
+            out_specs=[whole()] * 3,
+            out_shape=[shape(*dims) for dims in mix_shapes(count)],
+            scratch_shapes=mix_scratch(count),
+            compiler_params=params(),
+            name="mix",
+        )(edge, in_hbm(key_in), in_hbm(value_in))
+
+    def solve(slots, start, logits, unit_keys, key_dots, mixed):
+        count = len(slots)
+        return pl.pallas_call(
+            functools.partial(solve_kernel, slots, start, group, key_width, len(logits)),
+            in_specs=[whole()] * (len(logits) + 7),
             out_specs=[whole()] * (count + 4),
-            out_shape=[shape(2, DK, 2 * DK)] * count
-            + [
-                shape(count, 2, tokens, 2 * DK),
-                shape(count, 2, blocks - 1, DK, 2 * DK),
-                shape(count, 2 * blocks, BLOCK),
-                shape(count, BLOCK, DK),
-            ],
+            out_shape=solve_shapes(count),
             scratch_shapes=[VMEM((EDGE + 8, DK + 2 * DV), f32)],
             compiler_params=params(),
-            cost_estimate=pl.CostEstimate(
-                flops=4_000_000_000 * count, bytes_accessed=2_000_000 * count, transcendentals=0
-            ),
             name="solve",
-        )(
-            decay_scale,
-            dt_bias,
-            *logits,
-            unit_keys,
-            key_dots,
-            mixed,
-            in_hbm(key_in),
-            in_hbm(value_in),
-            before,
-            in_hbm(conv_key),
-            in_hbm(convolution_value_taps),
-        )
-
-    def query(slots, solved, starts, cumulative, first_keys):
+        )(scales, *logits, unit_keys, key_dots, mixed, before, edge, pick)
+
+    def mix_and_solve(slots, logits):
+        count = len(slots)
+        unit_shape, *others = mix_shapes(count)
+        return pl.pallas_call(
+            functools.partial(mix_and_solve_kernel, slots, group, key_width, len(logits)),
+            in_specs=[whole()] * (len(logits) + 4) + [whole(pl.ANY)] * 2,
+            out_specs=[whole()] * (count + 5),
+            out_shape=solve_shapes(count) + [shape(*unit_shape)],
+            scratch_shapes=[VMEM(dims, f32) for dims in others]
+            + mix_scratch(count)
+            + [VMEM((EDGE + 8, DK + 2 * DV), f32)],
+            compiler_params=params(),
+            name="mix_and_solve",
+        )(scales, *logits, before, edge, pick, in_hbm(key_in), in_hbm(value_in))
+
+    def query(slots, start, unit_keys, solved, starts, cumulative, first_keys):
         count = len(slots)
         return pl.pallas_call(
-            functools.partial(query_kernel, slots, group),
+            functools.partial(query_kernel, slots, start, group),
             in_specs=[whole()] * 8,
             out_specs=[whole()] * 3,
             out_shape=[shape(count, 2, tokens, DV)]
@@ -538,14 +650,22 @@
                 flops=2_000_000_000 * count, bytes_accessed=2_000_000 * count, transcendentals=0
             ),
             name="query",
-        )(in_hbm(query_in), before, in_hbm(conv_query), unit_keys, first_keys, cumulative, solved, starts)
+        )(query_in, before, edge, unit_keys, first_keys, cumulative, solved, starts)
 
     calls = solve_calls(group)
     messages, rest = [], []
-    for slots in calls:
-        results = solve(slots)
+    early = sum(calls[:-1], ())
+    early_mixed = mix(early)
+    start = 0
+    for slots in calls[:-1]:
+        results = solve(slots, start, logits, *early_mixed)
+        results, logits = lax.optimization_barrier((results, logits))
         messages += results[: len(slots)]
-        rest.append(results[len(slots) :])
+        rest.append([start, early_mixed[0], *results[len(slots) :]])
+        start += len(slots)
+    *results, unit_keys = mix_and_solve(calls[-1], logits)
+    messages += results[:1]
+    rest.append([0, unit_keys, *results[1:]])
 
     arrived = [None] * group
     for s in range(group):
@@ -554,8 +674,7 @@
             lax.ppermute(messages[s], "seq", [(i, i ^ d) for i in range(seq)]) if d else messages[s]
         )
 
-    reads = [query(calls[0], *rest[0])]
-    arrived, reads[0] = lax.optimization_barrier((arrived, reads[0]))
+    reads = []
     chain, leaving = pl.pallas_call(
         functools.partial(prefix_kernel, group),
         in_specs=[whole(pl.ANY)] * group,
@@ -565,6 +684,8 @@
         compiler_params=params(),
         name="prefix",
     )(*arrived)
+    leaving, rest = lax.optimization_barrier((leaving, [x[1:] for x in rest]))
+    starts = [sum(len(c) for c in calls[:k]) for k in range(len(calls) - 1)] + [0]
     enter = pl.pallas_call(
         functools.partial(enter_kernel, group),
         in_specs=[whole()] * 2,
@@ -576,14 +697,14 @@
     for hop in range(seq // group - 1):
         received = lax.ppermute(leaving, "seq", [(i, i + group) for i in range(seq - group)])
         if hop == 0:
-            reads += [query(slots, *outs) for slots, outs in zip(calls[1:-1], rest[1:-1])]
+            reads += [query(*x, *outs) for *x, outs in zip(calls[:-1], starts, rest)]
             received, reads = lax.optimization_barrier((received, reads))
         *entering, leaving = enter(received, chain)
 
     states = [entering[0]] + [
         lax.ppermute(entering[d], "seq", [(i, i ^ d) for i in range(seq)]) for d in range(1, group)
     ]
-    reads.append(query(calls[-1], *rest[-1]))
+    reads.append(query(calls[-1], starts[-1], *rest[-1]))
     return pl.pallas_call(
         functools.partial(output_kernel, group, calls),
         in_specs=[whole()] * (3 * len(calls) + group),

time: 63.1 us -> 51.8 us (0.82)
  Pallas kernels: 35.5 us -> 29.3 us
  starting transfers between devices: 19.2 us -> 16.3 us
  waiting for transfers between devices: 7.82 us -> 5.93 us
    pallas_call x7 -> x9, Pallas kernels: 30 us -> 23.6 us  [the longest x3 9.67 us: solve(): pl.pallas_call(functools.partial(solve_kernel, slots, start, group, key_w...]
    ppermute x4 -> x3, starting transfers between devices: 6.9 us -> 4.65 us  [the longest x1 2.55 us: per_device(): before = lax.ppermute(tail, 'seq', [(i, (i + 1) % seq) for i in range(seq)])]
    ppermute x3, waiting for transfers between devices: 3.76 us -> 2 us  [per_device(): lax.ppermute(messages[s], 'seq', [(i, i ^ d) for i in range(seq)])]
    ppermute x3, starting transfers between devices: 4.14 us -> 3.49 us  [per_device(): lax.ppermute(entering[d], 'seq', [(i, i ^ d) for i in range(seq)])]
  transfers between devices with their start and end apart: 11 -> 10, of which waited for: 4 -> 4; matrix products, arithmetic and copies ran while one was open for 0% -> 0% of each run, Pallas kernels for 40% -> 40%
where the time goes in v3:
time: 51.8 us; the launch traced here: 51.6 us
  Pallas kernels  29.3 us (57%)
  starting transfers between devices  16.3 us (31%)
  waiting for transfers between devices  5.93 us (11%)
    pallas_call x3, Pallas kernels, solve(): pl.pallas_call(functools.partial(solve_kernel, slots, start, group, key_w...  9.67 us
    pallas_call x1, Pallas kernels, mix_and_solve(): pl.pallas_call(functools.partial(mix_and_solve_kernel, slots, group, key_...  5.04 us
    pallas_call x4, Pallas kernels, query(): pl.pallas_call(functools.partial(query_kernel, slots, start, group), in_s...  4.59 us
    ppermute x1, starting transfers between devices, per_device(): lax.ppermute(leaving, 'seq', [(i, i + group) for i in range(seq - group)])  4.49 us
    pallas_call x1, Pallas kernels, mix(): pl.pallas_call(functools.partial(mix_kernel, slots, group, key_width), in...  4.34 us
    ppermute x3, waiting for transfers between devices, per_device(): lax.ppermute(entering[d], 'seq', [(i, i ^ d) for i in range(seq)])  3.91 us
    ppermute x3, starting transfers between devices, per_device(): lax.ppermute(messages[s], 'seq', [(i, i ^ d) for i in range(seq)])  3.62 us
    ppermute x3, starting transfers between devices, per_device(): lax.ppermute(entering[d], 'seq', [(i, i ^ d) for i in range(seq)])  3.49 us
  transfers between devices with their start and end apart: 10, of which 4 were waited for; matrix products, arithmetic and copies ran while one was open for 0% of the time, Pallas kernels for 40%

profile of v3, /device:TPU:0, one launch (start us, length us, event | category | flops | bytes accessed | tf_op | source)
XLA Modules:
  0.0 51.6 jit_solution(14401613438051780513)
XLA Ops:
  0.0 1.5 %logits.1 = (f32[2,16,512]{2,1,0:T(8,128)S(1)}, f32[2,16,512]{2,1,0:T(8,128)S(1)}, bf16[16,2048]{1,0:T(8,128)(2,1)S(1)}, f32[24,2048]{1,0:T(8,128)S(1)}, f32[8,512]{1,0:T(8,128)S(1)}) custom-call(f32[1,8]{1,0:T(1,128)} %bitcast.6, f32[1,8]{1,0:T(1,128)} %bitcast.7, bf16[512,512]{1,0:T(8,128)(2,1)} %hidden_ref.1, bf16[64,512]{1,0:T(8,128)(2,1)} %bitcast.5, ...), custom_call_target="tpu_custom_call" | custom-call | tf_op jit(solution)/shard_map/logits/pallas_call | solution.py:554
  1.5 0.0 copy-start
  1.5 0.5 collective-permute-start
  2.0 2.6 %collective-permute-start.2 = (bf16[16,2048]{1,0:T(8,128)(2,1)S(1)}, bf16[16,2048]{1,0:T(8,128)(2,1)S(1)}, u32[]{:S(2)}, u32[]{:S(2)}) collective-permute-start(bf16[16,2048]{1,0:T(8,128)(2,1)S(1)} %get-tuple-element.114), channel_id=1, source_target_pairs={{0,4},{4,8},{8,12},{12,16},{16,20},{20,24},{24,28},{28,0},{1,5},{5... | collective-permute-start | bytes 196616 | tf_op jit(solution)/shard_map/ppermute | solution.py:577
  4.6 0.0 collective-permute-done.refs_1_.refs_2_
  4.6 1.6 %collective-permute-start.1 = (f32[16,512]{1,0:T(8,128)S(1)}, f32[16,512]{1,0:T(8,128)S(1)}, u32[]{:S(2)}, u32[]{:S(2)}) collective-permute-start(f32[16,512]{1,0:T(8,128)S(1)} %fusion), channel_id=1, source_target_pairs={{0,2},{1,3},{2,0},{3,1},{4,6},{5,7},{6,4},{7,5},{8,10},{9,11},{10,... | collective-permute-start | bytes 98312 | tf_op jit(solution)/shard_map/ppermute | solution.py:574
  6.2 4.3 %mix.1 = (f32[3,512,128]{2,1,0:T(8,128)S(1)}, f32[3,4,128,128]{3,2,1,0:T(8,128)S(1)}, f32[3,512,256]{2,1,0:T(8,128)S(1)}) custom-call(f32[24,2048]{1,0:T(8,128)S(1)} %get-tuple-element.110.edge_ref.refs_7_.refs_5_, bf16[512,512]{1,0:T(8,128)(2,1)} %refs_7_.1, bf16[512,1024]{1,0:T(8,128)(2,1)} %refs_8_.4), custom_call_target="tpu_custom_call" | custom-call | tf_op jit(solution)/shard_map/mix/pallas_call | solution.py:602
  10.5 0.0 collective-permute-done.2.refs_6_.refs_4_.before_ref
  10.5 0.0 collective-permute-done.1.refs_2_.refs_3_
  10.6 3.2 %solve.3 = (f32[2,128,256]{2,1,0:T(8,128)S(1)}, f32[1,2,512,256]{3,2,1,0:T(8,128)S(1)}, f32[1,2,3,128,256]{4,3,2,1,0:T(8,128)S(1)}, f32[1,8,128]{2,1,0:T(8,128)S(1)}, f32[1,128,128]{2,1,0:T(8,128)S(1)}) custom-call(f32[8,512]{1,0:T(8,128)S(1)} %get-tuple-element.107.scales_ref.refs_0_, f32[2,16,512]{2,1,0:T(8,128)S(1)} %get-tuple-element.136.refs_0_.refs_1_, ...), custom_call_target="tpu_custom_call" | custom-call | tf_op jit(solution)/shard_map/solve/pallas_call | solution.py:614
  13.8 2.6 %collective-permute-start.5 = (f32[2,128,256]{2,1,0:T(8,128)S(1)}, f32[2,128,256]{2,1,0:T(8,128)S(1)}, u32[]{:S(2)}, u32[]{:S(2)}) collective-permute-start(f32[2,128,256]{2,1,0:T(8,128)S(1)} %get-tuple-element.142), channel_id=1, source_target_pairs={{0,12},{4,8},{8,4},{12,0},{16,28},{20,24},{24,20},{28,16},{1,13},{... | collective-permute-start | bytes 786440 | tf_op jit(solution)/shard_map/ppermute | solution.py:674
  16.4 3.2 %solve.4 = (f32[2,128,256]{2,1,0:T(8,128)S(1)}, f32[1,2,512,256]{3,2,1,0:T(8,128)S(1)}, f32[1,2,3,128,256]{4,3,2,1,0:T(8,128)S(1)}, f32[1,8,128]{2,1,0:T(8,128)S(1)}, f32[1,128,128]{2,1,0:T(8,128)S(1)}) custom-call(f32[8,512]{1,0:T(8,128)S(1)} %get-tuple-element.107.scales_ref.refs_0_, f32[2,16,512]{2,1,0:T(8,128)S(1)} %get-tuple-element.136.refs_0_.refs_1_, ...), custom_call_target="tpu_custom_call" | custom-call | tf_op jit(solution)/shard_map/solve/pallas_call | solution.py:614
  19.6 3.2 %solve.5 = (f32[2,128,256]{2,1,0:T(8,128)S(1)}, f32[1,2,512,256]{3,2,1,0:T(8,128)S(1)}, f32[1,2,3,128,256]{4,3,2,1,0:T(8,128)S(1)}, f32[1,8,128]{2,1,0:T(8,128)S(1)}, f32[1,128,128]{2,1,0:T(8,128)S(1)}) custom-call(f32[8,512]{1,0:T(8,128)S(1)} %get-tuple-element.107.scales_ref.refs_0_, f32[2,16,512]{2,1,0:T(8,128)S(1)} %get-tuple-element.136.refs_0_.refs_1_, ...), custom_call_target="tpu_custom_call" | custom-call | tf_op jit(solution)/shard_map/solve/pallas_call | solution.py:614
  22.9 0.0 copy-start.1
  22.9 0.5 %collective-permute-start.4 = (f32[2,128,256]{2,1,0:T(8,128)S(1)}, f32[2,128,256]{2,1,0:T(8,128)S(1)}, u32[]{:S(2)}, u32[]{:S(2)}) collective-permute-start(f32[2,128,256]{2,1,0:T(8,128)S(1)} %get-tuple-element.141), channel_id=1, source_target_pairs={{0,8},{4,12},{8,0},{12,4},{16,24},{20,28},{24,16},{28,20},{1,9},{5... | collective-permute-start | bytes 786440 | tf_op jit(solution)/shard_map/ppermute | solution.py:674
  23.4 0.5 collective-permute-start.3
  23.9 5.0 %mix_and_solve.1 = (f32[2,128,256]{2,1,0:T(8,128)S(1)}, f32[1,2,512,256]{3,2,1,0:T(8,128)S(1)}, f32[1,2,3,128,256]{4,3,2,1,0:T(8,128)S(1)}, f32[1,8,128]{2,1,0:T...) custom-call(f32[8,512]{1,0:T(8,128)S(1)} %get-tuple-element.107.scales_ref.refs_0_, ...), custom_call_target="tpu_custom_call" | custom-call | tf_op jit(solution)/shard_map/mix_and_solve/pallas_call | solution.py:627
  28.9 1.8 %collective-permute-done.4.refs_2_ = f32[2,128,256]{2,1,0:T(8,128)S(1)} collective-permute-done((f32[2,128,256]{2,1,0:T(8,128)S(1)}, f32[2,128,256]{2,1,0:T(8,128)S(1)}, u32[]{:S(2)}, u32[]{:S(2)}) %collective-permute-start.4) | collective-permute-done | bytes 262176 | tf_op jit(solution)/shard_map/ppermute | solution.py:674
  30.8 0.2 collective-permute-done.3.refs_1_
  30.9 0.8 %prefix.1 = (f32[4,2,128,256]{3,2,1,0:T(8,128)S(1)}, f32[2,128,128]{2,1,0:T(8,128)S(1)}) custom-call(f32[2,128,256]{2,1,0:T(8,128)S(1)} %get-tuple-element.139.refs_0_, f32[2,128,256]{2,1,0:T(8,128)S(1)} %collective-permute-done.3.refs_1_, f32[2,128,256]{2,1,0:T(8,128)S(1)} %collective-permute-done.4.refs_2_, f32[2,128,256]{2,1,0:T(8,128)S(1)} %collective-permute-done.5.refs_3_), custom_call_target="tpu_custom_call" | custom-call | tf_op jit(solution)/shard_map/prefix/pallas_call | solution.py:678
  31.7 4.5 %collective-permute-start.6 = (f32[2,128,128]{2,1,0:T(8,128)S(1)}, f32[2,128,128]{2,1,0:T(8,128)S(1)}, u32[]{:S(2)}, u32[]{:S(2)}) collective-permute-start(f32[2,128,128]{2,1,0:T(8,128)S(1)} %get-tuple-element.161), channel_id=1, source_target_pairs={{0,16},{4,20},{8,24},{12,28},{1,17},{5,21},{9,25},{13,29},{2,18},{... | collective-permute-start | bytes 393224 | tf_op jit(solution)/shard_map/ppermute | solution.py:698
  36.3 1.1 %query.4 = (f32[1,2,512,128]{3,2,1,0:T(8,128)S(1)}, bf16[1,2,512,128]{3,2,1,0:T(8,128)(2,1)S(1)}, bf16[1,2,512,128]{3,2,1,0:T(8,128)(2,1)S(1)}) custom-call(bf16[512,512]{1,0:T(8,128)(2,1)S(1)} %copy-done.1, bf16[16,2048]{1,0:T(8,128)(2,1)S(1)} %collective-permute-done.2.refs_6_.refs_4_.before_ref, ...), custom_call_target="tpu_custom_call" | custom-call | flops 2000000000 | bytes 2000000 | tf_op jit(solution)/shard_map/query/pallas_call | solution.py:641
  37.4 1.1 %query.5 = (f32[1,2,512,128]{3,2,1,0:T(8,128)S(1)}, bf16[1,2,512,128]{3,2,1,0:T(8,128)(2,1)S(1)}, bf16[1,2,512,128]{3,2,1,0:T(8,128)(2,1)S(1)}) custom-call(bf16[512,512]{1,0:T(8,128)(2,1)S(1)} %copy-done.1, bf16[16,2048]{1,0:T(8,128)(2,1)S(1)} %collective-permute-done.2.refs_6_.refs_4_.before_ref, ...), custom_call_target="tpu_custom_call" | custom-call | flops 2000000000 | bytes 2000000 | tf_op jit(solution)/shard_map/query/pallas_call | solution.py:641
  38.6 1.2 %query.6 = (f32[1,2,512,128]{3,2,1,0:T(8,128)S(1)}, bf16[1,2,512,128]{3,2,1,0:T(8,128)(2,1)S(1)}, bf16[1,2,512,128]{3,2,1,0:T(8,128)(2,1)S(1)}) custom-call(bf16[512,512]{1,0:T(8,128)(2,1)S(1)} %copy-done.1, bf16[16,2048]{1,0:T(8,128)(2,1)S(1)} %collective-permute-done.2.refs_6_.refs_4_.before_ref, ...), custom_call_target="tpu_custom_call" | custom-call | flops 2000000000 | bytes 2000000 | tf_op jit(solution)/shard_map/query/pallas_call | solution.py:641
  39.7 1.1 %enter.1 = (f32[2,128,128]{2,1,0:T(8,128)S(1)}, f32[2,128,128]{2,1,0:T(8,128)S(1)}, f32[2,128,128]{2,1,0:T(8,128)S(1)}, f32[2,128,128]{2,1,0:T(8,128)S(1)}, f32[2,128,128]{2,1,0:T(8,128)}) custom-call(f32[2,128,128]{2,1,0:T(8,128)S(1)} %collective-permute-done.6.entering_ref, f32[4,2,128,256]{3,2,1,0:T(8,128)S(1)} %get-tuple-element.204.chain_ref), custom_call_target="tpu_custom_call" | custom-call | tf_op jit(solution)/shard_map/enter/pallas_call | solution.py:702
  40.8 0.5 collective-permute-start.7
  41.3 2.2 %collective-permute-start.8 = (f32[2,128,128]{2,1,0:T(8,128)S(1)}, f32[2,128,128]{2,1,0:T(8,128)S(1)}, u32[]{:S(2)}, u32[]{:S(2)}) collective-permute-start(f32[2,128,128]{2,1,0:T(8,128)S(1)} %get-tuple-element.207), channel_id=1, source_target_pairs={{0,8},{4,12},{8,0},{12,4},{16,24},{20,28},{24,16},{28,20},{1,9},{5... | collective-permute-start | bytes 393224 | tf_op jit(solution)/shard_map/ppermute | solution.py:705
  43.5 0.8 %collective-permute-start.9 = (f32[2,128,128]{2,1,0:T(8,128)S(1)}, f32[2,128,128]{2,1,0:T(8,128)S(1)}, u32[]{:S(2)}, u32[]{:S(2)}) collective-permute-start(f32[2,128,128]{2,1,0:T(8,128)S(1)} %get-tuple-element.208), channel_id=1, source_target_pairs={{0,12},{4,8},{8,4},{12,0},{16,28},{20,24},{24,20},{28,16},{1,13},{... | collective-permute-start | bytes 393224 | tf_op jit(solution)/shard_map/ppermute | solution.py:705
  44.3 1.1 %query.7 = (f32[1,2,512,128]{3,2,1,0:T(8,128)S(1)}, bf16[1,2,512,128]{3,2,1,0:T(8,128)(2,1)S(1)}, bf16[1,2,512,128]{3,2,1,0:T(8,128)(2,1)S(1)}) custom-call(bf16[512,512]{1,0:T(8,128)(2,1)S(1)} %copy-done.1, bf16[16,2048]{1,0:T(8,128)(2,1)S(1)} %collective-permute-done.2.refs_6_.refs_4_.before_ref, ...), custom_call_target="tpu_custom_call" | custom-call | flops 2000000000 | bytes 2000000 | tf_op jit(solution)/shard_map/query/pallas_call | solution.py:641
  45.4 1.6 %collective-permute-done.7.refs_13_ = f32[2,128,128]{2,1,0:T(8,128)S(1)} collective-permute-done((f32[2,128,128]{2,1,0:T(8,128)S(1)}, f32[2,128,128]{2,1,0:T(8,128)S(1)}, u32[]{:S(2)}, u32[]{:S(2)}) %collective-permute-start.7) | collective-permute-done | bytes 131104 | tf_op jit(solution)/shard_map/ppermute | solution.py:705
  47.0 2.3 %collective-permute-done.9.refs_15_ = f32[2,128,128]{2,1,0:T(8,128)S(1)} collective-permute-done((f32[2,128,128]{2,1,0:T(8,128)S(1)}, f32[2,128,128]{2,1,0:T(8,128)S(1)}, u32[]{:S(2)}, u32[]{:S(2)}) %collective-permute-start.9) | collective-permute-done | bytes 131104 | tf_op jit(solution)/shard_map/ppermute | solution.py:705
  49.3 2.3 %outputs.1 = f32[512,1024]{1,0:T(8,128)} custom-call(f32[1,2,512,128]{3,2,1,0:T(8,128)S(1)} %get-tuple-element.186.refs_0_, bf16[1,2,512,128]{3,2,1,0:T(8,128)(2,1)S(1)} %get-tuple-element.187.refs_1_, bf16[1,2,512,128]{3,2,1,0:T(8,128)(2,1)S(1)} %get-tuple-element.188.refs_2_, f32[1,2,512,128]{3,2,1,0:T(8,128)S(1)} %get-tuple-element.189.refs_3_, ...), custom_call_target="tpu_custom_call" | custom-call | tf_op jit(solution)/shard_map/outputs/pallas_call | solution.py:708
  (6 shorter events, 0.0 us)
Async XLA Ops:
  1.5 9.1 %copy-start = (bf16[256,1920]{1,0:T(8,128)(2,1)S(1)}, bf16[256,1920]{1,0:T(8,128)(2,1)}, u32[]{:S(2)}) copy-start(bf16[256,1920]{1,0:T(8,128)(2,1)} %constant.2.clone.refs_8_.refs_6_) | copy-start | bytes 2949124
  1.5 3.1 %collective-permute-start = (f32[2,16,512]{2,1,0:T(8,128)S(1)}, f32[2,16,512]{2,1,0:T(8,128)S(1)}, u32[]{:S(2)}, u32[]{:S(2)}) collective-permute-start(f32[2,16,512]{2,1,0:T(8,128)S(1)} %get-tuple-element.109), channel_id=1, source_target_pairs={{0,1},{1,0},{2,3},{3,2},{4,5},{5,4},{6,7},{7,6},{8,9},{9,8},{10,11... | collective-permute-start | bytes 196616 | tf_op jit(solution)/shard_map/ppermute | solution.py:572
  2.0 8.5 %collective-permute-start.2 = (bf16[16,2048]{1,0:T(8,128)(2,1)S(1)}, bf16[16,2048]{1,0:T(8,128)(2,1)S(1)}, u32[]{:S(2)}, u32[]{:S(2)}) collective-permute-start(bf16[16,2048]{1,0:T(8,128)(2,1)S(1)} %get-tuple-element.114), channel_id=1, source_target_pairs={{0,4},{4,8},{8,12},{12,16},{16,20},{20,24},{24,28},{28,0},{1,5},{5... | collective-permute-start | bytes 196616 | tf_op jit(solution)/shard_map/ppermute | solution.py:577
  4.6 5.9 %collective-permute-start.1 = (f32[16,512]{1,0:T(8,128)S(1)}, f32[16,512]{1,0:T(8,128)S(1)}, u32[]{:S(2)}, u32[]{:S(2)}) collective-permute-start(f32[16,512]{1,0:T(8,128)S(1)} %fusion), channel_id=1, source_target_pairs={{0,2},{1,3},{2,0},{3,1},{4,6},{5,7},{6,4},{7,5},{8,10},{9,11},{10,... | collective-permute-start | bytes 98312 | tf_op jit(solution)/shard_map/ppermute | solution.py:574
  13.8 15.1 %collective-permute-start.5 = (f32[2,128,256]{2,1,0:T(8,128)S(1)}, f32[2,128,256]{2,1,0:T(8,128)S(1)}, u32[]{:S(2)}, u32[]{:S(2)}) collective-permute-start(f32[2,128,256]{2,1,0:T(8,128)S(1)} %get-tuple-element.142), channel_id=1, source_target_pairs={{0,12},{4,8},{8,4},{12,0},{16,28},{20,24},{24,20},{28,16},{1,13},{... | collective-permute-start | bytes 786440 | tf_op jit(solution)/shard_map/ppermute | solution.py:674
  22.9 13.4 %copy-start.1 = (bf16[512,512]{1,0:T(8,128)(2,1)S(1)}, bf16[512,512]{1,0:T(8,128)(2,1)}, u32[]{:S(2)}) copy-start(bf16[512,512]{1,0:T(8,128)(2,1)} %q_ref.7) | copy-start | bytes 1572868
  22.9 7.9 %collective-permute-start.4 = (f32[2,128,256]{2,1,0:T(8,128)S(1)}, f32[2,128,256]{2,1,0:T(8,128)S(1)}, u32[]{:S(2)}, u32[]{:S(2)}) collective-permute-start(f32[2,128,256]{2,1,0:T(8,128)S(1)} %get-tuple-element.141), channel_id=1, source_target_pairs={{0,8},{4,12},{8,0},{12,4},{16,24},{20,28},{24,16},{28,20},{1,9},{5... | collective-permute-start | bytes 786440 | tf_op jit(solution)/shard_map/ppermute | solution.py:674
  23.4 7.5 %collective-permute-start.3 = (f32[2,128,256]{2,1,0:T(8,128)S(1)}, f32[2,128,256]{2,1,0:T(8,128)S(1)}, u32[]{:S(2)}, u32[]{:S(2)}) collective-permute-start(f32[2,128,256]{2,1,0:T(8,128)S(1)} %get-tuple-element.140), channel_id=1, source_target_pairs={{0,4},{4,0},{8,12},{12,8},{16,20},{20,16},{24,28},{28,24},{1,5},{5... | collective-permute-start | bytes 786440 | tf_op jit(solution)/shard_map/ppermute | solution.py:674
  31.7 8.0 %collective-permute-start.6 = (f32[2,128,128]{2,1,0:T(8,128)S(1)}, f32[2,128,128]{2,1,0:T(8,128)S(1)}, u32[]{:S(2)}, u32[]{:S(2)}) collective-permute-start(f32[2,128,128]{2,1,0:T(8,128)S(1)} %get-tuple-element.161), channel_id=1, source_target_pairs={{0,16},{4,20},{8,24},{12,28},{1,17},{5,21},{9,25},{13,29},{2,18},{... | collective-permute-start | bytes 393224 | tf_op jit(solution)/shard_map/ppermute | solution.py:698
  40.8 6.3 %collective-permute-start.7 = (f32[2,128,128]{2,1,0:T(8,128)S(1)}, f32[2,128,128]{2,1,0:T(8,128)S(1)}, u32[]{:S(2)}, u32[]{:S(2)}) collective-permute-start(f32[2,128,128]{2,1,0:T(8,128)S(1)} %get-tuple-element.206), channel_id=1, source_target_pairs={{0,4},{4,0},{8,12},{12,8},{16,20},{20,16},{24,28},{28,24},{1,5},{5... | collective-permute-start | bytes 393224 | tf_op jit(solution)/shard_map/ppermute | solution.py:705
  41.3 5.8 %collective-permute-start.8 = (f32[2,128,128]{2,1,0:T(8,128)S(1)}, f32[2,128,128]{2,1,0:T(8,128)S(1)}, u32[]{:S(2)}, u32[]{:S(2)}) collective-permute-start(f32[2,128,128]{2,1,0:T(8,128)S(1)} %get-tuple-element.207), channel_id=1, source_target_pairs={{0,8},{4,12},{8,0},{12,4},{16,24},{20,28},{24,16},{28,20},{1,9},{5... | collective-permute-start | bytes 393224 | tf_op jit(solution)/shard_map/ppermute | solution.py:705
  43.5 5.9 %collective-permute-start.9 = (f32[2,128,128]{2,1,0:T(8,128)S(1)}, f32[2,128,128]{2,1,0:T(8,128)S(1)}, u32[]{:S(2)}, u32[]{:S(2)}) collective-permute-start(f32[2,128,128]{2,1,0:T(8,128)S(1)} %get-tuple-element.208), channel_id=1, source_target_pairs={{0,12},{4,8},{8,4},{12,0},{16,28},{20,24},{24,20},{28,16},{1,13},{... | collective-permute-start | bytes 393224 | tf_op jit(solution)/shard_map/ppermute | solution.py:705

commit v4 on v3

--- a/solution.py
+++ b/solution.py
@@ -48,10 +48,10 @@
     return x * (lax.rsqrt(jnp.sum(x * x, axis=-1, keepdims=True) + 1e-6) * factor)
 
 
-def conv_rows(padded_ref, taps, rows, columns):
-    total = taps[0:1] * padded_ref[pl.ds(8 - KCONV + 1, rows), columns]
+def conv_rows(padded_ref, taps, rows):
+    total = taps[0:1] * padded_ref[pl.ds(8 - KCONV + 1, rows), :]
     for j in range(1, KCONV):
-        total = total + taps[j : j + 1] * padded_ref[pl.ds(8 - KCONV + 1 + j, rows), columns]
+        total = total + taps[j : j + 1] * padded_ref[pl.ds(8 - KCONV + 1 + j, rows), :]
     return silu(total)
 
 
@@ -70,8 +70,7 @@
 
 
 def solve_calls(group):
-    half = group // 2
-    return [(s,) for s in range(group)]
+    return [(0,), tuple(range(1, group - 1)), (group - 1,)] if group > 2 else [(0,), (1,)]
 
 
 def in_hbm(x):
@@ -159,17 +158,20 @@
         p = place ^ slot_partner(group, s)
         key_taps = edge_ref[EDGE : EDGE + KCONV, lanes(key_width + p * DK, DK)]
         value_taps = edge_ref[EDGE : EDGE + KCONV, lanes(2 * key_width + p * 2 * DV, 2 * DV)]
-        padded[at, 0:8] = jnp.zeros((8, padded.shape[2]), f32)
+        for n in range(3):
+            padded[at, n, 0:8] = jnp.zeros((8, DK), f32)
         copies[at][0].wait()
-        padded[at, 8:, 0:DK] = k_held[at].astype(f32)
-        copies[at][1].wait()
-        padded[at, 8:, DK:] = v_held[at].astype(f32)
-        keys = unit(conv_rows(padded.at[at], key_taps, tokens, slice(0, DK)))
+        padded[at, 0, 8:] = k_held[at].astype(f32)
+        keys = unit(conv_rows(padded.at[at, 0], key_taps, tokens))
         unit_ref[at] = keys
         for c in range(tokens // BLOCK):
             part = split(keys[c * BLOCK : (c + 1) * BLOCK])
             dots_ref[at, c] = dot_split(part, part, NT)
-        mixed_ref[at] = conv_rows(padded.at[at], value_taps, tokens, slice(DK, None))
+        copies[at][1].wait()
+        for b in range(2):
+            here = slice(b * DV, (b + 1) * DV)
+            padded[at, 1 + b, 8:] = v_held[at, :, here].astype(f32)
+            mixed_ref[at, :, here] = conv_rows(padded.at[at, 1 + b], value_taps[:, here], tokens)
 
 
 def softplus(u):
@@ -223,7 +225,12 @@
         odd = iotas(size, BLOCK)[1] // size % 2 == 1
         dot = dot_wide if size < 64 else dot_split
         parts = [split(x) for x in inverses]
-        first = [dot(x, tuple(h * across for h in low)) for x, low in zip(parts, halves)]
+        if 2 * size < BLOCK:
+            first = [dot(x, tuple(h * across for h in low)) for x, low in zip(parts, halves)]
+        else:
+            first = [
+                dot(split(jnp.where(odd, x, 0.0)), low) for x, low in zip(inverses, halves)
+            ]
         spread = [
             tuple(jnp.concatenate([h] * (BLOCK // size), axis=0) * same for h in x) for x in parts
         ]
@@ -268,14 +275,19 @@
     for at, s in enumerate(slots):
         p = place ^ slot_partner(group, s)
         kcol, vcol = lanes(key_width + p * DK, DK), lanes(2 * key_width + p * 2 * DV, 2 * DV)
-        padded[0:8, 0:DK] = rows_before(before_ref, kcol)
-        padded[0:8, DK:] = rows_before(before_ref, vcol)
-        padded[8:, 0:DK] = edge_ref[0:EDGE, kcol]
-        padded[8:, DK:] = edge_ref[0:EDGE, vcol]
         key_taps = edge_ref[EDGE : EDGE + KCONV, kcol]
         value_taps = edge_ref[EDGE : EDGE + KCONV, vcol]
-        edge_keys = unit(conv_rows(padded, key_taps, EDGE, slice(0, DK)))
-        edge_values = conv_rows(padded, value_taps, EDGE, slice(DK, None))
+        padded[0, 0:8] = rows_before(before_ref, kcol)
+        padded[0, 8:] = edge_ref[0:EDGE, kcol]
+        edge_keys = unit(conv_rows(padded.at[0], key_taps, EDGE))
+        first_values, edge_values = rows_before(before_ref, vcol), edge_ref[0:EDGE, vcol]
+        edges = []
+        for b in range(2):
+            here = slice(b * DV, (b + 1) * DV)
+            padded[1 + b, 0:8] = first_values[:, here]
+            padded[1 + b, 8:] = edge_values[:, here]
+            edges.append(conv_rows(padded.at[1 + b], value_taps[:, here], EDGE))
+        edge_values = jnp.concatenate(edges, axis=1)
         decays, rates = [], []
         for b in range(2):
             h = 2 * p + b
@@ -365,34 +377,6 @@
             message_refs[at][b] = both
 
 
-def mix_and_solve_kernel(slots, group, key_width, pieces, *refs):
-    count = len(slots)
-    (scales_ref, *logit_refs), refs = refs[: 1 + pieces], refs[1 + pieces :]
-    (before_ref, edge_ref, pick_ref, k_ref, v_ref), refs = refs[:5], refs[5:]
-    outs, refs = refs[: count + 4], refs[count + 4 :]
-    unit_ref, dots_ref, mixed_ref, k_held, v_held, padded, sems, few = refs
-    mix_kernel(
-        slots, group, key_width, edge_ref, k_ref, v_ref, unit_ref, dots_ref, mixed_ref, k_held, v_held, padded, sems
-    )
-    solve_kernel(
-        slots,
-        0,
-        group,
-        key_width,
-        pieces,
-        scales_ref,
-        *logit_refs,
-        unit_ref,
-        dots_ref,
-        mixed_ref,
-        before_ref,
-        edge_ref,
-        pick_ref,
-        *outs,
-        few,
-    )
-
-
 def query_kernel(
     slots,
     start,
@@ -422,7 +406,7 @@
         padded[0:8] = rows_before(before_ref, columns)
         padded[8:] = q_ref[:, columns].astype(f32)
         taps = edge_ref[EDGE : EDGE + KCONV, columns]
-        queries = unit(conv_rows(padded, taps, tokens, slice(None)), 1.0 / math.sqrt(DK))
+        queries = unit(conv_rows(padded, taps, tokens), 1.0 / math.sqrt(DK))
         sums = cumulative_ref[at]
         cum_columns = jnp.transpose(sums)
         growth_columns = jnp.exp(cum_columns)
@@ -478,18 +462,20 @@
         leaving_ref[b] = chain[b][:, :DV]
 
 
-def enter_kernel(group, entering_ref, chain_ref, *refs):
-    *outs, leaving_ref = refs
+def enter_kernel(group, onward, entering_ref, chain_ref, *refs):
+    outs = refs[:group]
     place = lax.axis_index("seq") % group
     heads = entering_ref.shape[0]
-    states = [[entering_ref[b] for b in range(heads)]] + [[] for i in range(group)]
+    count = group if onward else group - 1
+    states = [[entering_ref[b] for b in range(heads)]] + [[] for i in range(count)]
     for b in range(heads):
-        moves = jnp.concatenate([chain_ref[i, b, :, DV:] for i in range(group)], axis=0)
+        moves = jnp.concatenate([chain_ref[i, b, :, DV:] for i in range(count)], axis=0)
         moved = dot_split(split(moves), split(states[0][b]))
-        for i in range(group):
+        for i in range(count):
             states[i + 1].append(chain_ref[i, b, :, 0:DV] + moved[i * DK : (i + 1) * DK])
-    for b in range(heads):
-        leaving_ref[b] = states[group][b]
+    if onward:
+        for b in range(heads):
+            refs[group][b] = states[group][b]
     for j in range(group):
 
         @pl.when(place == j)
@@ -499,17 +485,23 @@
                     outs[j ^ i][b] = states[i][b]
 
 
-def output_kernel(group, calls, *refs):
-    reads, entering, (out_ref,) = refs[: 3 * len(calls)], refs[3 * len(calls) : -1], refs[-1:]
+def output_kernel(group, slots, *refs):
+    reads, refs = refs[: 3 * len(slots)], refs[3 * len(slots) :]
+    entering, (out_ref, held, sems) = refs[: len(slots)], refs[-3:]
     place = lax.axis_index("seq") % group
-    for k, slots in enumerate(calls):
-        own_ref, high_ref, low_ref = reads[3 * k : 3 * k + 3]
-        for at, s in enumerate(slots):
-            d = slot_partner(group, s)
-            p = place ^ d
-            for b in range(2):
-                product = dot_split((high_ref[at, b], low_ref[at, b]), split(entering[d][b]))
-                out_ref[:, lanes(p * 2 * DV + b * DV, DV)] = own_ref[at, b] + product
+    copies = []
+    for n, (s, at) in enumerate(slots):
+        own_ref, high_ref, low_ref = reads[3 * n : 3 * n + 3]
+        p = place ^ slot_partner(group, s)
+        for b in range(2):
+            product = dot_split((high_ref[at, b], low_ref[at, b]), split(entering[n][b]))
+            held[n, :, b * DV : (b + 1) * DV] = own_ref[at, b] + product
+        copies.append(
+            pltpu.make_async_copy(held.at[n], out_ref.at[:, lanes(p * 2 * DV, 2 * DV)], sems.at[n])
+        )
+        copies[-1].start()
+    for copy in copies:
+        copy.wait()
 
 
 def shape(*dims, dtype=f32):
@@ -585,7 +577,7 @@
         return [
             VMEM((count, tokens, DK), bf16),
             VMEM((count, tokens, 2 * DV), bf16),
-            VMEM((count, tokens + 8, DK + 2 * DV), f32),
+            VMEM((count, 3, tokens + 8, DK), f32),
             pltpu.SemaphoreType.DMA((count, 2)),
         ]
 
@@ -616,25 +608,10 @@
             in_specs=[whole()] * (len(logits) + 7),
             out_specs=[whole()] * (count + 4),
             out_shape=solve_shapes(count),
-            scratch_shapes=[VMEM((EDGE + 8, DK + 2 * DV), f32)],
+            scratch_shapes=[VMEM((3, EDGE + 8, DK), f32)],
             compiler_params=params(),
             name="solve",
         )(scales, *logits, unit_keys, key_dots, mixed, before, edge, pick)
-
-    def mix_and_solve(slots, logits):
-        count = len(slots)
-        unit_shape, *others = mix_shapes(count)
-        return pl.pallas_call(
-            functools.partial(mix_and_solve_kernel, slots, group, key_width, len(logits)),
-            in_specs=[whole()] * (len(logits) + 4) + [whole(pl.ANY)] * 2,
-            out_specs=[whole()] * (count + 5),
-            out_shape=solve_shapes(count) + [shape(*unit_shape)],
-            scratch_shapes=[VMEM(dims, f32) for dims in others]
-            + mix_scratch(count)
-            + [VMEM((EDGE + 8, DK + 2 * DV), f32)],
-            compiler_params=params(),
-            name="mix_and_solve",
-        )(scales, *logits, before, edge, pick, in_hbm(key_in), in_hbm(value_in))
 
     def query(slots, start, unit_keys, solved, starts, cumulative, first_keys):
         count = len(slots)
@@ -653,19 +630,14 @@
         )(query_in, before, edge, unit_keys, first_keys, cumulative, solved, starts)
 
     calls = solve_calls(group)
-    messages, rest = [], []
-    early = sum(calls[:-1], ())
-    early_mixed = mix(early)
-    start = 0
-    for slots in calls[:-1]:
-        results = solve(slots, start, logits, *early_mixed)
+    mixed = mix(sum(calls, ()))
+    messages, rest, start = [], [], 0
+    for slots in calls:
+        results = solve(slots, start, logits, *mixed)
         results, logits = lax.optimization_barrier((results, logits))
         messages += results[: len(slots)]
-        rest.append([start, early_mixed[0], *results[len(slots) :]])
+        rest.append([mixed[0], *results[len(slots) :]])
         start += len(slots)
-    *results, unit_keys = mix_and_solve(calls[-1], logits)
-    messages += results[:1]
-    rest.append([0, unit_keys, *results[1:]])
 
     arrived = [None] * group
     for s in range(group):
@@ -674,7 +646,9 @@
             lax.ppermute(messages[s], "seq", [(i, i ^ d) for i in range(seq)]) if d else messages[s]
         )
 
-    reads = []
+    messages[-1], rest[0] = lax.optimization_barrier((messages[-1], rest[0]))
+    reads = [query(calls[0], 0, *rest[0])]
+    arrived, reads = lax.optimization_barrier((arrived, reads))
     chain, leaving = pl.pallas_call(
         functools.partial(prefix_kernel, group),
         in_specs=[whole(pl.ANY)] * group,
@@ -684,35 +658,56 @@
         compiler_params=params(),
         name="prefix",
     )(*arrived)
-    leaving, rest = lax.optimization_barrier((leaving, [x[1:] for x in rest]))
-    starts = [sum(len(c) for c in calls[:k]) for k in range(len(calls) - 1)] + [0]
-    enter = pl.pallas_call(
-        functools.partial(enter_kernel, group),
-        in_specs=[whole()] * 2,
-        out_specs=[whole()] * (group + 1),
-        out_shape=[shape(2, DK, DV)] * (group + 1),
-        compiler_params=params(),
-        name="enter",
-    )
-    for hop in range(seq // group - 1):
+    leaving, rest = lax.optimization_barrier((leaving, rest))
+    starts = [sum(len(c) for c in calls[:k]) for k in range(len(calls))]
+    def enter(received, onward):
+        return pl.pallas_call(
+            functools.partial(enter_kernel, group, onward),
+            in_specs=[whole()] * 2,
+            out_specs=[whole()] * (group + onward),
+            out_shape=[shape(2, DK, DV)] * (group + onward),
+            compiler_params=params(),
+            name="enter",
+        )(received, chain)
+
+    hops = seq // group - 1
+    if not hops:
+        entering = enter(jnp.zeros((2, DK, DV), f32), False)
+    for hop in range(hops):
         received = lax.ppermute(leaving, "seq", [(i, i + group) for i in range(seq - group)])
         if hop == 0:
-            reads += [query(*x, *outs) for *x, outs in zip(calls[:-1], starts, rest)]
-            received, reads = lax.optimization_barrier((received, reads))
-        *entering, leaving = enter(received, chain)
-
-    states = [entering[0]] + [
-        lax.ppermute(entering[d], "seq", [(i, i ^ d) for i in range(seq)]) for d in range(1, group)
-    ]
+            reads += [query(*x, *outs) for *x, outs in zip(calls[1:-1], starts[1:-1], rest[1:-1])]
+            received, reads, rest = lax.optimization_barrier((received, reads, rest))
+        entering = enter(received, hop < hops - 1)
+        if hop < hops - 1:
+            *entering, leaving = entering
+
+    states = {0: entering[0]}
+    for d in range(group - 1, 0, -1):
+        states[d] = lax.ppermute(entering[d], "seq", [(i, i ^ d) for i in range(seq)])
     reads.append(query(calls[-1], starts[-1], *rest[-1]))
-    return pl.pallas_call(
-        functools.partial(output_kernel, group, calls),
-        in_specs=[whole()] * (3 * len(calls) + group),
-        out_specs=whole(),
-        out_shape=shape(tokens, value_width),
-        compiler_params=params(),
-        name="outputs",
-    )(*[x for three in reads for x in three], *states)
+    where = {s: (k, at) for k, slots in enumerate(calls) for at, s in enumerate(slots)}
+
+    def outputs(slots, written):
+        operands = [x for s in slots for x in reads[where[s][0]]]
+        operands += [states[slot_partner(group, s)] for s in slots]
+        return pl.pallas_call(
+            functools.partial(output_kernel, group, [(s, where[s][1]) for s in slots]),
+            in_specs=[whole()] * len(operands) + [whole(pl.ANY)] * len(written),
+            out_specs=whole(pl.ANY),
+            out_shape=shape(tokens, value_width),
+            scratch_shapes=[
+                VMEM((len(slots), tokens, 2 * DV), f32),
+                pltpu.SemaphoreType.DMA((len(slots),)),
+            ],
+            input_output_aliases={len(operands): 0} if written else {},
+            compiler_params=params(),
+            name="outputs",
+        )(*operands, *written)
+
+    first = [s for s in range(group) if slot_partner(group, s) < 1]
+    written = outputs(first, [])
+    return outputs([s for s in range(group) if s not in first], [written])
 
 
 def solution(mesh):

time: 51.8 us -> 48.4 us (0.934)
  Pallas kernels: 29.3 us -> 25.9 us
    pallas_call x3, Pallas kernels: 8.39 us -> 3.1 us  [the longest x2 2.76 us: outputs(): pl.pallas_call(functools.partial(output_kernel, group, [(s, where[s][1])...]
    pallas_call x3, Pallas kernels: 9.67 us -> 11.9 us  [solve(): pl.pallas_call(functools.partial(solve_kernel, slots, start, group, key_w...]
    ppermute x3, waiting for transfers between devices: 3.91 us -> 2.59 us  [per_device(): lax.ppermute(entering[d], 'seq', [(i, i ^ d) for i in range(seq)])]
    ppermute x3, waiting for transfers between devices: 2 us -> 2.55 us  [per_device(): lax.ppermute(messages[s], 'seq', [(i, i ^ d) for i in range(seq)])]
    pallas_call x4 -> x3, Pallas kernels: 4.59 us -> 4.43 us  [query(): pl.pallas_call(functools.partial(query_kernel, slots, start, group), in_s...]
  transfers between devices with their start and end apart: 10 -> 10, of which waited for: 4 -> 6; matrix products, arithmetic and copies ran while one was open for 0% -> 0% of each run, Pallas kernels for 40% -> 38%
where the time goes in v4:
time: 48.4 us; the launch traced here: 48.3 us
  Pallas kernels  25.9 us (54%)
  starting transfers between devices  16.5 us (34%)
  waiting for transfers between devices  5.51 us (11%)
    pallas_call x3, Pallas kernels, solve(): pl.pallas_call(functools.partial(solve_kernel, slots, start, group, key_w...  11.9 us
    ppermute x1, starting transfers between devices, per_device(): lax.ppermute(leaving, 'seq', [(i, i + group) for i in range(seq - group)])  4.5 us
    pallas_call x3, Pallas kernels, query(): pl.pallas_call(functools.partial(query_kernel, slots, start, group), in_s...  4.43 us
    pallas_call x1, Pallas kernels, mix(): pl.pallas_call(functools.partial(mix_kernel, slots, group, key_width), in...  4.13 us
    ppermute x3, starting transfers between devices, per_device(): lax.ppermute(entering[d], 'seq', [(i, i ^ d) for i in range(seq)])  3.74 us
    ppermute x3, starting transfers between devices, per_device(): lax.ppermute(messages[s], 'seq', [(i, i ^ d) for i in range(seq)])  3.63 us
    pallas_call x2, Pallas kernels, outputs(): pl.pallas_call(functools.partial(output_kernel, group, [(s, where[s][1])...  2.76 us
    ppermute x3, waiting for transfers between devices, per_device(): lax.ppermute(entering[d], 'seq', [(i, i ^ d) for i in range(seq)])  2.59 us
  transfers between devices with their start and end apart: 10, of which 6 were waited for; matrix products, arithmetic and copies ran while one was open for 0% of the time, Pallas kernels for 38%

profile of v4, /device:TPU:0, one launch (start us, length us, event | category | flops | bytes accessed | tf_op | source)
XLA Modules:
  0.0 48.3 jit_solution(2364264993846959729)
XLA Ops:
  0.0 1.5 %logits.1 = (f32[2,16,512]{2,1,0:T(8,128)S(1)}, f32[2,16,512]{2,1,0:T(8,128)S(1)}, bf16[16,2048]{1,0:T(8,128)(2,1)S(1)}, f32[24,2048]{1,0:T(8,128)S(1)}, f32[8,512]{1,0:T(8,128)S(1)}) custom-call(f32[1,8]{1,0:T(1,128)} %bitcast.6, f32[1,8]{1,0:T(1,128)} %bitcast.7, bf16[512,512]{1,0:T(8,128)(2,1)} %hidden_ref.1, bf16[64,512]{1,0:T(8,128)(2,1)} %bitcast.5, ...), custom_call_target="tpu_custom_call" | custom-call | tf_op jit(solution)/shard_map/logits/pallas_call | solution.py:546
  1.5 0.0 copy-start
  1.5 0.5 %collective-permute-start = (f32[2,16,512]{2,1,0:T(8,128)S(1)}, f32[2,16,512]{2,1,0:T(8,128)S(1)}, u32[]{:S(2)}, u32[]{:S(2)}) collective-permute-start(f32[2,16,512]{2,1,0:T(8,128)S(1)} %get-tuple-element.103), channel_id=1, source_target_pairs={{0,1},{1,0},{2,3},{3,2},{4,5},{5,4},{6,7},{7,6},{8,9},{9,8},{10,11... | collective-permute-start | bytes 196616 | tf_op jit(solution)/shard_map/ppermute | solution.py:564
  2.0 2.6 %collective-permute-start.2 = (bf16[16,2048]{1,0:T(8,128)(2,1)S(1)}, bf16[16,2048]{1,0:T(8,128)(2,1)S(1)}, u32[]{:S(2)}, u32[]{:S(2)}) collective-permute-start(bf16[16,2048]{1,0:T(8,128)(2,1)S(1)} %get-tuple-element.108), channel_id=1, source_target_pairs={{0,4},{4,8},{8,12},{12,16},{16,20},{20,24},{24,28},{28,0},{1,5},{5... | collective-permute-start | bytes 196616 | tf_op jit(solution)/shard_map/ppermute | solution.py:569
  4.6 0.0 collective-permute-done.refs_1_
  4.6 1.6 %collective-permute-start.1 = (f32[16,512]{1,0:T(8,128)S(1)}, f32[16,512]{1,0:T(8,128)S(1)}, u32[]{:S(2)}, u32[]{:S(2)}) collective-permute-start(f32[16,512]{1,0:T(8,128)S(1)} %fusion), channel_id=1, source_target_pairs={{0,2},{1,3},{2,0},{3,1},{4,6},{5,7},{6,4},{7,5},{8,10},{9,11},{10,... | collective-permute-start | bytes 98312 | tf_op jit(solution)/shard_map/ppermute | solution.py:566
  6.2 4.1 %mix.1 = (f32[4,512,128]{2,1,0:T(8,128)S(1)}, f32[4,4,128,128]{3,2,1,0:T(8,128)S(1)}, f32[4,512,256]{2,1,0:T(8,128)S(1)}) custom-call(f32[24,2048]{1,0:T(8,128)S(1)} %get-tuple-element.104.edge_ref.refs_7_, bf16[512,512]{1,0:T(8,128)(2,1)} %k_ref.1, bf16[512,1024]{1,0:T(8,128)(2,1)} %v_ref.1), custom_call_target="tpu_custom_call" | custom-call | tf_op jit(solution)/shard_map/mix/pallas_call | solution.py:594
  10.3 0.0 collective-permute-done.1.refs_2_
  10.3 3.2 %solve.3 = (f32[2,128,256]{2,1,0:T(8,128)S(1)}, f32[1,2,512,256]{3,2,1,0:T(8,128)S(1)}, f32[1,2,3,128,256]{4,3,2,1,0:T(8,128)S(1)}, f32[1,8,128]{2,1,0:T(8,128)S(1)}, f32[1,128,128]{2,1,0:T(8,128)S(1)}) custom-call(f32[8,512]{1,0:T(8,128)S(1)} %get-tuple-element.101.scales_ref, f32[2,16,512]{2,1,0:T(8,128)S(1)} %get-tuple-element.123.refs_0_, ...), custom_call_target="tpu_custom_call" | custom-call | tf_op jit(solution)/shard_map/solve/pallas_call | solution.py:606
  13.5 2.6 %collective-permute-start.5 = (f32[2,128,256]{2,1,0:T(8,128)S(1)}, f32[2,128,256]{2,1,0:T(8,128)S(1)}, u32[]{:S(2)}, u32[]{:S(2)}) collective-permute-start(f32[2,128,256]{2,1,0:T(8,128)S(1)} %get-tuple-element.134), channel_id=1, source_target_pairs={{0,12},{4,8},{8,4},{12,0},{16,28},{20,24},{24,20},{28,16},{1,13},{... | collective-permute-start | bytes 786440 | tf_op jit(solution)/shard_map/ppermute | solution.py:646
  16.2 5.4 %solve.4 = (f32[2,128,256]{2,1,0:T(8,128)S(1)}, f32[2,128,256]{2,1,0:T(8,128)S(1)}, f32[2,2,512,256]{3,2,1,0:T(8,128)S(1)}, f32[2,2,3,128,256]{4,3,2,1,0:T(8,128...) custom-call(f32[8,512]{1,0:T(8,128)S(1)} %get-tuple-element.101.scales_ref, ...), custom_call_target="tpu_custom_call" | custom-call | tf_op jit(solution)/shard_map/solve/pallas_call | solution.py:606
  21.6 0.0 copy-start.1
  21.6 0.5 %collective-permute-start.3 = (f32[2,128,256]{2,1,0:T(8,128)S(1)}, f32[2,128,256]{2,1,0:T(8,128)S(1)}, u32[]{:S(2)}, u32[]{:S(2)}) collective-permute-start(f32[2,128,256]{2,1,0:T(8,128)S(1)} %get-tuple-element.132), channel_id=1, source_target_pairs={{0,4},{4,0},{8,12},{12,8},{16,20},{20,16},{24,28},{28,24},{1,5},{5... | collective-permute-start | bytes 786440 | tf_op jit(solution)/shard_map/ppermute | solution.py:646
  22.1 0.5 collective-permute-start.4
  22.6 3.4 %solve.5 = (f32[2,128,256]{2,1,0:T(8,128)S(1)}, f32[1,2,512,256]{3,2,1,0:T(8,128)S(1)}, f32[1,2,3,128,256]{4,3,2,1,0:T(8,128)S(1)}, f32[1,8,128]{2,1,0:T(8,128)S(1)}, f32[1,128,128]{2,1,0:T(8,128)S(1)}) custom-call(f32[8,512]{1,0:T(8,128)S(1)} %get-tuple-element.101.scales_ref, f32[2,16,512]{2,1,0:T(8,128)S(1)} %get-tuple-element.123.refs_0_, ...), custom_call_target="tpu_custom_call" | custom-call | tf_op jit(solution)/shard_map/solve/pallas_call | solution.py:606
  26.0 1.2 %query.3 = (f32[1,2,512,128]{3,2,1,0:T(8,128)S(1)}, bf16[1,2,512,128]{3,2,1,0:T(8,128)(2,1)S(1)}, bf16[1,2,512,128]{3,2,1,0:T(8,128)(2,1)S(1)}) custom-call(bf16[512,512]{1,0:T(8,128)(2,1)S(1)} %copy-done.1, bf16[16,2048]{1,0:T(8,128)(2,1)S(1)} %collective-permute-done.2.refs_6_.before_ref, f32[24,2048]{1,0:T(8,128)S(1)} %get-tuple-element.104.edge_ref.refs_7_, ...), custom_call_target="tpu_custom_call" | custom-call | flops 2000000000 | bytes 2000000 | tf_op jit(solution)/shard_map/query/pallas_call | solution.py:618
  27.1 2.3 %collective-permute-done.3.refs_1_ = f32[2,128,256]{2,1,0:T(8,128)S(1)} collective-permute-done((f32[2,128,256]{2,1,0:T(8,128)S(1)}, f32[2,128,256]{2,1,0:T(8,128)S(1)}, u32[]{:S(2)}, u32[]{:S(2)}) %collective-permute-start.3) | collective-permute-done | bytes 262176 | tf_op jit(solution)/shard_map/ppermute | solution.py:646
  29.5 0.2 collective-permute-done.4.refs_2_
  29.7 0.8 %prefix.1 = (f32[4,2,128,256]{3,2,1,0:T(8,128)S(1)}, f32[2,128,128]{2,1,0:T(8,128)S(1)}) custom-call(f32[2,128,256]{2,1,0:T(8,128)S(1)} %get-tuple-element.147.refs_0_, f32[2,128,256]{2,1,0:T(8,128)S(1)} %collective-permute-done.3.refs_1_, f32[2,128,256]{2,1,0:T(8,128)S(1)} %collective-permute-done.4.refs_2_, f32[2,128,256]{2,1,0:T(8,128)S(1)} %collective-permute-done.5.refs_3_), custom_call_target="tpu_custom_call" | custom-call | tf_op jit(solution)/shard_map/prefix/pallas_call | solution.py:652
  30.5 4.5 %collective-permute-start.6 = (f32[2,128,128]{2,1,0:T(8,128)S(1)}, f32[2,128,128]{2,1,0:T(8,128)S(1)}, u32[]{:S(2)}, u32[]{:S(2)}) collective-permute-start(f32[2,128,128]{2,1,0:T(8,128)S(1)} %get-tuple-element.160), channel_id=1, source_target_pairs={{0,16},{4,20},{8,24},{12,28},{1,17},{5,21},{9,25},{13,29},{2,18},{... | collective-permute-start | bytes 393224 | tf_op jit(solution)/shard_map/ppermute | solution.py:677
  35.0 2.1 %query.4 = (f32[2,2,512,128]{3,2,1,0:T(8,128)S(1)}, bf16[2,2,512,128]{3,2,1,0:T(8,128)(2,1)S(1)}, bf16[2,2,512,128]{3,2,1,0:T(8,128)(2,1)S(1)}) custom-call(bf16[512,512]{1,0:T(8,128)(2,1)S(1)} %copy-done.1, bf16[16,2048]{1,0:T(8,128)(2,1)S(1)} %collective-permute-done.2.refs_6_.before_ref, f32[24,2048]{1,0:T(8,128)S(1)} %get-tuple-element.104.edge_ref.refs_7_, ...), custom_call_target="tpu_custom_call" | custom-call | flops 4000000000 | bytes 4000000 | tf_op jit(solution)/shard_map/query/pallas_call | solution.py:618
  37.1 0.4 collective-permute-done.6.entering_ref
  37.5 0.3 enter.1
  37.9 3.1 %collective-permute-start.7 = (f32[2,128,128]{2,1,0:T(8,128)S(1)}, f32[2,128,128]{2,1,0:T(8,128)S(1)}, u32[]{:S(2)}, u32[]{:S(2)}) collective-permute-start(f32[2,128,128]{2,1,0:T(8,128)S(1)} %get-tuple-element.185), channel_id=1, source_target_pairs={{0,12},{4,8},{8,4},{12,0},{16,28},{20,24},{24,20},{28,16},{1,13},{... | collective-permute-start | bytes 393224 | tf_op jit(solution)/shard_map/ppermute | solution.py:687
  41.0 0.6 %collective-permute-start.8 = (f32[2,128,128]{2,1,0:T(8,128)S(1)}, f32[2,128,128]{2,1,0:T(8,128)S(1)}, u32[]{:S(2)}, u32[]{:S(2)}) collective-permute-start(f32[2,128,128]{2,1,0:T(8,128)S(1)} %get-tuple-element.186), channel_id=1, source_target_pairs={{0,4},{4,0},{8,12},{12,8},{16,20},{20,16},{24,28},{28,24},{1,5},{5... | collective-permute-start | bytes 393224 | tf_op jit(solution)/shard_map/ppermute | solution.py:687
  41.5 0.1 collective-permute-start.9
  41.6 1.1 %query.5 = (f32[1,2,512,128]{3,2,1,0:T(8,128)S(1)}, bf16[1,2,512,128]{3,2,1,0:T(8,128)(2,1)S(1)}, bf16[1,2,512,128]{3,2,1,0:T(8,128)(2,1)S(1)}) custom-call(bf16[512,512]{1,0:T(8,128)(2,1)S(1)} %copy-done.1, bf16[16,2048]{1,0:T(8,128)(2,1)S(1)} %collective-permute-done.2.refs_6_.before_ref, f32[24,2048]{1,0:T(8,128)S(1)} %get-tuple-element.104.edge_ref.refs_7_, ...), custom_call_target="tpu_custom_call" | custom-call | flops 2000000000 | bytes 2000000 | tf_op jit(solution)/shard_map/query/pallas_call | solution.py:618
  42.8 1.2 %outputs.2.refs_12_ = f32[512,1024]{1,0:T(8,128)} custom-call(f32[1,2,512,128]{3,2,1,0:T(8,128)S(1)} %get-tuple-element.193.refs_0_, bf16[1,2,512,128]{3,2,1,0:T(8,128)(2,1)S(1)} %get-tuple-element.194.refs_1_, bf16[1,2,512,128]{3,2,1,0:T(8,128)(2,1)S(1)} %get-tuple-element.195.refs_2_, f32[2,128,128]{2,1,0:T(8,128)S(1)} %get-tuple-element.196.refs_3_), custom_call_target="tpu_custom_call" | custom-call | tf_op jit(solution)/shard_map/outputs/pallas_call | solution.py:694
  43.9 0.7 %collective-permute-done.7.refs_9_ = f32[2,128,128]{2,1,0:T(8,128)S(1)} collective-permute-done((f32[2,128,128]{2,1,0:T(8,128)S(1)}, f32[2,128,128]{2,1,0:T(8,128)S(1)}, u32[]{:S(2)}, u32[]{:S(2)}) %collective-permute-start.7) | collective-permute-done | bytes 131104 | tf_op jit(solution)/shard_map/ppermute | solution.py:687
  44.6 1.4 %collective-permute-done.8.refs_10_ = f32[2,128,128]{2,1,0:T(8,128)S(1)} collective-permute-done((f32[2,128,128]{2,1,0:T(8,128)S(1)}, f32[2,128,128]{2,1,0:T(8,128)S(1)}, u32[]{:S(2)}, u32[]{:S(2)}) %collective-permute-start.8) | collective-permute-done | bytes 131104 | tf_op jit(solution)/shard_map/ppermute | solution.py:687
  46.0 0.5 %collective-permute-done.9.refs_11_ = f32[2,128,128]{2,1,0:T(8,128)S(1)} collective-permute-done((f32[2,128,128]{2,1,0:T(8,128)S(1)}, f32[2,128,128]{2,1,0:T(8,128)S(1)}, u32[]{:S(2)}, u32[]{:S(2)}) %collective-permute-start.9) | collective-permute-done | bytes 131104 | tf_op jit(solution)/shard_map/ppermute | solution.py:687
  46.5 1.6 %outputs.3 = f32[512,1024]{1,0:T(8,128)} custom-call(f32[1,2,512,128]{3,2,1,0:T(8,128)S(1)} %get-tuple-element.177.refs_0_, bf16[1,2,512,128]{3,2,1,0:T(8,128)(2,1)S(1)} %get-tuple-element.178.refs_1_, bf16[1,2,512,128]{3,2,1,0:T(8,128)(2,1)S(1)} %get-tuple-element.179.refs_2_, ...), custom_call_target="tpu_custom_call", output_to_operand_aliasing={{}: (12, {})} | custom-call | tf_op jit(solution)/shard_map/outputs/pallas_call | solution.py:694
  (5 shorter events, 0.0 us)
Async XLA Ops:
  1.5 8.8 %copy-start = (bf16[256,1920]{1,0:T(8,128)(2,1)S(1)}, bf16[256,1920]{1,0:T(8,128)(2,1)}, u32[]{:S(2)}) copy-start(bf16[256,1920]{1,0:T(8,128)(2,1)} %constant.2.clone.refs_8_) | copy-start | bytes 2949124
  1.5 3.1 %collective-permute-start = (f32[2,16,512]{2,1,0:T(8,128)S(1)}, f32[2,16,512]{2,1,0:T(8,128)S(1)}, u32[]{:S(2)}, u32[]{:S(2)}) collective-permute-start(f32[2,16,512]{2,1,0:T(8,128)S(1)} %get-tuple-element.103), channel_id=1, source_target_pairs={{0,1},{1,0},{2,3},{3,2},{4,5},{5,4},{6,7},{7,6},{8,9},{9,8},{10,11... | collective-permute-start | bytes 196616 | tf_op jit(solution)/shard_map/ppermute | solution.py:564
  2.0 8.3 %collective-permute-start.2 = (bf16[16,2048]{1,0:T(8,128)(2,1)S(1)}, bf16[16,2048]{1,0:T(8,128)(2,1)S(1)}, u32[]{:S(2)}, u32[]{:S(2)}) collective-permute-start(bf16[16,2048]{1,0:T(8,128)(2,1)S(1)} %get-tuple-element.108), channel_id=1, source_target_pairs={{0,4},{4,8},{8,12},{12,16},{16,20},{20,24},{24,28},{28,0},{1,5},{5... | collective-permute-start | bytes 196616 | tf_op jit(solution)/shard_map/ppermute | solution.py:569
  4.6 5.7 %collective-permute-start.1 = (f32[16,512]{1,0:T(8,128)S(1)}, f32[16,512]{1,0:T(8,128)S(1)}, u32[]{:S(2)}, u32[]{:S(2)}) collective-permute-start(f32[16,512]{1,0:T(8,128)S(1)} %fusion), channel_id=1, source_target_pairs={{0,2},{1,3},{2,0},{3,1},{4,6},{5,7},{6,4},{7,5},{8,10},{9,11},{10,... | collective-permute-start | bytes 98312 | tf_op jit(solution)/shard_map/ppermute | solution.py:566
  13.5 13.6 %collective-permute-start.5 = (f32[2,128,256]{2,1,0:T(8,128)S(1)}, f32[2,128,256]{2,1,0:T(8,128)S(1)}, u32[]{:S(2)}, u32[]{:S(2)}) collective-permute-start(f32[2,128,256]{2,1,0:T(8,128)S(1)} %get-tuple-element.134), channel_id=1, source_target_pairs={{0,12},{4,8},{8,4},{12,0},{16,28},{20,24},{24,20},{28,16},{1,13},{... | collective-permute-start | bytes 786440 | tf_op jit(solution)/shard_map/ppermute | solution.py:646
  21.6 4.4 %copy-start.1 = (bf16[512,512]{1,0:T(8,128)(2,1)S(1)}, bf16[512,512]{1,0:T(8,128)(2,1)}, u32[]{:S(2)}) copy-start(bf16[512,512]{1,0:T(8,128)(2,1)} %q_ref.5) | copy-start | bytes 1572868
  21.6 7.9 %collective-permute-start.3 = (f32[2,128,256]{2,1,0:T(8,128)S(1)}, f32[2,128,256]{2,1,0:T(8,128)S(1)}, u32[]{:S(2)}, u32[]{:S(2)}) collective-permute-start(f32[2,128,256]{2,1,0:T(8,128)S(1)} %get-tuple-element.132), channel_id=1, source_target_pairs={{0,4},{4,0},{8,12},{12,8},{16,20},{20,16},{24,28},{28,24},{1,5},{5... | collective-permute-start | bytes 786440 | tf_op jit(solution)/shard_map/ppermute | solution.py:646
  22.1 7.5 %collective-permute-start.4 = (f32[2,128,256]{2,1,0:T(8,128)S(1)}, f32[2,128,256]{2,1,0:T(8,128)S(1)}, u32[]{:S(2)}, u32[]{:S(2)}) collective-permute-start(f32[2,128,256]{2,1,0:T(8,128)S(1)} %get-tuple-element.133), channel_id=1, source_target_pairs={{0,8},{4,12},{8,0},{12,4},{16,24},{20,28},{24,16},{28,20},{1,9},{5... | collective-permute-start | bytes 786440 | tf_op jit(solution)/shard_map/ppermute | solution.py:646
  30.5 7.0 %collective-permute-start.6 = (f32[2,128,128]{2,1,0:T(8,128)S(1)}, f32[2,128,128]{2,1,0:T(8,128)S(1)}, u32[]{:S(2)}, u32[]{:S(2)}) collective-permute-start(f32[2,128,128]{2,1,0:T(8,128)S(1)} %get-tuple-element.160), channel_id=1, source_target_pairs={{0,16},{4,20},{8,24},{12,28},{1,17},{5,21},{9,25},{13,29},{2,18},{... | collective-permute-start | bytes 393224 | tf_op jit(solution)/shard_map/ppermute | solution.py:677
  37.9 6.7 %collective-permute-start.7 = (f32[2,128,128]{2,1,0:T(8,128)S(1)}, f32[2,128,128]{2,1,0:T(8,128)S(1)}, u32[]{:S(2)}, u32[]{:S(2)}) collective-permute-start(f32[2,128,128]{2,1,0:T(8,128)S(1)} %get-tuple-element.185), channel_id=1, source_target_pairs={{0,12},{4,8},{8,4},{12,0},{16,28},{20,24},{24,20},{28,16},{1,13},{... | collective-permute-start | bytes 393224 | tf_op jit(solution)/shard_map/ppermute | solution.py:687
  41.0 5.0 %collective-permute-start.8 = (f32[2,128,128]{2,1,0:T(8,128)S(1)}, f32[2,128,128]{2,1,0:T(8,128)S(1)}, u32[]{:S(2)}, u32[]{:S(2)}) collective-permute-start(f32[2,128,128]{2,1,0:T(8,128)S(1)} %get-tuple-element.186), channel_id=1, source_target_pairs={{0,4},{4,0},{8,12},{12,8},{16,20},{20,16},{24,28},{28,24},{1,5},{5... | collective-permute-start | bytes 393224 | tf_op jit(solution)/shard_map/ppermute | solution.py:687
  41.5 5.0 %collective-permute-start.9 = (f32[2,128,128]{2,1,0:T(8,128)S(1)}, f32[2,128,128]{2,1,0:T(8,128)S(1)}, u32[]{:S(2)}, u32[]{:S(2)}) collective-permute-start(f32[2,128,128]{2,1,0:T(8,128)S(1)} %get-tuple-element.187), channel_id=1, source_target_pairs={{0,8},{4,12},{8,0},{12,4},{16,24},{20,28},{24,16},{28,20},{1,9},{5... | collective-permute-start | bytes 393224 | tf_op jit(solution)/shard_map/ppermute | solution.py:687

commit v5 on v4

--- a/solution.py
+++ b/solution.py
@@ -164,9 +164,9 @@
         padded[at, 0, 8:] = k_held[at].astype(f32)
         keys = unit(conv_rows(padded.at[at, 0], key_taps, tokens))
         unit_ref[at] = keys
-        for c in range(tokens // BLOCK):
+        for c in range(1, tokens // BLOCK):
             part = split(keys[c * BLOCK : (c + 1) * BLOCK])
-            dots_ref[at, c] = dot_split(part, part, NT)
+            dots_ref[at, c - 1] = dot_split(part, part, NT)
         copies[at][1].wait()
         for b in range(2):
             here = slice(b * DV, (b + 1) * DV)
@@ -249,32 +249,79 @@
     return jnp.concatenate([both[:, :DV] + added, both[:, DV:]], axis=1)
 
 
+def gates(p, scales_ref, logit_refs):
+    row, column = iotas()
+    decays, rates = [], []
+    for b in range(2):
+        h = 2 * p + b
+        u = logit_refs[0][0, pl.ds(2 * h, 1), :] + logit_refs[1][0, pl.ds(2 * h, 1), :]
+        w = logit_refs[0][0, pl.ds(2 * h + 1, 1), :] + logit_refs[1][0, pl.ds(2 * h + 1, 1), :]
+        for ref in logit_refs[2:]:
+            u = u + ref[pl.ds(2 * h, 1), :]
+            w = w + ref[pl.ds(2 * h + 1, 1), :]
+        decays.append(-scales_ref[pl.ds(h, 1), :] * softplus(u))
+        rates.append(1.0 / (1.0 + jnp.exp(-w)))
+    blocks = decays[0].shape[1] // BLOCK
+    decay_rows, rate_rows = (
+        jnp.concatenate(
+            [x[:, c * BLOCK : (c + 1) * BLOCK] for x in both for c in range(blocks)], axis=0
+        )
+        for both in (decays, rates)
+    )
+    sums = jnp.dot(
+        decay_rows,
+        jnp.where(row <= column, 1.0, 0.0),
+        precision=lax.Precision.HIGHEST,
+        preferred_element_type=f32,
+    )
+    last = sums[:, BLOCK - 1 : BLOCK]
+    columns = jnp.concatenate(
+        [
+            jnp.transpose(x)
+            for x in (sums, rate_rows, rate_rows * jnp.exp(sums), jnp.exp(last - sums))
+        ],
+        axis=1,
+    )
+    return jnp.concatenate([sums, jnp.broadcast_to(jnp.exp(last), sums.shape)], axis=0), columns
+
+
 def solve_kernel(
     slots,
     start,
     group,
     key_width,
     pieces,
-    scales_ref,
     *refs,
 ):
-    logit_refs, refs = refs[:pieces], refs[pieces:]
+    if pieces:
+        (scales_ref, *logit_refs), refs = refs[: 1 + pieces], refs[1 + pieces :]
+    else:
+        (rows_ref, columns_ref), refs = refs[:2], refs[2:]
     (unit_ref, dots_ref, mixed_ref, before_ref, edge_ref, pick_ref), refs = refs[:6], refs[6:]
     count = len(slots)
     message_refs, refs = refs[:count], refs[count:]
-    solved_ref, starts_ref, cumulative_ref, first_ref, padded = refs
+    (solved_ref, starts_ref, first_ref), refs = refs[:3], refs[3:]
+    if pieces:
+        (rows_ref, columns_ref), refs = refs[:2], refs[2:]
+    (padded,) = refs
     tokens = unit_ref.shape[1]
     blocks = tokens // BLOCK
+    height = 2 * blocks
     place = lax.axis_index("seq") % group
     row, column = iotas()
-    upper = jnp.where(row <= column, 1.0, 0.0)
     identity = row == column
     strict = row > column
 
+    known = {}
+    if pieces:
+        for s in range(group):
+            known[s] = gates(place ^ slot_partner(group, s), scales_ref, logit_refs)
+            rows_ref[s], columns_ref[s] = known[s]
     systems, rights, tails, ends, key_parts = [], [], [], [], []
     for at, s in enumerate(slots):
         p = place ^ slot_partner(group, s)
         kcol, vcol = lanes(key_width + p * DK, DK), lanes(2 * key_width + p * 2 * DV, 2 * DV)
+        rows, columns = known[s] if s in known else (rows_ref[s], columns_ref[s])
         key_taps = edge_ref[EDGE : EDGE + KCONV, kcol]
         value_taps = edge_ref[EDGE : EDGE + KCONV, vcol]
         padded[0, 0:8] = rows_before(before_ref, kcol)
@@ -288,32 +335,6 @@
             padded[1 + b, 8:] = edge_values[:, here]
             edges.append(conv_rows(padded.at[1 + b], value_taps[:, here], EDGE))
         edge_values = jnp.concatenate(edges, axis=1)
-        decays, rates = [], []
-        for b in range(2):
-            h = 2 * p + b
-            u = logit_refs[0][0, pl.ds(2 * h, 1), :] + logit_refs[1][0, pl.ds(2 * h, 1), :]
-            w = logit_refs[0][0, pl.ds(2 * h + 1, 1), :] + logit_refs[1][0, pl.ds(2 * h + 1, 1), :]
-            for ref in logit_refs[2:]:
-                u = u + ref[pl.ds(2 * h, 1), :]
-                w = w + ref[pl.ds(2 * h + 1, 1), :]
-            decays.append(-scales_ref[pl.ds(h, 1), :] * softplus(u))
-            rates.append(1.0 / (1.0 + jnp.exp(-w)))
-        decay_rows = jnp.concatenate(
-            [d[:, c * BLOCK : (c + 1) * BLOCK] for d in decays for c in range(blocks)], axis=0
-        )
-        rate_rows = jnp.concatenate(
-            [r[:, c * BLOCK : (c + 1) * BLOCK] for r in rates for c in range(blocks)], axis=0
-        )
-        sums = jnp.dot(
-            decay_rows, upper, precision=lax.Precision.HIGHEST, preferred_element_type=f32
-        )
-        cumulative_ref[at] = sums
-        cum_columns = jnp.transpose(sums)
-        rate_columns = jnp.transpose(rate_rows)
-        growth_columns = jnp.exp(cum_columns)
-        last = sums[:, BLOCK - 1 : BLOCK]
-        tail_columns = jnp.exp(jnp.transpose(last - sums))
-        end_values = jnp.exp(last)
         for c in range(blocks):
             keys = unit_ref[start + at, pl.ds(c * BLOCK, BLOCK), :]
             values = mixed_ref[start + at, pl.ds(c * BLOCK, BLOCK), :]
@@ -323,24 +344,26 @@
                 first_ref[at] = keys
             parts = split(keys)
             key_parts.append(parts)
-            dots = dot_split(parts, parts, NT) if c == 0 else dots_ref[start + at, c]
+            dots = dot_split(parts, parts, NT) if c == 0 else dots_ref[start + at, c - 1]
             for b in range(2):
                 r = b * blocks + c
-                rate = rate_columns[:, r : r + 1]
-                spread = cum_columns[:, r : r + 1] - sums[r : r + 1, :]
+                cum, rate, scaled, tail = (
+                    columns[:, n * height + r : n * height + r + 1] for n in range(4)
+                )
+                spread = cum - rows[r : r + 1, :]
                 table = jnp.exp(jnp.where(strict, spread, FAR))
                 systems.append(rate * table * dots)
                 rights.append(
                     jnp.concatenate(
                         [
                             rate * values[:, b * DV : (b + 1) * DV],
-                            (rate * growth_columns[:, r : r + 1]) * keys,
+                            scaled * keys,
                         ],
                         axis=1,
                     )
                 )
-                tails.append(tail_columns[:, r : r + 1])
-                ends.append(end_values[r : r + 1, :])
+                tails.append(tail)
+                ends.append(rows[height + r : height + r + 1, :])
 
     inverses = invert_all(systems, pick_ref[...])
     solved = [dot_split(split(x), split(r)) for x, r in zip(inverses, rights)]
@@ -368,11 +391,9 @@
                         starts_ref[at, b, c - 1] = both
                     both = followed(moves[b, c], both)
                 parts.append(both)
-            both = parts[0]
-            for c in range(half, blocks):
-                starts_ref[at, b, c - 1] = both
-                if c < blocks - 1:
-                    both = followed(moves[b, c], both)
+            starts_ref[at, b, half - 1] = parts[0]
+            for c in range(half, blocks - 1):
+                starts_ref[at, b, c] = jnp.concatenate(moves[b, c], axis=1)
             both = followed((parts[1][:, :DV], parts[1][:, DV:]), parts[0])
             message_refs[at][b] = both
 
@@ -386,7 +407,8 @@
     edge_ref,
     unit_ref,
     first_ref,
-    cumulative_ref,
+    rows_ref,
+    columns_ref,
     solved_ref,
     starts_ref,
     own_ref,
@@ -407,8 +429,7 @@
         padded[8:] = q_ref[:, columns].astype(f32)
         taps = edge_ref[EDGE : EDGE + KCONV, columns]
         queries = unit(conv_rows(padded, taps, tokens), 1.0 / math.sqrt(DK))
-        sums = cumulative_ref[at]
-        cum_columns = jnp.transpose(sums)
+        sums, cum_columns = rows_ref[s], columns_ref[s]
         growth_columns = jnp.exp(cum_columns)
         for c in range(blocks):
             here = queries[c * BLOCK : (c + 1) * BLOCK]
@@ -424,10 +445,18 @@
         dot_split(attend, split(solved_ref[at, b, pl.ds(c * BLOCK, BLOCK), :]))
         for at, b, c, attend, grown in work
     ]
+    begins = {}
+    for at in range(len(slots)):
+        for b in range(2):
+            for c in range(1, blocks):
+                both = starts_ref[at, b, c - 1]
+                if c > blocks // 2:
+                    both = followed((both[:, :DV], both[:, DV:]), begins[at, b, c - 1])
+                begins[at, b, c] = both
     for (at, b, c, attend, grown), one in zip(work, seen):
         own, reads = one[:, :DV], grown - one[:, DV:]
         if c > 0:
-            through = dot_split(split(reads), split(starts_ref[at, b, c - 1]))
+            through = dot_split(split(reads), split(begins[at, b, c]))
             own, reads = own + through[:, :DV], through[:, DV:]
         here = pl.ds(c * BLOCK, BLOCK)
         own_ref[at, b, here, :] = own
@@ -467,7 +496,9 @@
     place = lax.axis_index("seq") % group
     heads = entering_ref.shape[0]
     count = group if onward else group - 1
-    states = [[entering_ref[b] for b in range(heads)]] + [[] for i in range(count)]
+    later = lax.axis_index("seq") >= group
+    states = [[jnp.where(later, entering_ref[b], 0.0) for b in range(heads)]]
+    states += [[] for i in range(count)]
     for b in range(heads):
         moves = jnp.concatenate([chain_ref[i, b, :, DV:] for i in range(count)], axis=0)
         moved = dot_split(split(moves), split(states[0][b]))
@@ -571,7 +602,7 @@
     pick = jnp.asarray(pick_matrix())
 
     def mix_shapes(count):
-        return [(count, tokens, DK), (count, blocks, BLOCK, BLOCK), (count, tokens, 2 * DV)]
+        return [(count, tokens, DK), (count, blocks - 1, BLOCK, BLOCK), (count, tokens, 2 * DV)]
 
     def mix_scratch(count):
         return [
@@ -579,14 +610,6 @@
             VMEM((count, tokens, 2 * DV), bf16),
             VMEM((count, 3, tokens + 8, DK), f32),
             pltpu.SemaphoreType.DMA((count, 2)),
-        ]
-
-    def solve_shapes(count):
-        return [shape(2, DK, 2 * DK)] * count + [
-            shape(count, 2, tokens, 2 * DK),
-            shape(count, 2, blocks - 1, DK, 2 * DK),
-            shape(count, 2 * blocks, BLOCK),
-            shape(count, BLOCK, DK),
         ]
 
     def mix(slots):
@@ -601,23 +624,35 @@
             name="mix",
         )(edge, in_hbm(key_in), in_hbm(value_in))
 
-    def solve(slots, start, logits, unit_keys, key_dots, mixed):
+    def solve(slots, start, known, first, unit_keys, key_dots, mixed):
         count = len(slots)
+        gate_shapes = [
+            shape(group, 4 * blocks, BLOCK),
+            shape(group, BLOCK, 8 * blocks),
+        ]
         return pl.pallas_call(
-            functools.partial(solve_kernel, slots, start, group, key_width, len(logits)),
-            in_specs=[whole()] * (len(logits) + 7),
-            out_specs=[whole()] * (count + 4),
-            out_shape=solve_shapes(count),
+            functools.partial(
+                solve_kernel, slots, start, group, key_width, len(known) - 1 if first else 0
+            ),
+            in_specs=[whole()] * (len(known) + 6),
+            out_specs=[whole()] * (count + 3 + 2 * first),
+            out_shape=[shape(2, DK, 2 * DK)] * count
+            + [
+                shape(count, 2, tokens, 2 * DK),
+                shape(count, 2, blocks - 1, DK, 2 * DK),
+                shape(count, BLOCK, DK),
+            ]
+            + gate_shapes * first,
             scratch_shapes=[VMEM((3, EDGE + 8, DK), f32)],
             compiler_params=params(),
             name="solve",
-        )(scales, *logits, unit_keys, key_dots, mixed, before, edge, pick)
-
-    def query(slots, start, unit_keys, solved, starts, cumulative, first_keys):
+        )(*known, unit_keys, key_dots, mixed, before, edge, pick)
+
+    def query(slots, start, unit_keys, solved, starts, first_keys):
         count = len(slots)
         return pl.pallas_call(
             functools.partial(query_kernel, slots, start, group),
-            in_specs=[whole()] * 8,
+            in_specs=[whole()] * 9,
             out_specs=[whole()] * 3,
             out_shape=[shape(count, 2, tokens, DV)]
             + [shape(count, 2, tokens, DK, dtype=bf16)] * 2,
@@ -627,14 +662,18 @@
                 flops=2_000_000_000 * count, bytes_accessed=2_000_000 * count, transcendentals=0
             ),
             name="query",
-        )(query_in, before, edge, unit_keys, first_keys, cumulative, solved, starts)
+        )(query_in, before, edge, unit_keys, first_keys, *known, solved, starts)
 
     calls = solve_calls(group)
     mixed = mix(sum(calls, ()))
     messages, rest, start = [], [], 0
+    known = [scales, *logits]
     for slots in calls:
-        results = solve(slots, start, logits, *mixed)
-        results, logits = lax.optimization_barrier((results, logits))
+        results = solve(slots, start, known, not start, *mixed)
+        if not start:
+            *results, rows, columns = results
+            known = [rows, columns]
+        results, known = lax.optimization_barrier((results, known))
         messages += results[: len(slots)]
         rest.append([mixed[0], *results[len(slots) :]])
         start += len(slots)
@@ -674,7 +713,7 @@
     if not hops:
         entering = enter(jnp.zeros((2, DK, DV), f32), False)
     for hop in range(hops):
-        received = lax.ppermute(leaving, "seq", [(i, i + group) for i in range(seq - group)])
+        received = lax.ppermute(leaving, "seq", [(i, (i + group) % seq) for i in range(seq)])
         if hop == 0:
             reads += [query(*x, *outs) for *x, outs in zip(calls[1:-1], starts[1:-1], rest[1:-1])]
             received, reads, rest = lax.optimization_barrier((received, reads, rest))

time: 48.4 us -> 48.1 us (level)
  waiting for transfers between devices: 5.51 us -> 7.97 us
  starting transfers between devices: 16.5 us -> 14.5 us
  Pallas kernels: 25.9 us -> 25.2 us
    ppermute x1, waiting for transfers between devices: 0.36 us -> 2.84 us  [per_device(): lax.ppermute(leaving, 'seq', [(i, (i + group) % seq) for i in range(seq)])]
    ppermute x1, starting transfers between devices: 4.5 us -> 2.66 us  [per_device(): lax.ppermute(leaving, 'seq', [(i, (i + group) % seq) for i in range(seq)])]
    pallas_call x3, Pallas kernels: 11.9 us -> 11.4 us  [solve(): pl.pallas_call(functools.partial(solve_kernel, slots, start, group, key_w...]
  transfers between devices with their start and end apart: 10 -> 10, of which waited for: 6 -> 6; matrix products, arithmetic and copies ran while one was open for 0% -> 0% of each run, Pallas kernels for 38% -> 37%
where the time goes in v5:
time: 48.1 us; the launch traced here: 47.9 us
  Pallas kernels  25.2 us (52%)
  starting transfers between devices  14.5 us (30%)
  waiting for transfers between devices  7.97 us (17%)
    pallas_call x3, Pallas kernels, solve(): pl.pallas_call(functools.partial(solve_kernel, slots, start, group, key_w...  11.4 us
    pallas_call x3, Pallas kernels, query(): pl.pallas_call(functools.partial(query_kernel, slots, start, group), in_s...  4.48 us
    pallas_call x1, Pallas kernels, mix(): pl.pallas_call(functools.partial(mix_kernel, slots, group, key_width), in...  3.92 us
    ppermute x3, starting transfers between devices, per_device(): lax.ppermute(messages[s], 'seq', [(i, i ^ d) for i in range(seq)])  3.63 us
    ppermute x3, starting transfers between devices, per_device(): lax.ppermute(entering[d], 'seq', [(i, i ^ d) for i in range(seq)])  3.55 us
    ppermute x1, waiting for transfers between devices, per_device(): lax.ppermute(leaving, 'seq', [(i, (i + group) % seq) for i in range(seq)])  2.84 us
    pallas_call x2, Pallas kernels, outputs(): pl.pallas_call(functools.partial(output_kernel, group, [(s, where[s][1])...  2.75 us
    ppermute x1, starting transfers between devices, per_device(): lax.ppermute(leaving, 'seq', [(i, (i + group) % seq) for i in range(seq)])  2.66 us
  transfers between devices with their start and end apart: 10, of which 6 were waited for; matrix products, arithmetic and copies ran while one was open for 0% of the time, Pallas kernels for 37%

profile of v5, /device:TPU:0, one launch (start us, length us, event | category | flops | bytes accessed | tf_op | source)
XLA Modules:
  0.0 47.9 jit_solution(11315863639088113528)
XLA Ops:
  0.0 1.5 %logits.1 = (f32[2,16,512]{2,1,0:T(8,128)S(1)}, f32[2,16,512]{2,1,0:T(8,128)S(1)}, bf16[16,2048]{1,0:T(8,128)(2,1)S(1)}, f32[24,2048]{1,0:T(8,128)S(1)}, f32[8,512]{1,0:T(8,128)S(1)}) custom-call(f32[1,8]{1,0:T(1,128)} %bitcast.6, f32[1,8]{1,0:T(1,128)} %bitcast.7, bf16[512,512]{1,0:T(8,128)(2,1)} %hidden_ref.1, bf16[64,512]{1,0:T(8,128)(2,1)} %bitcast.5, ...), custom_call_target="tpu_custom_call" | custom-call | tf_op jit(solution)/shard_map/logits/pallas_call | solution.py:577
  1.5 0.0 copy-start
  1.5 0.5 %collective-permute-start = (f32[2,16,512]{2,1,0:T(8,128)S(1)}, f32[2,16,512]{2,1,0:T(8,128)S(1)}, u32[]{:S(2)}, u32[]{:S(2)}) collective-permute-start(f32[2,16,512]{2,1,0:T(8,128)S(1)} %get-tuple-element.89), channel_id=1, source_target_pairs={{0,1},{1,0},{2,3},{3,2},{4,5},{5,4},{6,7},{7,6},{8,9},{9,8},{10,11... | collective-permute-start | bytes 196616 | tf_op jit(solution)/shard_map/ppermute | solution.py:595
  2.0 2.6 %collective-permute-start.2 = (bf16[16,2048]{1,0:T(8,128)(2,1)S(1)}, bf16[16,2048]{1,0:T(8,128)(2,1)S(1)}, u32[]{:S(2)}, u32[]{:S(2)}) collective-permute-start(bf16[16,2048]{1,0:T(8,128)(2,1)S(1)} %get-tuple-element.94), channel_id=1, source_target_pairs={{0,4},{4,8},{8,12},{12,16},{16,20},{20,24},{24,28},{28,0},{1,5},{5... | collective-permute-start | bytes 196616 | tf_op jit(solution)/shard_map/ppermute | solution.py:600
  4.6 0.0 collective-permute-done.refs_2_
  4.6 1.6 %collective-permute-start.1 = (f32[16,512]{1,0:T(8,128)S(1)}, f32[16,512]{1,0:T(8,128)S(1)}, u32[]{:S(2)}, u32[]{:S(2)}) collective-permute-start(f32[16,512]{1,0:T(8,128)S(1)} %fusion), channel_id=1, source_target_pairs={{0,2},{1,3},{2,0},{3,1},{4,6},{5,7},{6,4},{7,5},{8,10},{9,11},{10,... | collective-permute-start | bytes 98312 | tf_op jit(solution)/shard_map/ppermute | solution.py:597
  6.2 3.9 %mix.1 = (f32[4,512,128]{2,1,0:T(8,128)S(1)}, f32[4,3,128,128]{3,2,1,0:T(8,128)S(1)}, f32[4,512,256]{2,1,0:T(8,128)S(1)}) custom-call(f32[24,2048]{1,0:T(8,128)S(1)} %get-tuple-element.90.edge_ref.refs_8_.refs_6_, bf16[512,512]{1,0:T(8,128)(2,1)} %k_ref.1, bf16[512,1024]{1,0:T(8,128)(2,1)} %v_ref.1), custom_call_target="tpu_custom_call" | custom-call | tf_op jit(solution)/shard_map/mix/pallas_call | solution.py:617
  10.1 0.2 collective-permute-done.2.refs_7_.refs_5_.before_ref
  10.3 0.0 collective-permute-done.1.refs_3_
  10.3 3.5 %solve.3 = (f32[2,128,256]{2,1,0:T(8,128)S(1)}, f32[1,2,512,256]{3,2,1,0:T(8,128)S(1)}, f32[1,2,3,128,256]{4,3,2,1,0:T(8,128)S(1)}, f32[1,128,128]{2,1,0:T(8,128...) custom-call(f32[8,512]{1,0:T(8,128)S(1)} %get-tuple-element.87.refs_0_, ...), custom_call_target="tpu_custom_call" | custom-call | tf_op jit(solution)/shard_map/solve/pallas_call | solution.py:633
  13.8 2.4 %collective-permute-start.5 = (f32[2,128,256]{2,1,0:T(8,128)S(1)}, f32[2,128,256]{2,1,0:T(8,128)S(1)}, u32[]{:S(2)}, u32[]{:S(2)}) collective-permute-start(f32[2,128,256]{2,1,0:T(8,128)S(1)} %get-tuple-element.111), channel_id=1, source_target_pairs={{0,12},{4,8},{8,4},{12,0},{16,28},{20,24},{24,20},{28,16},{1,13},{... | collective-permute-start | bytes 786440 | tf_op jit(solution)/shard_map/ppermute | solution.py:685
  16.2 4.9 %solve.4 = (f32[2,128,256]{2,1,0:T(8,128)S(1)}, f32[2,128,256]{2,1,0:T(8,128)S(1)}, f32[2,2,512,256]{3,2,1,0:T(8,128)S(1)}, f32[2,2,3,128,256]{4,3,2,1,0:T(8,128)S(1)}, f32[2,128,128]{2,1,0:T(8,128)S(1)}) custom-call(f32[4,16,128]{2,1,0:T(8,128)S(1)} %get-tuple-element.117.refs_0_.rows_ref, f32[4,128,32]{2,1,0:T(8,128)S(1)} %get-tuple-element.118.refs_1_.columns_ref, ...), custom_call_target="tpu_custom_call" | custom-call | tf_op jit(solution)/shard_map/solve/pallas_call | solution.py:633
  21.1 0.0 copy-start.1
  21.1 0.5 %collective-permute-start.3 = (f32[2,128,256]{2,1,0:T(8,128)S(1)}, f32[2,128,256]{2,1,0:T(8,128)S(1)}, u32[]{:S(2)}, u32[]{:S(2)}) collective-permute-start(f32[2,128,256]{2,1,0:T(8,128)S(1)} %get-tuple-element.109), channel_id=1, source_target_pairs={{0,4},{4,0},{8,12},{12,8},{16,20},{20,16},{24,28},{28,24},{1,5},{5... | collective-permute-start | bytes 786440 | tf_op jit(solution)/shard_map/ppermute | solution.py:685
  21.6 0.6 %collective-permute-start.4 = (f32[2,128,256]{2,1,0:T(8,128)S(1)}, f32[2,128,256]{2,1,0:T(8,128)S(1)}, u32[]{:S(2)}, u32[]{:S(2)}) collective-permute-start(f32[2,128,256]{2,1,0:T(8,128)S(1)} %get-tuple-element.110), channel_id=1, source_target_pairs={{0,8},{4,12},{8,0},{12,4},{16,24},{20,28},{24,16},{28,20},{1,9},{5... | collective-permute-start | bytes 786440 | tf_op jit(solution)/shard_map/ppermute | solution.py:685
  22.3 3.1 %solve.5 = (f32[2,128,256]{2,1,0:T(8,128)S(1)}, f32[1,2,512,256]{3,2,1,0:T(8,128)S(1)}, f32[1,2,3,128,256]{4,3,2,1,0:T(8,128)S(1)}, f32[1,128,128]{2,1,0:T(8,128)S(1)}) custom-call(f32[4,16,128]{2,1,0:T(8,128)S(1)} %get-tuple-element.117.refs_0_.rows_ref, f32[4,128,32]{2,1,0:T(8,128)S(1)} %get-tuple-element.118.refs_1_.columns_ref, ...), custom_call_target="tpu_custom_call" | custom-call | tf_op jit(solution)/shard_map/solve/pallas_call | solution.py:633
  25.4 1.2 %query.3 = (f32[1,2,512,128]{3,2,1,0:T(8,128)S(1)}, bf16[1,2,512,128]{3,2,1,0:T(8,128)(2,1)S(1)}, bf16[1,2,512,128]{3,2,1,0:T(8,128)(2,1)S(1)}) custom-call(bf16[512,512]{1,0:T(8,128)(2,1)S(1)} %copy-done.1, bf16[16,2048]{1,0:T(8,128)(2,1)S(1)} %collective-permute-done.2.refs_7_.refs_5_.before_ref, ...), custom_call_target="tpu_custom_call" | custom-call | flops 2000000000 | bytes 2000000 | tf_op jit(solution)/shard_map/query/pallas_call | solution.py:653
  26.6 2.4 %collective-permute-done.3.refs_1_ = f32[2,128,256]{2,1,0:T(8,128)S(1)} collective-permute-done((f32[2,128,256]{2,1,0:T(8,128)S(1)}, f32[2,128,256]{2,1,0:T(8,128)S(1)}, u32[]{:S(2)}, u32[]{:S(2)}) %collective-permute-start.3) | collective-permute-done | bytes 262176 | tf_op jit(solution)/shard_map/ppermute | solution.py:685
  29.0 0.2 collective-permute-done.4.refs_2_
  29.2 0.8 %prefix.1 = (f32[4,2,128,256]{3,2,1,0:T(8,128)S(1)}, f32[2,128,128]{2,1,0:T(8,128)S(1)}) custom-call(f32[2,128,256]{2,1,0:T(8,128)S(1)} %get-tuple-element.124.refs_0_, f32[2,128,256]{2,1,0:T(8,128)S(1)} %collective-permute-done.3.refs_1_, f32[2,128,256]{2,1,0:T(8,128)S(1)} %collective-permute-done.4.refs_2_, f32[2,128,256]{2,1,0:T(8,128)S(1)} %collective-permute-done.5.refs_3_), custom_call_target="tpu_custom_call" | custom-call | tf_op jit(solution)/shard_map/prefix/pallas_call | solution.py:691
  30.0 2.7 %collective-permute-start.6 = (f32[2,128,128]{2,1,0:T(8,128)S(1)}, f32[2,128,128]{2,1,0:T(8,128)S(1)}, u32[]{:S(2)}, u32[]{:S(2)}) collective-permute-start(f32[2,128,128]{2,1,0:T(8,128)S(1)} %get-tuple-element.135), channel_id=1, source_target_pairs={{0,16},{4,20},{8,24},{12,28},{16,0},{20,4},{24,8},{28,12},{1,17},{... | collective-permute-start | bytes 393224 | tf_op jit(solution)/shard_map/ppermute | solution.py:716
  32.6 2.2 %query.4 = (f32[2,2,512,128]{3,2,1,0:T(8,128)S(1)}, bf16[2,2,512,128]{3,2,1,0:T(8,128)(2,1)S(1)}, bf16[2,2,512,128]{3,2,1,0:T(8,128)(2,1)S(1)}) custom-call(bf16[512,512]{1,0:T(8,128)(2,1)S(1)} %copy-done.1, bf16[16,2048]{1,0:T(8,128)(2,1)S(1)} %collective-permute-done.2.refs_7_.refs_5_.before_ref, ...), custom_call_target="tpu_custom_call" | custom-call | flops 4000000000 | bytes 4000000 | tf_op jit(solution)/shard_map/query/pallas_call | solution.py:653
  34.8 2.8 %collective-permute-done.6.entering_ref = f32[2,128,128]{2,1,0:T(8,128)S(1)} collective-permute-done((f32[2,128,128]{2,1,0:T(8,128)S(1)}, f32[2,128,128]{2,1,0:T(8,128)S(1)}, u32[]{:S(2)}, u32[]{:S(2)}) %collective-permute-start.6) | collective-permute-done | bytes 131104 | tf_op jit(solution)/shard_map/ppermute | solution.py:716
  37.7 0.4 enter.1
  38.0 1.4 %collective-permute-start.7 = (f32[2,128,128]{2,1,0:T(8,128)S(1)}, f32[2,128,128]{2,1,0:T(8,128)S(1)}, u32[]{:S(2)}, u32[]{:S(2)}) collective-permute-start(f32[2,128,128]{2,1,0:T(8,128)S(1)} %get-tuple-element.158), channel_id=1, source_target_pairs={{0,12},{4,8},{8,4},{12,0},{16,28},{20,24},{24,20},{28,16},{1,13},{... | collective-permute-start | bytes 393224 | tf_op jit(solution)/shard_map/ppermute | solution.py:726
  39.4 0.7 %collective-permute-start.8 = (f32[2,128,128]{2,1,0:T(8,128)S(1)}, f32[2,128,128]{2,1,0:T(8,128)S(1)}, u32[]{:S(2)}, u32[]{:S(2)}) collective-permute-start(f32[2,128,128]{2,1,0:T(8,128)S(1)} %get-tuple-element.159), channel_id=1, source_target_pairs={{0,4},{4,0},{8,12},{12,8},{16,20},{20,16},{24,28},{28,24},{1,5},{5... | collective-permute-start | bytes 393224 | tf_op jit(solution)/shard_map/ppermute | solution.py:726
  40.1 1.5 %collective-permute-start.9 = (f32[2,128,128]{2,1,0:T(8,128)S(1)}, f32[2,128,128]{2,1,0:T(8,128)S(1)}, u32[]{:S(2)}, u32[]{:S(2)}) collective-permute-start(f32[2,128,128]{2,1,0:T(8,128)S(1)} %get-tuple-element.160), channel_id=1, source_target_pairs={{0,8},{4,12},{8,0},{12,4},{16,24},{20,28},{24,16},{28,20},{1,9},{5... | collective-permute-start | bytes 393224 | tf_op jit(solution)/shard_map/ppermute | solution.py:726
  41.6 1.1 %query.5 = (f32[1,2,512,128]{3,2,1,0:T(8,128)S(1)}, bf16[1,2,512,128]{3,2,1,0:T(8,128)(2,1)S(1)}, bf16[1,2,512,128]{3,2,1,0:T(8,128)(2,1)S(1)}) custom-call(bf16[512,512]{1,0:T(8,128)(2,1)S(1)} %copy-done.1, bf16[16,2048]{1,0:T(8,128)(2,1)S(1)} %collective-permute-done.2.refs_7_.refs_5_.before_ref, ...), custom_call_target="tpu_custom_call" | custom-call | flops 2000000000 | bytes 2000000 | tf_op jit(solution)/shard_map/query/pallas_call | solution.py:653
  42.7 1.2 %outputs.2.refs_12_ = f32[512,1024]{1,0:T(8,128)} custom-call(f32[1,2,512,128]{3,2,1,0:T(8,128)S(1)} %get-tuple-element.165.refs_0_, bf16[1,2,512,128]{3,2,1,0:T(8,128)(2,1)S(1)} %get-tuple-element.166.refs_1_, bf16[1,2,512,128]{3,2,1,0:T(8,128)(2,1)S(1)} %get-tuple-element.167.refs_2_, f32[2,128,128]{2,1,0:T(8,128)S(1)} %get-tuple-element.168.refs_3_), custom_call_target="tpu_custom_call" | custom-call | tf_op jit(solution)/shard_map/outputs/pallas_call | solution.py:733
  43.9 1.5 %collective-permute-done.7.refs_9_ = f32[2,128,128]{2,1,0:T(8,128)S(1)} collective-permute-done((f32[2,128,128]{2,1,0:T(8,128)S(1)}, f32[2,128,128]{2,1,0:T(8,128)S(1)}, u32[]{:S(2)}, u32[]{:S(2)}) %collective-permute-start.7) | collective-permute-done | bytes 131104 | tf_op jit(solution)/shard_map/ppermute | solution.py:726
  45.4 0.8 %collective-permute-done.8.refs_10_ = f32[2,128,128]{2,1,0:T(8,128)S(1)} collective-permute-done((f32[2,128,128]{2,1,0:T(8,128)S(1)}, f32[2,128,128]{2,1,0:T(8,128)S(1)}, u32[]{:S(2)}, u32[]{:S(2)}) %collective-permute-start.8) | collective-permute-done | bytes 131104 | tf_op jit(solution)/shard_map/ppermute | solution.py:726
  46.2 1.6 %outputs.3 = f32[512,1024]{1,0:T(8,128)} custom-call(f32[1,2,512,128]{3,2,1,0:T(8,128)S(1)} %get-tuple-element.150.refs_0_, bf16[1,2,512,128]{3,2,1,0:T(8,128)(2,1)S(1)} %get-tuple-element.151.refs_1_, bf16[1,2,512,128]{3,2,1,0:T(8,128)(2,1)S(1)} %get-tuple-element.152.refs_2_, ...), custom_call_target="tpu_custom_call", output_to_operand_aliasing={{}: (12, {})} | custom-call | tf_op jit(solution)/shard_map/outputs/pallas_call | solution.py:733
  (5 shorter events, 0.0 us)
Async XLA Ops:
  1.5 8.8 %copy-start = (bf16[256,1920]{1,0:T(8,128)(2,1)S(1)}, bf16[256,1920]{1,0:T(8,128)(2,1)}, u32[]{:S(2)}) copy-start(bf16[256,1920]{1,0:T(8,128)(2,1)} %constant.2.clone.refs_9_.refs_7_) | copy-start | bytes 2949124
  1.5 3.1 %collective-permute-start = (f32[2,16,512]{2,1,0:T(8,128)S(1)}, f32[2,16,512]{2,1,0:T(8,128)S(1)}, u32[]{:S(2)}, u32[]{:S(2)}) collective-permute-start(f32[2,16,512]{2,1,0:T(8,128)S(1)} %get-tuple-element.89), channel_id=1, source_target_pairs={{0,1},{1,0},{2,3},{3,2},{4,5},{5,4},{6,7},{7,6},{8,9},{9,8},{10,11... | collective-permute-start | bytes 196616 | tf_op jit(solution)/shard_map/ppermute | solution.py:595
  2.0 8.3 %collective-permute-start.2 = (bf16[16,2048]{1,0:T(8,128)(2,1)S(1)}, bf16[16,2048]{1,0:T(8,128)(2,1)S(1)}, u32[]{:S(2)}, u32[]{:S(2)}) collective-permute-start(bf16[16,2048]{1,0:T(8,128)(2,1)S(1)} %get-tuple-element.94), channel_id=1, source_target_pairs={{0,4},{4,8},{8,12},{12,16},{16,20},{20,24},{24,28},{28,0},{1,5},{5... | collective-permute-start | bytes 196616 | tf_op jit(solution)/shard_map/ppermute | solution.py:600
  4.6 5.7 %collective-permute-start.1 = (f32[16,512]{1,0:T(8,128)S(1)}, f32[16,512]{1,0:T(8,128)S(1)}, u32[]{:S(2)}, u32[]{:S(2)}) collective-permute-start(f32[16,512]{1,0:T(8,128)S(1)} %fusion), channel_id=1, source_target_pairs={{0,2},{1,3},{2,0},{3,1},{4,6},{5,7},{6,4},{7,5},{8,10},{9,11},{10,... | collective-permute-start | bytes 98312 | tf_op jit(solution)/shard_map/ppermute | solution.py:597
  13.8 12.8 %collective-permute-start.5 = (f32[2,128,256]{2,1,0:T(8,128)S(1)}, f32[2,128,256]{2,1,0:T(8,128)S(1)}, u32[]{:S(2)}, u32[]{:S(2)}) collective-permute-start(f32[2,128,256]{2,1,0:T(8,128)S(1)} %get-tuple-element.111), channel_id=1, source_target_pairs={{0,12},{4,8},{8,4},{12,0},{16,28},{20,24},{24,20},{28,16},{1,13},{... | collective-permute-start | bytes 786440 | tf_op jit(solution)/shard_map/ppermute | solution.py:685
  21.1 4.3 %copy-start.1 = (bf16[512,512]{1,0:T(8,128)(2,1)S(1)}, bf16[512,512]{1,0:T(8,128)(2,1)}, u32[]{:S(2)}) copy-start(bf16[512,512]{1,0:T(8,128)(2,1)} %q_ref.5) | copy-start | bytes 1572868
  21.1 7.9 %collective-permute-start.3 = (f32[2,128,256]{2,1,0:T(8,128)S(1)}, f32[2,128,256]{2,1,0:T(8,128)S(1)}, u32[]{:S(2)}, u32[]{:S(2)}) collective-permute-start(f32[2,128,256]{2,1,0:T(8,128)S(1)} %get-tuple-element.109), channel_id=1, source_target_pairs={{0,4},{4,0},{8,12},{12,8},{16,20},{20,16},{24,28},{28,24},{1,5},{5... | collective-permute-start | bytes 786440 | tf_op jit(solution)/shard_map/ppermute | solution.py:685
  21.6 7.5 %collective-permute-start.4 = (f32[2,128,256]{2,1,0:T(8,128)S(1)}, f32[2,128,256]{2,1,0:T(8,128)S(1)}, u32[]{:S(2)}, u32[]{:S(2)}) collective-permute-start(f32[2,128,256]{2,1,0:T(8,128)S(1)} %get-tuple-element.110), channel_id=1, source_target_pairs={{0,8},{4,12},{8,0},{12,4},{16,24},{20,28},{24,16},{28,20},{1,9},{5... | collective-permute-start | bytes 786440 | tf_op jit(solution)/shard_map/ppermute | solution.py:685
  30.0 7.7 %collective-permute-start.6 = (f32[2,128,128]{2,1,0:T(8,128)S(1)}, f32[2,128,128]{2,1,0:T(8,128)S(1)}, u32[]{:S(2)}, u32[]{:S(2)}) collective-permute-start(f32[2,128,128]{2,1,0:T(8,128)S(1)} %get-tuple-element.135), channel_id=1, source_target_pairs={{0,16},{4,20},{8,24},{12,28},{16,0},{20,4},{24,8},{28,12},{1,17},{... | collective-permute-start | bytes 393224 | tf_op jit(solution)/shard_map/ppermute | solution.py:716
  38.0 7.3 %collective-permute-start.7 = (f32[2,128,128]{2,1,0:T(8,128)S(1)}, f32[2,128,128]{2,1,0:T(8,128)S(1)}, u32[]{:S(2)}, u32[]{:S(2)}) collective-permute-start(f32[2,128,128]{2,1,0:T(8,128)S(1)} %get-tuple-element.158), channel_id=1, source_target_pairs={{0,12},{4,8},{8,4},{12,0},{16,28},{20,24},{24,20},{28,16},{1,13},{... | collective-permute-start | bytes 393224 | tf_op jit(solution)/shard_map/ppermute | solution.py:726
  39.4 6.8 %collective-permute-start.8 = (f32[2,128,128]{2,1,0:T(8,128)S(1)}, f32[2,128,128]{2,1,0:T(8,128)S(1)}, u32[]{:S(2)}, u32[]{:S(2)}) collective-permute-start(f32[2,128,128]{2,1,0:T(8,128)S(1)} %get-tuple-element.159), channel_id=1, source_target_pairs={{0,4},{4,0},{8,12},{12,8},{16,20},{20,16},{24,28},{28,24},{1,5},{5... | collective-permute-start | bytes 393224 | tf_op jit(solution)/shard_map/ppermute | solution.py:726
  40.1 6.1 %collective-permute-start.9 = (f32[2,128,128]{2,1,0:T(8,128)S(1)}, f32[2,128,128]{2,1,0:T(8,128)S(1)}, u32[]{:S(2)}, u32[]{:S(2)}) collective-permute-start(f32[2,128,128]{2,1,0:T(8,128)S(1)} %get-tuple-element.160), channel_id=1, source_target_pairs={{0,8},{4,12},{8,0},{12,4},{16,24},{20,28},{24,16},{28,20},{1,9},{5... | collective-permute-start | bytes 393224 | tf_op jit(solution)/shard_map/ppermute | solution.py:726

commit v6 on v5

--- a/solution.py
+++ b/solution.py
@@ -77,9 +77,17 @@
     return pltpu.with_memory_space_constraint(x, pltpu.HBM)
 
 
-def rows_before(before_ref, columns):
-    rows = before_ref[:, columns].astype(f32)[EDGE - 8 :]
-    return jnp.where(lax.axis_index("seq") > 0, rows, 0.0)
+HELD = 4
+
+
+def unpack_before(before_ref, earlier_ref):
+    rows = before_ref[...]
+    earlier_ref[...] = jnp.where(lax.axis_index("seq") > 0, rows, 0.0)
+
+
+def fill_before(padded_ref, earlier_ref, tile):
+    for i in range(1, KCONV):
+        padded_ref[8 - KCONV + i : 9 - KCONV + i, :] = earlier_ref[pl.ds(HELD * tile + i, 1), :]
 
 
 def lanes(start, size):
@@ -107,6 +115,7 @@
     edge_ref,
     scales_ref,
     held,
+    packed,
 ):
     rows = proj_ref.shape[0] // head_count
     everything = lax.dot_general(
@@ -128,13 +137,18 @@
     for h in range(heads):
         kept_ref[0, 2 * h : 2 * h + 1, :] = kept_ref[0, 2 * h : 2 * h + 1, :] + bias[h : h + 1]
     edge_ref[...] = jnp.zeros_like(edge_ref)
+    packed[...] = jnp.zeros_like(packed)
     start = 0
     for first, last, taps in ((q_first, q_last, q_taps), (k_first, k_last, k_taps), (v_first, v_last, v_taps)):
         here = slice(start, start + first.shape[1])
-        tail_ref[:, here] = last[...]
+        rows = last[...].astype(f32)[EDGE - KCONV + 1 :]
+        for n in range(first.shape[1] // DK):
+            at = HELD * (start // DK + n)
+            packed[at + 1 : at + KCONV, :] = rows[:, n * DK : (n + 1) * DK]
         edge_ref[0:EDGE, here] = first[...].astype(f32)
         edge_ref[EDGE : EDGE + KCONV, here] = taps[...].astype(f32)
         start += first.shape[1]
+    tail_ref[...] = packed[...]
 
 
 def mix_kernel(slots, group, key_width, edge_ref, k_ref, v_ref, unit_ref, dots_ref, mixed_ref, k_held, v_held, padded, sems):
@@ -303,7 +317,7 @@
     (solved_ref, starts_ref, first_ref), refs = refs[:3], refs[3:]
     if pieces:
         (rows_ref, columns_ref), refs = refs[:2], refs[2:]
-    (padded,) = refs
+    padded, earlier = refs
     tokens = unit_ref.shape[1]
     blocks = tokens // BLOCK
     height = 2 * blocks
@@ -313,6 +327,7 @@
     strict = row > column
 
     known = {}
+    unpack_before(before_ref, earlier)
     if pieces:
         for s in range(group):
             known[s] = gates(place ^ slot_partner(group, s), scales_ref, logit_refs)
@@ -324,14 +339,14 @@
         rows, columns = known[s] if s in known else (rows_ref[s], columns_ref[s])
         key_taps = edge_ref[EDGE : EDGE + KCONV, kcol]
         value_taps = edge_ref[EDGE : EDGE + KCONV, vcol]
-        padded[0, 0:8] = rows_before(before_ref, kcol)
+        fill_before(padded.at[0], earlier, key_width // DK + p)
         padded[0, 8:] = edge_ref[0:EDGE, kcol]
         edge_keys = unit(conv_rows(padded.at[0], key_taps, EDGE))
-        first_values, edge_values = rows_before(before_ref, vcol), edge_ref[0:EDGE, vcol]
+        edge_values = edge_ref[0:EDGE, vcol]
         edges = []
         for b in range(2):
             here = slice(b * DV, (b + 1) * DV)
-            padded[1 + b, 0:8] = first_values[:, here]
+            fill_before(padded.at[1 + b], earlier, 2 * key_width // DK + 2 * p + b)
             padded[1 + b, 8:] = edge_values[:, here]
             edges.append(conv_rows(padded.at[1 + b], value_taps[:, here], EDGE))
         edge_values = jnp.concatenate(edges, axis=1)
@@ -415,17 +430,19 @@
     high_ref,
     low_ref,
     padded,
+    earlier,
 ):
     place = lax.axis_index("seq") % group
     tokens = q_ref.shape[0]
     blocks = tokens // BLOCK
     row, column = iotas()
     causal = row >= column
+    unpack_before(before_ref, earlier)
     work = []
     for at, s in enumerate(slots):
         p = place ^ slot_partner(group, s)
         columns = lanes(p * DK, DK)
-        padded[0:8] = rows_before(before_ref, columns)
+        fill_before(padded, earlier, p)
         padded[8:] = q_ref[:, columns].astype(f32)
         taps = edge_ref[EDGE : EDGE + KCONV, columns]
         queries = unit(conv_rows(padded, taps, tokens), 1.0 / math.sqrt(DK))
@@ -464,31 +481,24 @@
 
 
 def prefix_kernel(group, *refs):
-    messages, refs = refs[:group], refs[group:]
-    chain_ref, leaving_ref, held, sems = refs
+    messages, (chain_ref, leaving_ref) = refs[:group], refs[group:]
     place = lax.axis_index("seq") % group
-    copies = [
-        pltpu.make_async_copy(messages[d], held.at[place ^ d], sems.at[d]) for d in range(group)
-    ]
-    for copy in copies:
-        copy.start()
-    for copy in copies:
-        copy.wait()
     heads = leaving_ref.shape[0]
-    chain = [held[0, b] for b in range(heads)]
-    for i in range(1, group):
-        for b in range(heads):
-            chain_ref[i - 1, b] = chain[b]
-        chain = [
-            dot_split(split(held[i, b, :, DV:]), split(chain[b])) for b in range(heads)
-        ]
-        chain = [
-            jnp.concatenate([chain[b][:, :DV] + held[i, b, :, 0:DV], chain[b][:, DV:]], axis=1)
-            for b in range(heads)
-        ]
-    for b in range(heads):
-        chain_ref[group - 1, b] = chain[b]
-        leaving_ref[b] = chain[b][:, :DV]
+    for j in range(group):
+
+        @pl.when(place == j)
+        def _():
+            chain = [messages[j][b] for b in range(heads)]
+            for i in range(1, group):
+                for b in range(heads):
+                    chain_ref[i - 1, b] = chain[b]
+                later = messages[j ^ i]
+                chain = [
+                    followed((later[b, :, 0:DV], later[b, :, DV:]), chain[b]) for b in range(heads)
+                ]
+            for b in range(heads):
+                chain_ref[group - 1, b] = chain[b]
+                leaving_ref[b] = chain[b][:, :DV]
 
 
 def enter_kernel(group, onward, entering_ref, chain_ref, *refs):
@@ -525,12 +535,19 @@
         own_ref, high_ref, low_ref = reads[3 * n : 3 * n + 3]
         p = place ^ slot_partner(group, s)
         for b in range(2):
-            product = dot_split((high_ref[at, b], low_ref[at, b]), split(entering[n][b]))
-            held[n, :, b * DV : (b + 1) * DV] = own_ref[at, b] + product
-        copies.append(
-            pltpu.make_async_copy(held.at[n], out_ref.at[:, lanes(p * 2 * DV, 2 * DV)], sems.at[n])
-        )
-        copies[-1].start()
+            state = jnp.concatenate(split(entering[n][b]), axis=1)
+            product = jnp.dot(
+                jnp.concatenate([high_ref[at, b], low_ref[at, b]], axis=1),
+                jnp.concatenate([state, state], axis=0),
+                preferred_element_type=f32,
+            )
+            held[n, b] = own_ref[at, b] + (product[:, :DV] + product[:, DV:])
+            copies.append(
+                pltpu.make_async_copy(
+                    held.at[n, b], out_ref.at[:, lanes((p * 2 + b) * DV, DV)], sems.at[n, b]
+                )
+            )
+            copies[-1].start()
     for copy in copies:
         copy.wait()
 
@@ -583,8 +600,11 @@
         + [full(x.shape) for x in taps],
         out_specs=[whole()] * 5,
         out_shape=[shape(head_count // 2, 2 * heads, tokens)] * 2
-        + [shape(EDGE, width, dtype=bf16), shape(EDGE + 8, width), shape(heads, tokens)],
-        scratch_shapes=[VMEM((head_count, 2 * heads, tokens), f32)],
+        + [shape(HELD * width // DK, DK), shape(EDGE + 8, width), shape(heads, tokens)],
+        scratch_shapes=[
+            VMEM((head_count, 2 * heads, tokens), f32),
+            VMEM((HELD * width // DK, DK), f32),
+        ],
         compiler_params=params(),
         name="logits",
     )(
@@ -612,7 +632,7 @@
             pltpu.SemaphoreType.DMA((count, 2)),
         ]
 
-    def mix(slots):
+    def mix(slots, edge):
         count = len(slots)
         return pl.pallas_call(
             functools.partial(mix_kernel, slots, group, key_width),
@@ -643,7 +663,7 @@
                 shape(count, BLOCK, DK),
             ]
             + gate_shapes * first,
-            scratch_shapes=[VMEM((3, EDGE + 8, DK), f32)],
+            scratch_shapes=[VMEM((3, EDGE + 8, DK), f32), VMEM(before.shape, f32)],
             compiler_params=params(),
             name="solve",
         )(*known, unit_keys, key_dots, mixed, before, edge, pick)
@@ -656,7 +676,7 @@
             out_specs=[whole()] * 3,
             out_shape=[shape(count, 2, tokens, DV)]
             + [shape(count, 2, tokens, DK, dtype=bf16)] * 2,
-            scratch_shapes=[VMEM((tokens + 8, DK), f32)],
+            scratch_shapes=[VMEM((tokens + 8, DK), f32), VMEM(before.shape, f32)],
             compiler_params=params(),
             cost_estimate=pl.CostEstimate(
                 flops=2_000_000_000 * count, bytes_accessed=2_000_000 * count, transcendentals=0
@@ -665,12 +685,15 @@
         )(query_in, before, edge, unit_keys, first_keys, *known, solved, starts)
 
     calls = solve_calls(group)
-    mixed = mix(sum(calls, ()))
+    mixed = mix(sum(calls[:-1], ()), edge)
     messages, rest, start = [], [], 0
     known = [scales, *logits]
     for slots in calls:
-        results = solve(slots, start, known, not start, *mixed)
-        if not start:
+        if slots == calls[-1]:
+            known, late = lax.optimization_barrier((known, edge))
+            mixed, start = mix(slots, late), 0
+        results = solve(slots, start, known, not messages, *mixed)
+        if not messages:
             *results, rows, columns = results
             known = [rows, columns]
         results, known = lax.optimization_barrier((results, known))
@@ -690,15 +713,14 @@
     arrived, reads = lax.optimization_barrier((arrived, reads))
     chain, leaving = pl.pallas_call(
         functools.partial(prefix_kernel, group),
-        in_specs=[whole(pl.ANY)] * group,
+        in_specs=[whole()] * group,
         out_specs=[whole()] * 2,
         out_shape=[shape(group, 2, DK, 2 * DK), shape(2, DK, DV)],
-        scratch_shapes=[VMEM((group, 2, DK, 2 * DK), f32), pltpu.SemaphoreType.DMA((group,))],
         compiler_params=params(),
         name="prefix",
     )(*arrived)
     leaving, rest = lax.optimization_barrier((leaving, rest))
-    starts = [sum(len(c) for c in calls[:k]) for k in range(len(calls))]
+    starts = [sum(len(c) for c in calls[:k]) for k in range(len(calls) - 1)] + [0]
     def enter(received, onward):
         return pl.pallas_call(
             functools.partial(enter_kernel, group, onward),
@@ -736,8 +758,8 @@
             out_specs=whole(pl.ANY),
             out_shape=shape(tokens, value_width),
             scratch_shapes=[
-                VMEM((len(slots), tokens, 2 * DV), f32),
-                pltpu.SemaphoreType.DMA((len(slots),)),
+                VMEM((len(slots), 2, tokens, DV), f32),
+                pltpu.SemaphoreType.DMA((len(slots), 2)),
             ],
             input_output_aliases={len(operands): 0} if written else {},
             compiler_params=params(),

time: 48.1 us -> 47.2 us (0.981)
  waiting for transfers between devices: 7.97 us -> 6.36 us
  Pallas kernels: 25.2 us -> 25.9 us
    ppermute x3, waiting for transfers between devices: 2.62 us -> 0.89 us  [per_device(): lax.ppermute(messages[s], 'seq', [(i, i ^ d) for i in range(seq)])]
    pallas_call x1 -> x2, Pallas kernels: 3.92 us -> 4.83 us  [mix(): pl.pallas_call(functools.partial(mix_kernel, slots, group, key_width), in...]
  transfers between devices with their start and end apart: 10 -> 10, of which waited for: 6 -> 6; matrix products, arithmetic and copies ran while one was open for 0% -> 0% of each run, Pallas kernels for 37% -> 39%
where the time goes in v6:
time: 47.2 us; the launch traced here: 47 us
  Pallas kernels  25.9 us (55%)
  starting transfers between devices  14.5 us (31%)
  waiting for transfers between devices  6.36 us (13%)
    pallas_call x3, Pallas kernels, solve(): pl.pallas_call(functools.partial(solve_kernel, slots, start, group, key_w...  11.4 us
    pallas_call x2, Pallas kernels, mix(): pl.pallas_call(functools.partial(mix_kernel, slots, group, key_width), in...  4.83 us
    pallas_call x3, Pallas kernels, query(): pl.pallas_call(functools.partial(query_kernel, slots, start, group), in_s...  4.47 us
    ppermute x3, starting transfers between devices, per_device(): lax.ppermute(messages[s], 'seq', [(i, i ^ d) for i in range(seq)])  3.63 us
    ppermute x3, starting transfers between devices, per_device(): lax.ppermute(entering[d], 'seq', [(i, i ^ d) for i in range(seq)])  3.55 us
    ppermute x1, waiting for transfers between devices, per_device(): lax.ppermute(leaving, 'seq', [(i, (i + group) % seq) for i in range(seq)])  2.85 us
    ppermute x1, starting transfers between devices, per_device(): lax.ppermute(leaving, 'seq', [(i, (i + group) % seq) for i in range(seq)])  2.66 us
    pallas_call x2, Pallas kernels, outputs(): pl.pallas_call(functools.partial(output_kernel, group, [(s, where[s][1])...  2.61 us
  transfers between devices with their start and end apart: 10, of which 6 were waited for; matrix products, arithmetic and copies ran while one was open for 0% of the time, Pallas kernels for 39%

profile of v6, /device:TPU:0, one launch (start us, length us, event | category | flops | bytes accessed | tf_op | source)
XLA Modules:
  0.0 47.0 jit_solution(2128539295202592475)
XLA Ops:
  0.0 1.5 %logits.1 = (f32[2,16,512]{2,1,0:T(8,128)S(1)}, f32[2,16,512]{2,1,0:T(8,128)S(1)}, f32[64,128]{1,0:T(8,128)S(1)}, f32[24,2048]{1,0:T(8,128)S(1)}, f32[8,512]{1,0:T(8,128)S(1)}) custom-call(f32[1,8]{1,0:T(1,128)} %bitcast.6, f32[1,8]{1,0:T(1,128)} %bitcast.7, bf16[512,512]{1,0:T(8,128)(2,1)} %hidden_ref.1, bf16[64,512]{1,0:T(8,128)(2,1)} %bitcast.5, ...), custom_call_target="tpu_custom_call" | custom-call | tf_op jit(solution)/shard_map/logits/pallas_call | solution.py:594
  1.5 0.0 copy-start
  1.5 0.5 %collective-permute-start = (f32[2,16,512]{2,1,0:T(8,128)S(1)}, f32[2,16,512]{2,1,0:T(8,128)S(1)}, u32[]{:S(2)}, u32[]{:S(2)}) collective-permute-start(f32[2,16,512]{2,1,0:T(8,128)S(1)} %get-tuple-element.95), channel_id=1, source_target_pairs={{0,1},{1,0},{2,3},{3,2},{4,5},{5,4},{6,7},{7,6},{8,9},{9,8},{10,11... | collective-permute-start | bytes 196616 | tf_op jit(solution)/shard_map/ppermute | solution.py:615
  2.0 2.6 %collective-permute-start.2 = (f32[64,128]{1,0:T(8,128)S(1)}, f32[64,128]{1,0:T(8,128)S(1)}, u32[]{:S(2)}, u32[]{:S(2)}) collective-permute-start(f32[64,128]{1,0:T(8,128)S(1)} %get-tuple-element.100), channel_id=1, source_target_pairs={{0,4},{4,8},{8,12},{12,16},{16,20},{20,24},{24,28},{28,0},{1,5},{5... | collective-permute-start | bytes 98312 | tf_op jit(solution)/shard_map/ppermute | solution.py:620
  4.6 1.6 %collective-permute-start.1 = (f32[16,512]{1,0:T(8,128)S(1)}, f32[16,512]{1,0:T(8,128)S(1)}, u32[]{:S(2)}, u32[]{:S(2)}) collective-permute-start(f32[16,512]{1,0:T(8,128)S(1)} %fusion), channel_id=1, source_target_pairs={{0,2},{1,3},{2,0},{3,1},{4,6},{5,7},{6,4},{7,5},{8,10},{9,11},{10,... | collective-permute-start | bytes 98312 | tf_op jit(solution)/shard_map/ppermute | solution.py:617
  6.2 3.2 %mix.2 = (f32[3,512,128]{2,1,0:T(8,128)S(1)}, f32[3,3,128,128]{3,2,1,0:T(8,128)S(1)}, f32[3,512,256]{2,1,0:T(8,128)S(1)}) custom-call(f32[24,2048]{1,0:T(8,128)S(1)} %get-tuple-element.112.edge_ref.refs_8_.refs_6_, bf16[512,512]{1,0:T(8,128)(2,1)} %k_ref.3, bf16[512,1024]{1,0:T(8,128)(2,1)} %v_ref.3), custom_call_target="tpu_custom_call" | custom-call | tf_op jit(solution)/shard_map/mix/pallas_call | solution.py:637
  9.3 0.3 collective-permute-done.2.refs_7_.refs_5_.before_ref
  9.6 0.0 collective-permute-done.1.refs_3_
  9.6 3.5 %solve.3 = (f32[2,128,256]{2,1,0:T(8,128)S(1)}, f32[1,2,512,256]{3,2,1,0:T(8,128)S(1)}, f32[1,2,3,128,256]{4,3,2,1,0:T(8,128)S(1)}, f32[1,128,128]{2,1,0:T(8,128...) custom-call(f32[8,512]{1,0:T(8,128)S(1)} %get-tuple-element.93.refs_0_, ...), custom_call_target="tpu_custom_call" | custom-call | tf_op jit(solution)/shard_map/solve/pallas_call | solution.py:653
  13.1 2.4 %collective-permute-start.5 = (f32[2,128,256]{2,1,0:T(8,128)S(1)}, f32[2,128,256]{2,1,0:T(8,128)S(1)}, u32[]{:S(2)}, u32[]{:S(2)}) collective-permute-start(f32[2,128,256]{2,1,0:T(8,128)S(1)} %get-tuple-element.123), channel_id=1, source_target_pairs={{0,12},{4,8},{8,4},{12,0},{16,28},{20,24},{24,20},{28,16},{1,13},{... | collective-permute-start | bytes 786440 | tf_op jit(solution)/shard_map/ppermute | solution.py:708
  15.5 4.9 %solve.4 = (f32[2,128,256]{2,1,0:T(8,128)S(1)}, f32[2,128,256]{2,1,0:T(8,128)S(1)}, f32[2,2,512,256]{3,2,1,0:T(8,128)S(1)}, f32[2,2,3,128,256]{4,3,2,1,0:T(8,128)S(1)}, f32[2,128,128]{2,1,0:T(8,128)S(1)}) custom-call(f32[4,16,128]{2,1,0:T(8,128)S(1)} %get-tuple-element.129.refs_0_.rows_ref, f32[4,128,32]{2,1,0:T(8,128)S(1)} %get-tuple-element.130.refs_1_.columns_ref, ...), custom_call_target="tpu_custom_call" | custom-call | tf_op jit(solution)/shard_map/solve/pallas_call | solution.py:653
  20.3 0.0 copy-start.1
  20.3 0.6 %collective-permute-start.3 = (f32[2,128,256]{2,1,0:T(8,128)S(1)}, f32[2,128,256]{2,1,0:T(8,128)S(1)}, u32[]{:S(2)}, u32[]{:S(2)}) collective-permute-start(f32[2,128,256]{2,1,0:T(8,128)S(1)} %get-tuple-element.121), channel_id=1, source_target_pairs={{0,4},{4,0},{8,12},{12,8},{16,20},{20,16},{24,28},{28,24},{1,5},{5... | collective-permute-start | bytes 786440 | tf_op jit(solution)/shard_map/ppermute | solution.py:708
  20.9 0.7 %collective-permute-start.4 = (f32[2,128,256]{2,1,0:T(8,128)S(1)}, f32[2,128,256]{2,1,0:T(8,128)S(1)}, u32[]{:S(2)}, u32[]{:S(2)}) collective-permute-start(f32[2,128,256]{2,1,0:T(8,128)S(1)} %get-tuple-element.122), channel_id=1, source_target_pairs={{0,8},{4,12},{8,0},{12,4},{16,24},{20,28},{24,16},{28,20},{1,9},{5... | collective-permute-start | bytes 786440 | tf_op jit(solution)/shard_map/ppermute | solution.py:708
  21.6 1.7 %mix.3 = (f32[1,512,128]{2,1,0:T(8,128)S(1)}, f32[1,3,128,128]{3,2,1,0:T(8,128)S(1)}, f32[1,512,256]{2,1,0:T(8,128)S(1)}) custom-call(f32[24,2048]{1,0:T(8,128)S(1)} %get-tuple-element.112.edge_ref.refs_8_.refs_6_, bf16[512,512]{1,0:T(8,128)(2,1)} %k_ref.3, bf16[512,1024]{1,0:T(8,128)(2,1)} %v_ref.3), custom_call_target="tpu_custom_call" | custom-call | tf_op jit(solution)/shard_map/mix/pallas_call | solution.py:637
  23.3 3.1 %solve.5 = (f32[2,128,256]{2,1,0:T(8,128)S(1)}, f32[1,2,512,256]{3,2,1,0:T(8,128)S(1)}, f32[1,2,3,128,256]{4,3,2,1,0:T(8,128)S(1)}, f32[1,128,128]{2,1,0:T(8,128)S(1)}) custom-call(f32[4,16,128]{2,1,0:T(8,128)S(1)} %get-tuple-element.129.refs_0_.rows_ref, f32[4,128,32]{2,1,0:T(8,128)S(1)} %get-tuple-element.130.refs_1_.columns_ref, ...), custom_call_target="tpu_custom_call" | custom-call | tf_op jit(solution)/shard_map/solve/pallas_call | solution.py:653
  26.4 1.2 %query.3 = (f32[1,2,512,128]{3,2,1,0:T(8,128)S(1)}, bf16[1,2,512,128]{3,2,1,0:T(8,128)(2,1)S(1)}, bf16[1,2,512,128]{3,2,1,0:T(8,128)(2,1)S(1)}) custom-call(bf16[512,512]{1,0:T(8,128)(2,1)S(1)} %copy-done.1, f32[64,128]{1,0:T(8,128)S(1)} %collective-permute-done.2.refs_7_.refs_5_.before_ref, f32[24,2048]{1,0:T(8,128)S(1)} %get-tuple-element.112.edge_ref.refs_8_.refs_6_, ...), custom_call_target="tpu_custom_call" | custom-call | flops 2000000000 | bytes 2000000 | tf_op jit(solution)/shard_map/query/pallas_call | solution.py:673
  27.5 0.7 %collective-permute-done.3.refs_1_ = f32[2,128,256]{2,1,0:T(8,128)S(1)} collective-permute-done((f32[2,128,256]{2,1,0:T(8,128)S(1)}, f32[2,128,256]{2,1,0:T(8,128)S(1)}, u32[]{:S(2)}, u32[]{:S(2)}) %collective-permute-start.3) | collective-permute-done | bytes 262176 | tf_op jit(solution)/shard_map/ppermute | solution.py:708
  28.2 0.2 collective-permute-done.4.refs_2_
  28.4 0.7 %prefix.1 = (f32[4,2,128,256]{3,2,1,0:T(8,128)S(1)}, f32[2,128,128]{2,1,0:T(8,128)S(1)}) custom-call(f32[2,128,256]{2,1,0:T(8,128)S(1)} %get-tuple-element.136.refs_0_, f32[2,128,256]{2,1,0:T(8,128)S(1)} %collective-permute-done.3.refs_1_, f32[2,128,256]{2,1,0:T(8,128)S(1)} %collective-permute-done.4.refs_2_, f32[2,128,256]{2,1,0:T(8,128)S(1)} %collective-permute-done.5.refs_3_), custom_call_target="tpu_custom_call" | custom-call | tf_op jit(solution)/shard_map/prefix/pallas_call | solution.py:714
  29.1 2.7 %collective-permute-start.6 = (f32[2,128,128]{2,1,0:T(8,128)S(1)}, f32[2,128,128]{2,1,0:T(8,128)S(1)}, u32[]{:S(2)}, u32[]{:S(2)}) collective-permute-start(f32[2,128,128]{2,1,0:T(8,128)S(1)} %get-tuple-element.147), channel_id=1, source_target_pairs={{0,16},{4,20},{8,24},{12,28},{16,0},{20,4},{24,8},{28,12},{1,17},{... | collective-permute-start | bytes 393224 | tf_op jit(solution)/shard_map/ppermute | solution.py:738
  31.8 2.2 %query.4 = (f32[2,2,512,128]{3,2,1,0:T(8,128)S(1)}, bf16[2,2,512,128]{3,2,1,0:T(8,128)(2,1)S(1)}, bf16[2,2,512,128]{3,2,1,0:T(8,128)(2,1)S(1)}) custom-call(bf16[512,512]{1,0:T(8,128)(2,1)S(1)} %copy-done.1, f32[64,128]{1,0:T(8,128)S(1)} %collective-permute-done.2.refs_7_.refs_5_.before_ref, f32[24,2048]{1,0:T(8,128)S(1)} %get-tuple-element.112.edge_ref.refs_8_.refs_6_, ...), custom_call_target="tpu_custom_call" | custom-call | flops 4000000000 | bytes 4000000 | tf_op jit(solution)/shard_map/query/pallas_call | solution.py:673
  34.0 2.8 %collective-permute-done.6.entering_ref = f32[2,128,128]{2,1,0:T(8,128)S(1)} collective-permute-done((f32[2,128,128]{2,1,0:T(8,128)S(1)}, f32[2,128,128]{2,1,0:T(8,128)S(1)}, u32[]{:S(2)}, u32[]{:S(2)}) %collective-permute-start.6) | collective-permute-done | bytes 131104 | tf_op jit(solution)/shard_map/ppermute | solution.py:738
  36.8 0.4 enter.1
  37.2 1.4 %collective-permute-start.7 = (f32[2,128,128]{2,1,0:T(8,128)S(1)}, f32[2,128,128]{2,1,0:T(8,128)S(1)}, u32[]{:S(2)}, u32[]{:S(2)}) collective-permute-start(f32[2,128,128]{2,1,0:T(8,128)S(1)} %get-tuple-element.170), channel_id=1, source_target_pairs={{0,12},{4,8},{8,4},{12,0},{16,28},{20,24},{24,20},{28,16},{1,13},{... | collective-permute-start | bytes 393224 | tf_op jit(solution)/shard_map/ppermute | solution.py:748
  38.6 0.6 %collective-permute-start.8 = (f32[2,128,128]{2,1,0:T(8,128)S(1)}, f32[2,128,128]{2,1,0:T(8,128)S(1)}, u32[]{:S(2)}, u32[]{:S(2)}) collective-permute-start(f32[2,128,128]{2,1,0:T(8,128)S(1)} %get-tuple-element.171), channel_id=1, source_target_pairs={{0,4},{4,0},{8,12},{12,8},{16,20},{20,16},{24,28},{28,24},{1,5},{5... | collective-permute-start | bytes 393224 | tf_op jit(solution)/shard_map/ppermute | solution.py:748
  39.2 1.5 %collective-permute-start.9 = (f32[2,128,128]{2,1,0:T(8,128)S(1)}, f32[2,128,128]{2,1,0:T(8,128)S(1)}, u32[]{:S(2)}, u32[]{:S(2)}) collective-permute-start(f32[2,128,128]{2,1,0:T(8,128)S(1)} %get-tuple-element.172), channel_id=1, source_target_pairs={{0,8},{4,12},{8,0},{12,4},{16,24},{20,28},{24,16},{28,20},{1,9},{5... | collective-permute-start | bytes 393224 | tf_op jit(solution)/shard_map/ppermute | solution.py:748
  40.8 1.1 %query.5 = (f32[1,2,512,128]{3,2,1,0:T(8,128)S(1)}, bf16[1,2,512,128]{3,2,1,0:T(8,128)(2,1)S(1)}, bf16[1,2,512,128]{3,2,1,0:T(8,128)(2,1)S(1)}) custom-call(bf16[512,512]{1,0:T(8,128)(2,1)S(1)} %copy-done.1, f32[64,128]{1,0:T(8,128)S(1)} %collective-permute-done.2.refs_7_.refs_5_.before_ref, f32[24,2048]{1,0:T(8,128)S(1)} %get-tuple-element.112.edge_ref.refs_8_.refs_6_, ...), custom_call_target="tpu_custom_call" | custom-call | flops 2000000000 | bytes 2000000 | tf_op jit(solution)/shard_map/query/pallas_call | solution.py:673
  41.9 1.1 %outputs.2.refs_12_ = f32[512,1024]{1,0:T(8,128)} custom-call(f32[1,2,512,128]{3,2,1,0:T(8,128)S(1)} %get-tuple-element.177.refs_0_, bf16[1,2,512,128]{3,2,1,0:T(8,128)(2,1)S(1)} %get-tuple-element.178.refs_1_, bf16[1,2,512,128]{3,2,1,0:T(8,128)(2,1)S(1)} %get-tuple-element.179.refs_2_, f32[2,128,128]{2,1,0:T(8,128)S(1)} %get-tuple-element.180.refs_3_), custom_call_target="tpu_custom_call" | custom-call | tf_op jit(solution)/shard_map/outputs/pallas_call | solution.py:755
  43.0 1.5 %collective-permute-done.7.refs_9_ = f32[2,128,128]{2,1,0:T(8,128)S(1)} collective-permute-done((f32[2,128,128]{2,1,0:T(8,128)S(1)}, f32[2,128,128]{2,1,0:T(8,128)S(1)}, u32[]{:S(2)}, u32[]{:S(2)}) %collective-permute-start.7) | collective-permute-done | bytes 131104 | tf_op jit(solution)/shard_map/ppermute | solution.py:748
  44.5 0.8 %collective-permute-done.8.refs_10_ = f32[2,128,128]{2,1,0:T(8,128)S(1)} collective-permute-done((f32[2,128,128]{2,1,0:T(8,128)S(1)}, f32[2,128,128]{2,1,0:T(8,128)S(1)}, u32[]{:S(2)}, u32[]{:S(2)}) %collective-permute-start.8) | collective-permute-done | bytes 131104 | tf_op jit(solution)/shard_map/ppermute | solution.py:748
  45.4 1.5 %outputs.3 = f32[512,1024]{1,0:T(8,128)} custom-call(f32[1,2,512,128]{3,2,1,0:T(8,128)S(1)} %get-tuple-element.162.refs_0_, bf16[1,2,512,128]{3,2,1,0:T(8,128)(2,1)S(1)} %get-tuple-element.163.refs_1_, bf16[1,2,512,128]{3,2,1,0:T(8,128)(2,1)S(1)} %get-tuple-element.164.refs_2_, ...), custom_call_target="tpu_custom_call", output_to_operand_aliasing={{}: (12, {})} | custom-call | tf_op jit(solution)/shard_map/outputs/pallas_call | solution.py:755
  (6 shorter events, 0.0 us)
Async XLA Ops:
  1.5 8.1 %copy-start = (bf16[256,1920]{1,0:T(8,128)(2,1)S(1)}, bf16[256,1920]{1,0:T(8,128)(2,1)}, u32[]{:S(2)}) copy-start(bf16[256,1920]{1,0:T(8,128)(2,1)} %constant.2.clone.refs_9_.refs_7_) | copy-start | bytes 2949124
  1.5 3.1 %collective-permute-start = (f32[2,16,512]{2,1,0:T(8,128)S(1)}, f32[2,16,512]{2,1,0:T(8,128)S(1)}, u32[]{:S(2)}, u32[]{:S(2)}) collective-permute-start(f32[2,16,512]{2,1,0:T(8,128)S(1)} %get-tuple-element.95), channel_id=1, source_target_pairs={{0,1},{1,0},{2,3},{3,2},{4,5},{5,4},{6,7},{7,6},{8,9},{9,8},{10,11... | collective-permute-start | bytes 196616 | tf_op jit(solution)/shard_map/ppermute | solution.py:615
  2.0 7.6 %collective-permute-start.2 = (f32[64,128]{1,0:T(8,128)S(1)}, f32[64,128]{1,0:T(8,128)S(1)}, u32[]{:S(2)}, u32[]{:S(2)}) collective-permute-start(f32[64,128]{1,0:T(8,128)S(1)} %get-tuple-element.100), channel_id=1, source_target_pairs={{0,4},{4,8},{8,12},{12,16},{16,20},{20,24},{24,28},{28,0},{1,5},{5... | collective-permute-start | bytes 98312 | tf_op jit(solution)/shard_map/ppermute | solution.py:620
  4.6 5.0 %collective-permute-start.1 = (f32[16,512]{1,0:T(8,128)S(1)}, f32[16,512]{1,0:T(8,128)S(1)}, u32[]{:S(2)}, u32[]{:S(2)}) collective-permute-start(f32[16,512]{1,0:T(8,128)S(1)} %fusion), channel_id=1, source_target_pairs={{0,2},{1,3},{2,0},{3,1},{4,6},{5,7},{6,4},{7,5},{8,10},{9,11},{10,... | collective-permute-start | bytes 98312 | tf_op jit(solution)/shard_map/ppermute | solution.py:617
  13.1 14.5 %collective-permute-start.5 = (f32[2,128,256]{2,1,0:T(8,128)S(1)}, f32[2,128,256]{2,1,0:T(8,128)S(1)}, u32[]{:S(2)}, u32[]{:S(2)}) collective-permute-start(f32[2,128,256]{2,1,0:T(8,128)S(1)} %get-tuple-element.123), channel_id=1, source_target_pairs={{0,12},{4,8},{8,4},{12,0},{16,28},{20,24},{24,20},{28,16},{1,13},{... | collective-permute-start | bytes 786440 | tf_op jit(solution)/shard_map/ppermute | solution.py:708
  20.3 6.0 %copy-start.1 = (bf16[512,512]{1,0:T(8,128)(2,1)S(1)}, bf16[512,512]{1,0:T(8,128)(2,1)}, u32[]{:S(2)}) copy-start(bf16[512,512]{1,0:T(8,128)(2,1)} %q_ref.5) | copy-start | bytes 1572868
  20.3 7.9 %collective-permute-start.3 = (f32[2,128,256]{2,1,0:T(8,128)S(1)}, f32[2,128,256]{2,1,0:T(8,128)S(1)}, u32[]{:S(2)}, u32[]{:S(2)}) collective-permute-start(f32[2,128,256]{2,1,0:T(8,128)S(1)} %get-tuple-element.121), channel_id=1, source_target_pairs={{0,4},{4,0},{8,12},{12,8},{16,20},{20,16},{24,28},{28,24},{1,5},{5... | collective-permute-start | bytes 786440 | tf_op jit(solution)/shard_map/ppermute | solution.py:708
  20.9 7.5 %collective-permute-start.4 = (f32[2,128,256]{2,1,0:T(8,128)S(1)}, f32[2,128,256]{2,1,0:T(8,128)S(1)}, u32[]{:S(2)}, u32[]{:S(2)}) collective-permute-start(f32[2,128,256]{2,1,0:T(8,128)S(1)} %get-tuple-element.122), channel_id=1, source_target_pairs={{0,8},{4,12},{8,0},{12,4},{16,24},{20,28},{24,16},{28,20},{1,9},{5... | collective-permute-start | bytes 786440 | tf_op jit(solution)/shard_map/ppermute | solution.py:708
  29.1 7.7 %collective-permute-start.6 = (f32[2,128,128]{2,1,0:T(8,128)S(1)}, f32[2,128,128]{2,1,0:T(8,128)S(1)}, u32[]{:S(2)}, u32[]{:S(2)}) collective-permute-start(f32[2,128,128]{2,1,0:T(8,128)S(1)} %get-tuple-element.147), channel_id=1, source_target_pairs={{0,16},{4,20},{8,24},{12,28},{16,0},{20,4},{24,8},{28,12},{1,17},{... | collective-permute-start | bytes 393224 | tf_op jit(solution)/shard_map/ppermute | solution.py:738
  37.2 7.3 %collective-permute-start.7 = (f32[2,128,128]{2,1,0:T(8,128)S(1)}, f32[2,128,128]{2,1,0:T(8,128)S(1)}, u32[]{:S(2)}, u32[]{:S(2)}) collective-permute-start(f32[2,128,128]{2,1,0:T(8,128)S(1)} %get-tuple-element.170), channel_id=1, source_target_pairs={{0,12},{4,8},{8,4},{12,0},{16,28},{20,24},{24,20},{28,16},{1,13},{... | collective-permute-start | bytes 393224 | tf_op jit(solution)/shard_map/ppermute | solution.py:748
  38.6 6.8 %collective-permute-start.8 = (f32[2,128,128]{2,1,0:T(8,128)S(1)}, f32[2,128,128]{2,1,0:T(8,128)S(1)}, u32[]{:S(2)}, u32[]{:S(2)}) collective-permute-start(f32[2,128,128]{2,1,0:T(8,128)S(1)} %get-tuple-element.171), channel_id=1, source_target_pairs={{0,4},{4,0},{8,12},{12,8},{16,20},{20,16},{24,28},{28,24},{1,5},{5... | collective-permute-start | bytes 393224 | tf_op jit(solution)/shard_map/ppermute | solution.py:748
  39.2 6.2 %collective-permute-start.9 = (f32[2,128,128]{2,1,0:T(8,128)S(1)}, f32[2,128,128]{2,1,0:T(8,128)S(1)}, u32[]{:S(2)}, u32[]{:S(2)}) collective-permute-start(f32[2,128,128]{2,1,0:T(8,128)S(1)} %get-tuple-element.172), channel_id=1, source_target_pairs={{0,8},{4,12},{8,0},{12,4},{16,24},{20,28},{24,16},{28,20},{1,9},{5... | collective-permute-start | bytes 393224 | tf_op jit(solution)/shard_map/ppermute | solution.py:748

commit v7 on v6

--- a/solution.py
+++ b/solution.py
@@ -709,8 +709,7 @@
         )
 
     messages[-1], rest[0] = lax.optimization_barrier((messages[-1], rest[0]))
-    reads = [query(calls[0], 0, *rest[0])]
-    arrived, reads = lax.optimization_barrier((arrived, reads))
+    reads = []
     chain, leaving = pl.pallas_call(
         functools.partial(prefix_kernel, group),
         in_specs=[whole()] * group,
@@ -737,7 +736,7 @@
     for hop in range(hops):
         received = lax.ppermute(leaving, "seq", [(i, (i + group) % seq) for i in range(seq)])
         if hop == 0:
-            reads += [query(*x, *outs) for *x, outs in zip(calls[1:-1], starts[1:-1], rest[1:-1])]
+            reads += [query(*x, *outs) for *x, outs in zip(calls[:-1], starts[:-1], rest[:-1])]
             received, reads, rest = lax.optimization_barrier((received, reads, rest))
         entering = enter(received, hop < hops - 1)
         if hop < hops - 1:

time: 47.2 us -> 47.2 us (level)
    ppermute x1, waiting for transfers between devices: 2.85 us -> 1.68 us  [per_device(): lax.ppermute(leaving, 'seq', [(i, (i + group) % seq) for i in range(seq)])]
    ppermute x3, waiting for transfers between devices: 0.89 us -> 2.05 us  [per_device(): lax.ppermute(messages[s], 'seq', [(i, i ^ d) for i in range(seq)])]
where the time goes in v7:
time: 47.2 us; the launch traced here: 47 us
  Pallas kernels  25.9 us (55%)
  starting transfers between devices  14.5 us (31%)
  waiting for transfers between devices  6.35 us (13%)
    pallas_call x3, Pallas kernels, solve(): pl.pallas_call(functools.partial(solve_kernel, slots, start, group, key_w...  11.4 us
    pallas_call x2, Pallas kernels, mix(): pl.pallas_call(functools.partial(mix_kernel, slots, group, key_width), in...  4.83 us
    pallas_call x3, Pallas kernels, query(): pl.pallas_call(functools.partial(query_kernel, slots, start, group), in_s...  4.46 us
    ppermute x3, starting transfers between devices, per_device(): lax.ppermute(messages[s], 'seq', [(i, i ^ d) for i in range(seq)])  3.63 us
    ppermute x3, starting transfers between devices, per_device(): lax.ppermute(entering[d], 'seq', [(i, i ^ d) for i in range(seq)])  3.55 us
    ppermute x1, starting transfers between devices, per_device(): lax.ppermute(leaving, 'seq', [(i, (i + group) % seq) for i in range(seq)])  2.66 us
    pallas_call x2, Pallas kernels, outputs(): pl.pallas_call(functools.partial(output_kernel, group, [(s, where[s][1])...  2.61 us
    ppermute x1, starting transfers between devices, per_device(): before = lax.ppermute(tail, 'seq', [(i, (i + 1) % seq) for i in range(seq)])  2.55 us
  transfers between devices with their start and end apart: 10, of which 6 were waited for; matrix products, arithmetic and copies ran while one was open for 0% of the time, Pallas kernels for 39%

profile of v7, /device:TPU:0, one launch (start us, length us, event | category | flops | bytes accessed | tf_op | source)
XLA Modules:
  0.0 47.0 jit_solution(17729492420860224260)
XLA Ops:
  0.0 1.5 %logits.1 = (f32[2,16,512]{2,1,0:T(8,128)S(1)}, f32[2,16,512]{2,1,0:T(8,128)S(1)}, f32[64,128]{1,0:T(8,128)S(1)}, f32[24,2048]{1,0:T(8,128)S(1)}, f32[8,512]{1,0:T(8,128)S(1)}) custom-call(f32[1,8]{1,0:T(1,128)} %bitcast.6, f32[1,8]{1,0:T(1,128)} %bitcast.7, bf16[512,512]{1,0:T(8,128)(2,1)} %hidden_ref.1, bf16[64,512]{1,0:T(8,128)(2,1)} %bitcast.5, ...), custom_call_target="tpu_custom_call" | custom-call | tf_op jit(solution)/shard_map/logits/pallas_call | solution.py:594
  1.5 0.0 copy-start
  1.5 0.5 %collective-permute-start = (f32[2,16,512]{2,1,0:T(8,128)S(1)}, f32[2,16,512]{2,1,0:T(8,128)S(1)}, u32[]{:S(2)}, u32[]{:S(2)}) collective-permute-start(f32[2,16,512]{2,1,0:T(8,128)S(1)} %get-tuple-element.92), channel_id=1, source_target_pairs={{0,1},{1,0},{2,3},{3,2},{4,5},{5,4},{6,7},{7,6},{8,9},{9,8},{10,11... | collective-permute-start | bytes 196616 | tf_op jit(solution)/shard_map/ppermute | solution.py:615
  2.0 2.6 %collective-permute-start.2 = (f32[64,128]{1,0:T(8,128)S(1)}, f32[64,128]{1,0:T(8,128)S(1)}, u32[]{:S(2)}, u32[]{:S(2)}) collective-permute-start(f32[64,128]{1,0:T(8,128)S(1)} %get-tuple-element.97), channel_id=1, source_target_pairs={{0,4},{4,8},{8,12},{12,16},{16,20},{20,24},{24,28},{28,0},{1,5},{5... | collective-permute-start | bytes 98312 | tf_op jit(solution)/shard_map/ppermute | solution.py:620
  4.6 0.0 collective-permute-done.refs_2_
  4.6 1.6 %collective-permute-start.1 = (f32[16,512]{1,0:T(8,128)S(1)}, f32[16,512]{1,0:T(8,128)S(1)}, u32[]{:S(2)}, u32[]{:S(2)}) collective-permute-start(f32[16,512]{1,0:T(8,128)S(1)} %fusion), channel_id=1, source_target_pairs={{0,2},{1,3},{2,0},{3,1},{4,6},{5,7},{6,4},{7,5},{8,10},{9,11},{10,... | collective-permute-start | bytes 98312 | tf_op jit(solution)/shard_map/ppermute | solution.py:617
  6.2 3.2 %mix.2 = (f32[3,512,128]{2,1,0:T(8,128)S(1)}, f32[3,3,128,128]{3,2,1,0:T(8,128)S(1)}, f32[3,512,256]{2,1,0:T(8,128)S(1)}) custom-call(f32[24,2048]{1,0:T(8,128)S(1)} %get-tuple-element.109.edge_ref.refs_8_.refs_6_, bf16[512,512]{1,0:T(8,128)(2,1)} %k_ref.3, bf16[512,1024]{1,0:T(8,128)(2,1)} %v_ref.3), custom_call_target="tpu_custom_call" | custom-call | tf_op jit(solution)/shard_map/mix/pallas_call | solution.py:637
  9.3 0.3 collective-permute-done.2.refs_7_.refs_5_.before_ref
  9.6 3.5 %solve.3 = (f32[2,128,256]{2,1,0:T(8,128)S(1)}, f32[1,2,512,256]{3,2,1,0:T(8,128)S(1)}, f32[1,2,3,128,256]{4,3,2,1,0:T(8,128)S(1)}, f32[1,128,128]{2,1,0:T(8,128...) custom-call(f32[8,512]{1,0:T(8,128)S(1)} %get-tuple-element.90.refs_0_, ...), custom_call_target="tpu_custom_call" | custom-call | tf_op jit(solution)/shard_map/solve/pallas_call | solution.py:653
  13.1 2.4 %collective-permute-start.5 = (f32[2,128,256]{2,1,0:T(8,128)S(1)}, f32[2,128,256]{2,1,0:T(8,128)S(1)}, u32[]{:S(2)}, u32[]{:S(2)}) collective-permute-start(f32[2,128,256]{2,1,0:T(8,128)S(1)} %get-tuple-element.120), channel_id=1, source_target_pairs={{0,12},{4,8},{8,4},{12,0},{16,28},{20,24},{24,20},{28,16},{1,13},{... | collective-permute-start | bytes 786440 | tf_op jit(solution)/shard_map/ppermute | solution.py:708
  15.5 4.9 %solve.4 = (f32[2,128,256]{2,1,0:T(8,128)S(1)}, f32[2,128,256]{2,1,0:T(8,128)S(1)}, f32[2,2,512,256]{3,2,1,0:T(8,128)S(1)}, f32[2,2,3,128,256]{4,3,2,1,0:T(8,128)S(1)}, f32[2,128,128]{2,1,0:T(8,128)S(1)}) custom-call(f32[4,16,128]{2,1,0:T(8,128)S(1)} %get-tuple-element.138.refs_0_.rows_ref, f32[4,128,32]{2,1,0:T(8,128)S(1)} %get-tuple-element.139.refs_1_.columns_ref, ...), custom_call_target="tpu_custom_call" | custom-call | tf_op jit(solution)/shard_map/solve/pallas_call | solution.py:653
  20.3 0.6 %collective-permute-start.3 = (f32[2,128,256]{2,1,0:T(8,128)S(1)}, f32[2,128,256]{2,1,0:T(8,128)S(1)}, u32[]{:S(2)}, u32[]{:S(2)}) collective-permute-start(f32[2,128,256]{2,1,0:T(8,128)S(1)} %get-tuple-element.118), channel_id=1, source_target_pairs={{0,4},{4,0},{8,12},{12,8},{16,20},{20,16},{24,28},{28,24},{1,5},{5... | collective-permute-start | bytes 786440 | tf_op jit(solution)/shard_map/ppermute | solution.py:708
  20.9 0.7 %collective-permute-start.4 = (f32[2,128,256]{2,1,0:T(8,128)S(1)}, f32[2,128,256]{2,1,0:T(8,128)S(1)}, u32[]{:S(2)}, u32[]{:S(2)}) collective-permute-start(f32[2,128,256]{2,1,0:T(8,128)S(1)} %get-tuple-element.119), channel_id=1, source_target_pairs={{0,8},{4,12},{8,0},{12,4},{16,24},{20,28},{24,16},{28,20},{1,9},{5... | collective-permute-start | bytes 786440 | tf_op jit(solution)/shard_map/ppermute | solution.py:708
  21.6 1.7 %mix.3 = (f32[1,512,128]{2,1,0:T(8,128)S(1)}, f32[1,3,128,128]{3,2,1,0:T(8,128)S(1)}, f32[1,512,256]{2,1,0:T(8,128)S(1)}) custom-call(f32[24,2048]{1,0:T(8,128)S(1)} %get-tuple-element.109.edge_ref.refs_8_.refs_6_, bf16[512,512]{1,0:T(8,128)(2,1)} %k_ref.3, bf16[512,1024]{1,0:T(8,128)(2,1)} %v_ref.3), custom_call_target="tpu_custom_call" | custom-call | tf_op jit(solution)/shard_map/mix/pallas_call | solution.py:637
  23.2 0.0 copy-start.1
  23.3 3.1 %solve.5 = (f32[2,128,256]{2,1,0:T(8,128)S(1)}, f32[1,2,512,256]{3,2,1,0:T(8,128)S(1)}, f32[1,2,3,128,256]{4,3,2,1,0:T(8,128)S(1)}, f32[1,128,128]{2,1,0:T(8,128)S(1)}) custom-call(f32[4,16,128]{2,1,0:T(8,128)S(1)} %get-tuple-element.138.refs_0_.rows_ref, f32[4,128,32]{2,1,0:T(8,128)S(1)} %get-tuple-element.139.refs_1_.columns_ref, ...), custom_call_target="tpu_custom_call" | custom-call | tf_op jit(solution)/shard_map/solve/pallas_call | solution.py:653
  26.4 1.9 %collective-permute-done.3.refs_1_ = f32[2,128,256]{2,1,0:T(8,128)S(1)} collective-permute-done((f32[2,128,256]{2,1,0:T(8,128)S(1)}, f32[2,128,256]{2,1,0:T(8,128)S(1)}, u32[]{:S(2)}, u32[]{:S(2)}) %collective-permute-start.3) | collective-permute-done | bytes 262176 | tf_op jit(solution)/shard_map/ppermute | solution.py:708
  28.2 0.2 collective-permute-done.4.refs_2_
  28.4 0.7 %prefix.1 = (f32[4,2,128,256]{3,2,1,0:T(8,128)S(1)}, f32[2,128,128]{2,1,0:T(8,128)S(1)}) custom-call(f32[2,128,256]{2,1,0:T(8,128)S(1)} %get-tuple-element.117.refs_0_, f32[2,128,256]{2,1,0:T(8,128)S(1)} %collective-permute-done.3.refs_1_, f32[2,128,256]{2,1,0:T(8,128)S(1)} %collective-permute-done.4.refs_2_, f32[2,128,256]{2,1,0:T(8,128)S(1)} %collective-permute-done.5.refs_3_), custom_call_target="tpu_custom_call" | custom-call | tf_op jit(solution)/shard_map/prefix/pallas_call | solution.py:713
  29.1 2.7 %collective-permute-start.6 = (f32[2,128,128]{2,1,0:T(8,128)S(1)}, f32[2,128,128]{2,1,0:T(8,128)S(1)}, u32[]{:S(2)}, u32[]{:S(2)}) collective-permute-start(f32[2,128,128]{2,1,0:T(8,128)S(1)} %get-tuple-element.135), channel_id=1, source_target_pairs={{0,16},{4,20},{8,24},{12,28},{16,0},{20,4},{24,8},{28,12},{1,17},{... | collective-permute-start | bytes 393224 | tf_op jit(solution)/shard_map/ppermute | solution.py:737
  31.8 2.2 %query.4 = (f32[2,2,512,128]{3,2,1,0:T(8,128)S(1)}, bf16[2,2,512,128]{3,2,1,0:T(8,128)(2,1)S(1)}, bf16[2,2,512,128]{3,2,1,0:T(8,128)(2,1)S(1)}) custom-call(bf16[512,512]{1,0:T(8,128)(2,1)S(1)} %copy-done.1, f32[64,128]{1,0:T(8,128)S(1)} %collective-permute-done.2.refs_7_.refs_5_.before_ref, f32[24,2048]{1,0:T(8,128)S(1)} %get-tuple-element.109.edge_ref.refs_8_.refs_6_, ...), custom_call_target="tpu_custom_call" | custom-call | flops 4000000000 | bytes 4000000 | tf_op jit(solution)/shard_map/query/pallas_call | solution.py:673
  34.0 1.2 %query.3 = (f32[1,2,512,128]{3,2,1,0:T(8,128)S(1)}, bf16[1,2,512,128]{3,2,1,0:T(8,128)(2,1)S(1)}, bf16[1,2,512,128]{3,2,1,0:T(8,128)(2,1)S(1)}) custom-call(bf16[512,512]{1,0:T(8,128)(2,1)S(1)} %copy-done.1, f32[64,128]{1,0:T(8,128)S(1)} %collective-permute-done.2.refs_7_.refs_5_.before_ref, f32[24,2048]{1,0:T(8,128)S(1)} %get-tuple-element.109.edge_ref.refs_8_.refs_6_, ...), custom_call_target="tpu_custom_call" | custom-call | flops 2000000000 | bytes 2000000 | tf_op jit(solution)/shard_map/query/pallas_call | solution.py:673
  35.1 1.7 %collective-permute-done.6.entering_ref = f32[2,128,128]{2,1,0:T(8,128)S(1)} collective-permute-done((f32[2,128,128]{2,1,0:T(8,128)S(1)}, f32[2,128,128]{2,1,0:T(8,128)S(1)}, u32[]{:S(2)}, u32[]{:S(2)}) %collective-permute-start.6) | collective-permute-done | bytes 131104 | tf_op jit(solution)/shard_map/ppermute | solution.py:737
  36.8 0.4 enter.1
  37.2 1.4 %collective-permute-start.7 = (f32[2,128,128]{2,1,0:T(8,128)S(1)}, f32[2,128,128]{2,1,0:T(8,128)S(1)}, u32[]{:S(2)}, u32[]{:S(2)}) collective-permute-start(f32[2,128,128]{2,1,0:T(8,128)S(1)} %get-tuple-element.164), channel_id=1, source_target_pairs={{0,12},{4,8},{8,4},{12,0},{16,28},{20,24},{24,20},{28,16},{1,13},{... | collective-permute-start | bytes 393224 | tf_op jit(solution)/shard_map/ppermute | solution.py:747
  38.6 0.6 %collective-permute-start.8 = (f32[2,128,128]{2,1,0:T(8,128)S(1)}, f32[2,128,128]{2,1,0:T(8,128)S(1)}, u32[]{:S(2)}, u32[]{:S(2)}) collective-permute-start(f32[2,128,128]{2,1,0:T(8,128)S(1)} %get-tuple-element.165), channel_id=1, source_target_pairs={{0,4},{4,0},{8,12},{12,8},{16,20},{20,16},{24,28},{28,24},{1,5},{5... | collective-permute-start | bytes 393224 | tf_op jit(solution)/shard_map/ppermute | solution.py:747
  39.2 1.5 %collective-permute-start.9 = (f32[2,128,128]{2,1,0:T(8,128)S(1)}, f32[2,128,128]{2,1,0:T(8,128)S(1)}, u32[]{:S(2)}, u32[]{:S(2)}) collective-permute-start(f32[2,128,128]{2,1,0:T(8,128)S(1)} %get-tuple-element.166), channel_id=1, source_target_pairs={{0,8},{4,12},{8,0},{12,4},{16,24},{20,28},{24,16},{28,20},{1,9},{5... | collective-permute-start | bytes 393224 | tf_op jit(solution)/shard_map/ppermute | solution.py:747
  40.7 1.1 %query.5 = (f32[1,2,512,128]{3,2,1,0:T(8,128)S(1)}, bf16[1,2,512,128]{3,2,1,0:T(8,128)(2,1)S(1)}, bf16[1,2,512,128]{3,2,1,0:T(8,128)(2,1)S(1)}) custom-call(bf16[512,512]{1,0:T(8,128)(2,1)S(1)} %copy-done.1, f32[64,128]{1,0:T(8,128)S(1)} %collective-permute-done.2.refs_7_.refs_5_.before_ref, f32[24,2048]{1,0:T(8,128)S(1)} %get-tuple-element.109.edge_ref.refs_8_.refs_6_, ...), custom_call_target="tpu_custom_call" | custom-call | flops 2000000000 | bytes 2000000 | tf_op jit(solution)/shard_map/query/pallas_call | solution.py:673
  41.9 1.1 %outputs.2.refs_12_ = f32[512,1024]{1,0:T(8,128)} custom-call(f32[1,2,512,128]{3,2,1,0:T(8,128)S(1)} %get-tuple-element.171.refs_0_, bf16[1,2,512,128]{3,2,1,0:T(8,128)(2,1)S(1)} %get-tuple-element.172.refs_1_, bf16[1,2,512,128]{3,2,1,0:T(8,128)(2,1)S(1)} %get-tuple-element.173.refs_2_, f32[2,128,128]{2,1,0:T(8,128)S(1)} %get-tuple-element.174.refs_3_), custom_call_target="tpu_custom_call" | custom-call | tf_op jit(solution)/shard_map/outputs/pallas_call | solution.py:754
  43.0 1.5 %collective-permute-done.7.refs_9_ = f32[2,128,128]{2,1,0:T(8,128)S(1)} collective-permute-done((f32[2,128,128]{2,1,0:T(8,128)S(1)}, f32[2,128,128]{2,1,0:T(8,128)S(1)}, u32[]{:S(2)}, u32[]{:S(2)}) %collective-permute-start.7) | collective-permute-done | bytes 131104 | tf_op jit(solution)/shard_map/ppermute | solution.py:747
  44.5 0.9 %collective-permute-done.8.refs_10_ = f32[2,128,128]{2,1,0:T(8,128)S(1)} collective-permute-done((f32[2,128,128]{2,1,0:T(8,128)S(1)}, f32[2,128,128]{2,1,0:T(8,128)S(1)}, u32[]{:S(2)}, u32[]{:S(2)}) %collective-permute-start.8) | collective-permute-done | bytes 131104 | tf_op jit(solution)/shard_map/ppermute | solution.py:747
  45.3 1.5 %outputs.3 = f32[512,1024]{1,0:T(8,128)} custom-call(f32[1,2,512,128]{3,2,1,0:T(8,128)S(1)} %get-tuple-element.156.refs_0_, bf16[1,2,512,128]{3,2,1,0:T(8,128)(2,1)S(1)} %get-tuple-element.157.refs_1_, bf16[1,2,512,128]{3,2,1,0:T(8,128)(2,1)S(1)} %get-tuple-element.158.refs_2_, ...), custom_call_target="tpu_custom_call", output_to_operand_aliasing={{}: (12, {})} | custom-call | tf_op jit(solution)/shard_map/outputs/pallas_call | solution.py:754
  (6 shorter events, 0.0 us)
Async XLA Ops:
  1.5 8.1 %copy-start = (bf16[256,1920]{1,0:T(8,128)(2,1)S(1)}, bf16[256,1920]{1,0:T(8,128)(2,1)}, u32[]{:S(2)}) copy-start(bf16[256,1920]{1,0:T(8,128)(2,1)} %constant.2.clone.refs_9_.refs_7_) | copy-start | bytes 2949124
  1.5 3.1 %collective-permute-start = (f32[2,16,512]{2,1,0:T(8,128)S(1)}, f32[2,16,512]{2,1,0:T(8,128)S(1)}, u32[]{:S(2)}, u32[]{:S(2)}) collective-permute-start(f32[2,16,512]{2,1,0:T(8,128)S(1)} %get-tuple-element.92), channel_id=1, source_target_pairs={{0,1},{1,0},{2,3},{3,2},{4,5},{5,4},{6,7},{7,6},{8,9},{9,8},{10,11... | collective-permute-start | bytes 196616 | tf_op jit(solution)/shard_map/ppermute | solution.py:615
  2.0 7.6 %collective-permute-start.2 = (f32[64,128]{1,0:T(8,128)S(1)}, f32[64,128]{1,0:T(8,128)S(1)}, u32[]{:S(2)}, u32[]{:S(2)}) collective-permute-start(f32[64,128]{1,0:T(8,128)S(1)} %get-tuple-element.97), channel_id=1, source_target_pairs={{0,4},{4,8},{8,12},{12,16},{16,20},{20,24},{24,28},{28,0},{1,5},{5... | collective-permute-start | bytes 98312 | tf_op jit(solution)/shard_map/ppermute | solution.py:620
  4.6 5.0 %collective-permute-start.1 = (f32[16,512]{1,0:T(8,128)S(1)}, f32[16,512]{1,0:T(8,128)S(1)}, u32[]{:S(2)}, u32[]{:S(2)}) collective-permute-start(f32[16,512]{1,0:T(8,128)S(1)} %fusion), channel_id=1, source_target_pairs={{0,2},{1,3},{2,0},{3,1},{4,6},{5,7},{6,4},{7,5},{8,10},{9,11},{10,... | collective-permute-start | bytes 98312 | tf_op jit(solution)/shard_map/ppermute | solution.py:617
  13.1 13.3 %collective-permute-start.5 = (f32[2,128,256]{2,1,0:T(8,128)S(1)}, f32[2,128,256]{2,1,0:T(8,128)S(1)}, u32[]{:S(2)}, u32[]{:S(2)}) collective-permute-start(f32[2,128,256]{2,1,0:T(8,128)S(1)} %get-tuple-element.120), channel_id=1, source_target_pairs={{0,12},{4,8},{8,4},{12,0},{16,28},{20,24},{24,20},{28,16},{1,13},{... | collective-permute-start | bytes 786440 | tf_op jit(solution)/shard_map/ppermute | solution.py:708
  20.3 7.9 %collective-permute-start.3 = (f32[2,128,256]{2,1,0:T(8,128)S(1)}, f32[2,128,256]{2,1,0:T(8,128)S(1)}, u32[]{:S(2)}, u32[]{:S(2)}) collective-permute-start(f32[2,128,256]{2,1,0:T(8,128)S(1)} %get-tuple-element.118), channel_id=1, source_target_pairs={{0,4},{4,0},{8,12},{12,8},{16,20},{20,16},{24,28},{28,24},{1,5},{5... | collective-permute-start | bytes 786440 | tf_op jit(solution)/shard_map/ppermute | solution.py:708
  20.9 7.5 %collective-permute-start.4 = (f32[2,128,256]{2,1,0:T(8,128)S(1)}, f32[2,128,256]{2,1,0:T(8,128)S(1)}, u32[]{:S(2)}, u32[]{:S(2)}) collective-permute-start(f32[2,128,256]{2,1,0:T(8,128)S(1)} %get-tuple-element.119), channel_id=1, source_target_pairs={{0,8},{4,12},{8,0},{12,4},{16,24},{20,28},{24,16},{28,20},{1,9},{5... | collective-permute-start | bytes 786440 | tf_op jit(solution)/shard_map/ppermute | solution.py:708
  23.2 8.6 %copy-start.1 = (bf16[512,512]{1,0:T(8,128)(2,1)S(1)}, bf16[512,512]{1,0:T(8,128)(2,1)}, u32[]{:S(2)}) copy-start(bf16[512,512]{1,0:T(8,128)(2,1)} %q_ref.5) | copy-start | bytes 1572868
  29.1 7.7 %collective-permute-start.6 = (f32[2,128,128]{2,1,0:T(8,128)S(1)}, f32[2,128,128]{2,1,0:T(8,128)S(1)}, u32[]{:S(2)}, u32[]{:S(2)}) collective-permute-start(f32[2,128,128]{2,1,0:T(8,128)S(1)} %get-tuple-element.135), channel_id=1, source_target_pairs={{0,16},{4,20},{8,24},{12,28},{16,0},{20,4},{24,8},{28,12},{1,17},{... | collective-permute-start | bytes 393224 | tf_op jit(solution)/shard_map/ppermute | solution.py:737
  37.2 7.3 %collective-permute-start.7 = (f32[2,128,128]{2,1,0:T(8,128)S(1)}, f32[2,128,128]{2,1,0:T(8,128)S(1)}, u32[]{:S(2)}, u32[]{:S(2)}) collective-permute-start(f32[2,128,128]{2,1,0:T(8,128)S(1)} %get-tuple-element.164), channel_id=1, source_target_pairs={{0,12},{4,8},{8,4},{12,0},{16,28},{20,24},{24,20},{28,16},{1,13},{... | collective-permute-start | bytes 393224 | tf_op jit(solution)/shard_map/ppermute | solution.py:747
  38.6 6.8 %collective-permute-start.8 = (f32[2,128,128]{2,1,0:T(8,128)S(1)}, f32[2,128,128]{2,1,0:T(8,128)S(1)}, u32[]{:S(2)}, u32[]{:S(2)}) collective-permute-start(f32[2,128,128]{2,1,0:T(8,128)S(1)} %get-tuple-element.165), channel_id=1, source_target_pairs={{0,4},{4,0},{8,12},{12,8},{16,20},{20,16},{24,28},{28,24},{1,5},{5... | collective-permute-start | bytes 393224 | tf_op jit(solution)/shard_map/ppermute | solution.py:747
  39.2 6.1 %collective-permute-start.9 = (f32[2,128,128]{2,1,0:T(8,128)S(1)}, f32[2,128,128]{2,1,0:T(8,128)S(1)}, u32[]{:S(2)}, u32[]{:S(2)}) collective-permute-start(f32[2,128,128]{2,1,0:T(8,128)S(1)} %get-tuple-element.166), channel_id=1, source_target_pairs={{0,8},{4,12},{8,0},{12,4},{16,24},{20,28},{24,16},{28,20},{1,9},{5... | collective-permute-start | bytes 393224 | tf_op jit(solution)/shard_map/ppermute | solution.py:747

commit v8 on v6

--- a/solution.py
+++ b/solution.py
@@ -480,7 +480,7 @@
         high_ref[at, b, here, :], low_ref[at, b, here, :] = split(reads)
 
 
-def prefix_kernel(group, *refs):
+def prefix_kernel(group, onward, *refs):
     messages, (chain_ref, leaving_ref) = refs[:group], refs[group:]
     place = lax.axis_index("seq") % group
     heads = leaving_ref.shape[0]
@@ -493,11 +493,19 @@
                 for b in range(heads):
                     chain_ref[i - 1, b] = chain[b]
                 later = messages[j ^ i]
+                if i == group - 1 and not onward:
+                    chain = [chain[b][:, :DV] for b in range(heads)]
+                    chain = [
+                        later[b, :, 0:DV] + dot_split(split(later[b, :, DV:]), split(chain[b]))
+                        for b in range(heads)
+                    ]
+                    break
                 chain = [
                     followed((later[b, :, 0:DV], later[b, :, DV:]), chain[b]) for b in range(heads)
                 ]
             for b in range(heads):
-                chain_ref[group - 1, b] = chain[b]
+                if onward:
+                    chain_ref[group - 1, b] = chain[b]
                 leaving_ref[b] = chain[b][:, :DV]
 
 
@@ -711,11 +719,12 @@
     messages[-1], rest[0] = lax.optimization_barrier((messages[-1], rest[0]))
     reads = [query(calls[0], 0, *rest[0])]
     arrived, reads = lax.optimization_barrier((arrived, reads))
+    hops = seq // group - 1
     chain, leaving = pl.pallas_call(
-        functools.partial(prefix_kernel, group),
+        functools.partial(prefix_kernel, group, hops > 1),
         in_specs=[whole()] * group,
         out_specs=[whole()] * 2,
-        out_shape=[shape(group, 2, DK, 2 * DK), shape(2, DK, DV)],
+        out_shape=[shape(group if hops > 1 else group - 1, 2, DK, 2 * DK), shape(2, DK, DV)],
         compiler_params=params(),
         name="prefix",
     )(*arrived)
@@ -731,7 +740,6 @@
             name="enter",
         )(received, chain)
 
-    hops = seq // group - 1
     if not hops:
         entering = enter(jnp.zeros((2, DK, DV), f32), False)
     for hop in range(hops):

time: 47.2 us -> 47.2 us (level)
  no operation moved by 1% of the time
where the time goes in v8:
time: 47.2 us; the launch traced here: 47 us
  Pallas kernels  25.8 us (55%)
  starting transfers between devices  14.5 us (31%)
  waiting for transfers between devices  6.36 us (13%)
    pallas_call x3, Pallas kernels, solve(): pl.pallas_call(functools.partial(solve_kernel, slots, start, group, key_w...  11.4 us
    pallas_call x2, Pallas kernels, mix(): pl.pallas_call(functools.partial(mix_kernel, slots, group, key_width), in...  4.83 us
    pallas_call x3, Pallas kernels, query(): pl.pallas_call(functools.partial(query_kernel, slots, start, group), in_s...  4.46 us
    ppermute x3, starting transfers between devices, per_device(): lax.ppermute(messages[s], 'seq', [(i, i ^ d) for i in range(seq)])  3.63 us
    ppermute x3, starting transfers between devices, per_device(): lax.ppermute(entering[d], 'seq', [(i, i ^ d) for i in range(seq)])  3.55 us
    ppermute x1, waiting for transfers between devices, per_device(): lax.ppermute(leaving, 'seq', [(i, (i + group) % seq) for i in range(seq)])  2.84 us
    ppermute x1, starting transfers between devices, per_device(): lax.ppermute(leaving, 'seq', [(i, (i + group) % seq) for i in range(seq)])  2.66 us
    pallas_call x2, Pallas kernels, outputs(): pl.pallas_call(functools.partial(output_kernel, group, [(s, where[s][1])...  2.61 us
  transfers between devices with their start and end apart: 10, of which 6 were waited for; matrix products, arithmetic and copies ran while one was open for 0% of the time, Pallas kernels for 39%

profile of v8, /device:TPU:0, one launch (start us, length us, event | category | flops | bytes accessed | tf_op | source)
XLA Modules:
  0.0 47.0 jit_solution(6273711947233712387)
XLA Ops:
  0.0 1.5 %logits.1 = (f32[2,16,512]{2,1,0:T(8,128)S(1)}, f32[2,16,512]{2,1,0:T(8,128)S(1)}, f32[64,128]{1,0:T(8,128)S(1)}, f32[24,2048]{1,0:T(8,128)S(1)}, f32[8,512]{1,0:T(8,128)S(1)}) custom-call(f32[1,8]{1,0:T(1,128)} %bitcast.6, f32[1,8]{1,0:T(1,128)} %bitcast.7, bf16[512,512]{1,0:T(8,128)(2,1)} %hidden_ref.1, bf16[64,512]{1,0:T(8,128)(2,1)} %bitcast.5, ...), custom_call_target="tpu_custom_call" | custom-call | tf_op jit(solution)/shard_map/logits/pallas_call | solution.py:602
  1.5 0.0 copy-start
  1.5 0.5 %collective-permute-start = (f32[2,16,512]{2,1,0:T(8,128)S(1)}, f32[2,16,512]{2,1,0:T(8,128)S(1)}, u32[]{:S(2)}, u32[]{:S(2)}) collective-permute-start(f32[2,16,512]{2,1,0:T(8,128)S(1)} %get-tuple-element.95), channel_id=1, source_target_pairs={{0,1},{1,0},{2,3},{3,2},{4,5},{5,4},{6,7},{7,6},{8,9},{9,8},{10,11... | collective-permute-start | bytes 196616 | tf_op jit(solution)/shard_map/ppermute | solution.py:623
  2.0 2.6 %collective-permute-start.2 = (f32[64,128]{1,0:T(8,128)S(1)}, f32[64,128]{1,0:T(8,128)S(1)}, u32[]{:S(2)}, u32[]{:S(2)}) collective-permute-start(f32[64,128]{1,0:T(8,128)S(1)} %get-tuple-element.100), channel_id=1, source_target_pairs={{0,4},{4,8},{8,12},{12,16},{16,20},{20,24},{24,28},{28,0},{1,5},{5... | collective-permute-start | bytes 98312 | tf_op jit(solution)/shard_map/ppermute | solution.py:628
  4.6 0.0 collective-permute-done.refs_2_
  4.6 1.6 %collective-permute-start.1 = (f32[16,512]{1,0:T(8,128)S(1)}, f32[16,512]{1,0:T(8,128)S(1)}, u32[]{:S(2)}, u32[]{:S(2)}) collective-permute-start(f32[16,512]{1,0:T(8,128)S(1)} %fusion), channel_id=1, source_target_pairs={{0,2},{1,3},{2,0},{3,1},{4,6},{5,7},{6,4},{7,5},{8,10},{9,11},{10,... | collective-permute-start | bytes 98312 | tf_op jit(solution)/shard_map/ppermute | solution.py:625
  6.2 3.2 %mix.2 = (f32[3,512,128]{2,1,0:T(8,128)S(1)}, f32[3,3,128,128]{3,2,1,0:T(8,128)S(1)}, f32[3,512,256]{2,1,0:T(8,128)S(1)}) custom-call(f32[24,2048]{1,0:T(8,128)S(1)} %get-tuple-element.112.edge_ref.refs_8_.refs_6_, bf16[512,512]{1,0:T(8,128)(2,1)} %k_ref.3, bf16[512,1024]{1,0:T(8,128)(2,1)} %v_ref.3), custom_call_target="tpu_custom_call" | custom-call | tf_op jit(solution)/shard_map/mix/pallas_call | solution.py:645
  9.3 0.3 collective-permute-done.2.refs_7_.refs_5_.before_ref
  9.6 3.5 %solve.3 = (f32[2,128,256]{2,1,0:T(8,128)S(1)}, f32[1,2,512,256]{3,2,1,0:T(8,128)S(1)}, f32[1,2,3,128,256]{4,3,2,1,0:T(8,128)S(1)}, f32[1,128,128]{2,1,0:T(8,128...) custom-call(f32[8,512]{1,0:T(8,128)S(1)} %get-tuple-element.93.refs_0_, ...), custom_call_target="tpu_custom_call" | custom-call | tf_op jit(solution)/shard_map/solve/pallas_call | solution.py:661
  13.1 2.4 %collective-permute-start.5 = (f32[2,128,256]{2,1,0:T(8,128)S(1)}, f32[2,128,256]{2,1,0:T(8,128)S(1)}, u32[]{:S(2)}, u32[]{:S(2)}) collective-permute-start(f32[2,128,256]{2,1,0:T(8,128)S(1)} %get-tuple-element.123), channel_id=1, source_target_pairs={{0,12},{4,8},{8,4},{12,0},{16,28},{20,24},{24,20},{28,16},{1,13},{... | collective-permute-start | bytes 786440 | tf_op jit(solution)/shard_map/ppermute | solution.py:716
  15.5 4.9 %solve.4 = (f32[2,128,256]{2,1,0:T(8,128)S(1)}, f32[2,128,256]{2,1,0:T(8,128)S(1)}, f32[2,2,512,256]{3,2,1,0:T(8,128)S(1)}, f32[2,2,3,128,256]{4,3,2,1,0:T(8,128)S(1)}, f32[2,128,128]{2,1,0:T(8,128)S(1)}) custom-call(f32[4,16,128]{2,1,0:T(8,128)S(1)} %get-tuple-element.129.refs_0_.rows_ref, f32[4,128,32]{2,1,0:T(8,128)S(1)} %get-tuple-element.130.refs_1_.columns_ref, ...), custom_call_target="tpu_custom_call" | custom-call | tf_op jit(solution)/shard_map/solve/pallas_call | solution.py:661
  20.3 0.0 copy-start.1
  20.3 0.6 %collective-permute-start.3 = (f32[2,128,256]{2,1,0:T(8,128)S(1)}, f32[2,128,256]{2,1,0:T(8,128)S(1)}, u32[]{:S(2)}, u32[]{:S(2)}) collective-permute-start(f32[2,128,256]{2,1,0:T(8,128)S(1)} %get-tuple-element.121), channel_id=1, source_target_pairs={{0,4},{4,0},{8,12},{12,8},{16,20},{20,16},{24,28},{28,24},{1,5},{5... | collective-permute-start | bytes 786440 | tf_op jit(solution)/shard_map/ppermute | solution.py:716
  20.9 0.7 %collective-permute-start.4 = (f32[2,128,256]{2,1,0:T(8,128)S(1)}, f32[2,128,256]{2,1,0:T(8,128)S(1)}, u32[]{:S(2)}, u32[]{:S(2)}) collective-permute-start(f32[2,128,256]{2,1,0:T(8,128)S(1)} %get-tuple-element.122), channel_id=1, source_target_pairs={{0,8},{4,12},{8,0},{12,4},{16,24},{20,28},{24,16},{28,20},{1,9},{5... | collective-permute-start | bytes 786440 | tf_op jit(solution)/shard_map/ppermute | solution.py:716
  21.6 1.7 %mix.3 = (f32[1,512,128]{2,1,0:T(8,128)S(1)}, f32[1,3,128,128]{3,2,1,0:T(8,128)S(1)}, f32[1,512,256]{2,1,0:T(8,128)S(1)}) custom-call(f32[24,2048]{1,0:T(8,128)S(1)} %get-tuple-element.112.edge_ref.refs_8_.refs_6_, bf16[512,512]{1,0:T(8,128)(2,1)} %k_ref.3, bf16[512,1024]{1,0:T(8,128)(2,1)} %v_ref.3), custom_call_target="tpu_custom_call" | custom-call | tf_op jit(solution)/shard_map/mix/pallas_call | solution.py:645
  23.3 3.1 %solve.5 = (f32[2,128,256]{2,1,0:T(8,128)S(1)}, f32[1,2,512,256]{3,2,1,0:T(8,128)S(1)}, f32[1,2,3,128,256]{4,3,2,1,0:T(8,128)S(1)}, f32[1,128,128]{2,1,0:T(8,128)S(1)}) custom-call(f32[4,16,128]{2,1,0:T(8,128)S(1)} %get-tuple-element.129.refs_0_.rows_ref, f32[4,128,32]{2,1,0:T(8,128)S(1)} %get-tuple-element.130.refs_1_.columns_ref, ...), custom_call_target="tpu_custom_call" | custom-call | tf_op jit(solution)/shard_map/solve/pallas_call | solution.py:661
  26.4 1.2 %query.3 = (f32[1,2,512,128]{3,2,1,0:T(8,128)S(1)}, bf16[1,2,512,128]{3,2,1,0:T(8,128)(2,1)S(1)}, bf16[1,2,512,128]{3,2,1,0:T(8,128)(2,1)S(1)}) custom-call(bf16[512,512]{1,0:T(8,128)(2,1)S(1)} %copy-done.1, f32[64,128]{1,0:T(8,128)S(1)} %collective-permute-done.2.refs_7_.refs_5_.before_ref, f32[24,2048]{1,0:T(8,128)S(1)} %get-tuple-element.112.edge_ref.refs_8_.refs_6_, ...), custom_call_target="tpu_custom_call" | custom-call | flops 2000000000 | bytes 2000000 | tf_op jit(solution)/shard_map/query/pallas_call | solution.py:681
  27.5 0.7 %collective-permute-done.3.refs_1_ = f32[2,128,256]{2,1,0:T(8,128)S(1)} collective-permute-done((f32[2,128,256]{2,1,0:T(8,128)S(1)}, f32[2,128,256]{2,1,0:T(8,128)S(1)}, u32[]{:S(2)}, u32[]{:S(2)}) %collective-permute-start.3) | collective-permute-done | bytes 262176 | tf_op jit(solution)/shard_map/ppermute | solution.py:716
  28.2 0.2 collective-permute-done.4.refs_2_
  28.4 0.7 %prefix.1 = (f32[3,2,128,256]{3,2,1,0:T(8,128)S(1)}, f32[2,128,128]{2,1,0:T(8,128)S(1)}) custom-call(f32[2,128,256]{2,1,0:T(8,128)S(1)} %get-tuple-element.136.refs_0_, f32[2,128,256]{2,1,0:T(8,128)S(1)} %collective-permute-done.3.refs_1_, f32[2,128,256]{2,1,0:T(8,128)S(1)} %collective-permute-done.4.refs_2_, f32[2,128,256]{2,1,0:T(8,128)S(1)} %collective-permute-done.5.refs_3_), custom_call_target="tpu_custom_call" | custom-call | tf_op jit(solution)/shard_map/prefix/pallas_call | solution.py:723
  29.1 2.7 %collective-permute-start.6 = (f32[2,128,128]{2,1,0:T(8,128)S(1)}, f32[2,128,128]{2,1,0:T(8,128)S(1)}, u32[]{:S(2)}, u32[]{:S(2)}) collective-permute-start(f32[2,128,128]{2,1,0:T(8,128)S(1)} %get-tuple-element.147), channel_id=1, source_target_pairs={{0,16},{4,20},{8,24},{12,28},{16,0},{20,4},{24,8},{28,12},{1,17},{... | collective-permute-start | bytes 393224 | tf_op jit(solution)/shard_map/ppermute | solution.py:746
  31.8 2.2 %query.4 = (f32[2,2,512,128]{3,2,1,0:T(8,128)S(1)}, bf16[2,2,512,128]{3,2,1,0:T(8,128)(2,1)S(1)}, bf16[2,2,512,128]{3,2,1,0:T(8,128)(2,1)S(1)}) custom-call(bf16[512,512]{1,0:T(8,128)(2,1)S(1)} %copy-done.1, f32[64,128]{1,0:T(8,128)S(1)} %collective-permute-done.2.refs_7_.refs_5_.before_ref, f32[24,2048]{1,0:T(8,128)S(1)} %get-tuple-element.112.edge_ref.refs_8_.refs_6_, ...), custom_call_target="tpu_custom_call" | custom-call | flops 4000000000 | bytes 4000000 | tf_op jit(solution)/shard_map/query/pallas_call | solution.py:681
  34.0 2.8 %collective-permute-done.6.entering_ref = f32[2,128,128]{2,1,0:T(8,128)S(1)} collective-permute-done((f32[2,128,128]{2,1,0:T(8,128)S(1)}, f32[2,128,128]{2,1,0:T(8,128)S(1)}, u32[]{:S(2)}, u32[]{:S(2)}) %collective-permute-start.6) | collective-permute-done | bytes 131104 | tf_op jit(solution)/shard_map/ppermute | solution.py:746
  36.8 0.4 enter.1
  37.2 1.4 %collective-permute-start.7 = (f32[2,128,128]{2,1,0:T(8,128)S(1)}, f32[2,128,128]{2,1,0:T(8,128)S(1)}, u32[]{:S(2)}, u32[]{:S(2)}) collective-permute-start(f32[2,128,128]{2,1,0:T(8,128)S(1)} %get-tuple-element.170), channel_id=1, source_target_pairs={{0,12},{4,8},{8,4},{12,0},{16,28},{20,24},{24,20},{28,16},{1,13},{... | collective-permute-start | bytes 393224 | tf_op jit(solution)/shard_map/ppermute | solution.py:756
  38.5 0.6 %collective-permute-start.8 = (f32[2,128,128]{2,1,0:T(8,128)S(1)}, f32[2,128,128]{2,1,0:T(8,128)S(1)}, u32[]{:S(2)}, u32[]{:S(2)}) collective-permute-start(f32[2,128,128]{2,1,0:T(8,128)S(1)} %get-tuple-element.171), channel_id=1, source_target_pairs={{0,4},{4,0},{8,12},{12,8},{16,20},{20,16},{24,28},{28,24},{1,5},{5... | collective-permute-start | bytes 393224 | tf_op jit(solution)/shard_map/ppermute | solution.py:756
  39.2 1.5 %collective-permute-start.9 = (f32[2,128,128]{2,1,0:T(8,128)S(1)}, f32[2,128,128]{2,1,0:T(8,128)S(1)}, u32[]{:S(2)}, u32[]{:S(2)}) collective-permute-start(f32[2,128,128]{2,1,0:T(8,128)S(1)} %get-tuple-element.172), channel_id=1, source_target_pairs={{0,8},{4,12},{8,0},{12,4},{16,24},{20,28},{24,16},{28,20},{1,9},{5... | collective-permute-start | bytes 393224 | tf_op jit(solution)/shard_map/ppermute | solution.py:756
  40.7 1.1 %query.5 = (f32[1,2,512,128]{3,2,1,0:T(8,128)S(1)}, bf16[1,2,512,128]{3,2,1,0:T(8,128)(2,1)S(1)}, bf16[1,2,512,128]{3,2,1,0:T(8,128)(2,1)S(1)}) custom-call(bf16[512,512]{1,0:T(8,128)(2,1)S(1)} %copy-done.1, f32[64,128]{1,0:T(8,128)S(1)} %collective-permute-done.2.refs_7_.refs_5_.before_ref, f32[24,2048]{1,0:T(8,128)S(1)} %get-tuple-element.112.edge_ref.refs_8_.refs_6_, ...), custom_call_target="tpu_custom_call" | custom-call | flops 2000000000 | bytes 2000000 | tf_op jit(solution)/shard_map/query/pallas_call | solution.py:681
  41.8 1.1 %outputs.2.refs_12_ = f32[512,1024]{1,0:T(8,128)} custom-call(f32[1,2,512,128]{3,2,1,0:T(8,128)S(1)} %get-tuple-element.177.refs_0_, bf16[1,2,512,128]{3,2,1,0:T(8,128)(2,1)S(1)} %get-tuple-element.178.refs_1_, bf16[1,2,512,128]{3,2,1,0:T(8,128)(2,1)S(1)} %get-tuple-element.179.refs_2_, f32[2,128,128]{2,1,0:T(8,128)S(1)} %get-tuple-element.180.refs_3_), custom_call_target="tpu_custom_call" | custom-call | tf_op jit(solution)/shard_map/outputs/pallas_call | solution.py:763
  43.0 1.5 %collective-permute-done.7.refs_9_ = f32[2,128,128]{2,1,0:T(8,128)S(1)} collective-permute-done((f32[2,128,128]{2,1,0:T(8,128)S(1)}, f32[2,128,128]{2,1,0:T(8,128)S(1)}, u32[]{:S(2)}, u32[]{:S(2)}) %collective-permute-start.7) | collective-permute-done | bytes 131104 | tf_op jit(solution)/shard_map/ppermute | solution.py:756
  44.5 0.8 %collective-permute-done.8.refs_10_ = f32[2,128,128]{2,1,0:T(8,128)S(1)} collective-permute-done((f32[2,128,128]{2,1,0:T(8,128)S(1)}, f32[2,128,128]{2,1,0:T(8,128)S(1)}, u32[]{:S(2)}, u32[]{:S(2)}) %collective-permute-start.8) | collective-permute-done | bytes 131104 | tf_op jit(solution)/shard_map/ppermute | solution.py:756
  45.3 1.5 %outputs.3 = f32[512,1024]{1,0:T(8,128)} custom-call(f32[1,2,512,128]{3,2,1,0:T(8,128)S(1)} %get-tuple-element.162.refs_0_, bf16[1,2,512,128]{3,2,1,0:T(8,128)(2,1)S(1)} %get-tuple-element.163.refs_1_, bf16[1,2,512,128]{3,2,1,0:T(8,128)(2,1)S(1)} %get-tuple-element.164.refs_2_, ...), custom_call_target="tpu_custom_call", output_to_operand_aliasing={{}: (12, {})} | custom-call | tf_op jit(solution)/shard_map/outputs/pallas_call | solution.py:763
  (6 shorter events, 0.0 us)
Async XLA Ops:
  1.5 8.1 %copy-start = (bf16[256,1920]{1,0:T(8,128)(2,1)S(1)}, bf16[256,1920]{1,0:T(8,128)(2,1)}, u32[]{:S(2)}) copy-start(bf16[256,1920]{1,0:T(8,128)(2,1)} %constant.2.clone.refs_9_.refs_7_) | copy-start | bytes 2949124
  1.5 3.1 %collective-permute-start = (f32[2,16,512]{2,1,0:T(8,128)S(1)}, f32[2,16,512]{2,1,0:T(8,128)S(1)}, u32[]{:S(2)}, u32[]{:S(2)}) collective-permute-start(f32[2,16,512]{2,1,0:T(8,128)S(1)} %get-tuple-element.95), channel_id=1, source_target_pairs={{0,1},{1,0},{2,3},{3,2},{4,5},{5,4},{6,7},{7,6},{8,9},{9,8},{10,11... | collective-permute-start | bytes 196616 | tf_op jit(solution)/shard_map/ppermute | solution.py:623
  2.0 7.6 %collective-permute-start.2 = (f32[64,128]{1,0:T(8,128)S(1)}, f32[64,128]{1,0:T(8,128)S(1)}, u32[]{:S(2)}, u32[]{:S(2)}) collective-permute-start(f32[64,128]{1,0:T(8,128)S(1)} %get-tuple-element.100), channel_id=1, source_target_pairs={{0,4},{4,8},{8,12},{12,16},{16,20},{20,24},{24,28},{28,0},{1,5},{5... | collective-permute-start | bytes 98312 | tf_op jit(solution)/shard_map/ppermute | solution.py:628
  4.6 5.0 %collective-permute-start.1 = (f32[16,512]{1,0:T(8,128)S(1)}, f32[16,512]{1,0:T(8,128)S(1)}, u32[]{:S(2)}, u32[]{:S(2)}) collective-permute-start(f32[16,512]{1,0:T(8,128)S(1)} %fusion), channel_id=1, source_target_pairs={{0,2},{1,3},{2,0},{3,1},{4,6},{5,7},{6,4},{7,5},{8,10},{9,11},{10,... | collective-permute-start | bytes 98312 | tf_op jit(solution)/shard_map/ppermute | solution.py:625
  13.1 14.5 %collective-permute-start.5 = (f32[2,128,256]{2,1,0:T(8,128)S(1)}, f32[2,128,256]{2,1,0:T(8,128)S(1)}, u32[]{:S(2)}, u32[]{:S(2)}) collective-permute-start(f32[2,128,256]{2,1,0:T(8,128)S(1)} %get-tuple-element.123), channel_id=1, source_target_pairs={{0,12},{4,8},{8,4},{12,0},{16,28},{20,24},{24,20},{28,16},{1,13},{... | collective-permute-start | bytes 786440 | tf_op jit(solution)/shard_map/ppermute | solution.py:716
  20.3 6.0 %copy-start.1 = (bf16[512,512]{1,0:T(8,128)(2,1)S(1)}, bf16[512,512]{1,0:T(8,128)(2,1)}, u32[]{:S(2)}) copy-start(bf16[512,512]{1,0:T(8,128)(2,1)} %q_ref.5) | copy-start | bytes 1572868
  20.3 7.9 %collective-permute-start.3 = (f32[2,128,256]{2,1,0:T(8,128)S(1)}, f32[2,128,256]{2,1,0:T(8,128)S(1)}, u32[]{:S(2)}, u32[]{:S(2)}) collective-permute-start(f32[2,128,256]{2,1,0:T(8,128)S(1)} %get-tuple-element.121), channel_id=1, source_target_pairs={{0,4},{4,0},{8,12},{12,8},{16,20},{20,16},{24,28},{28,24},{1,5},{5... | collective-permute-start | bytes 786440 | tf_op jit(solution)/shard_map/ppermute | solution.py:716
  20.9 7.5 %collective-permute-start.4 = (f32[2,128,256]{2,1,0:T(8,128)S(1)}, f32[2,128,256]{2,1,0:T(8,128)S(1)}, u32[]{:S(2)}, u32[]{:S(2)}) collective-permute-start(f32[2,128,256]{2,1,0:T(8,128)S(1)} %get-tuple-element.122), channel_id=1, source_target_pairs={{0,8},{4,12},{8,0},{12,4},{16,24},{20,28},{24,16},{28,20},{1,9},{5... | collective-permute-start | bytes 786440 | tf_op jit(solution)/shard_map/ppermute | solution.py:716
  29.1 7.7 %collective-permute-start.6 = (f32[2,128,128]{2,1,0:T(8,128)S(1)}, f32[2,128,128]{2,1,0:T(8,128)S(1)}, u32[]{:S(2)}, u32[]{:S(2)}) collective-permute-start(f32[2,128,128]{2,1,0:T(8,128)S(1)} %get-tuple-element.147), channel_id=1, source_target_pairs={{0,16},{4,20},{8,24},{12,28},{16,0},{20,4},{24,8},{28,12},{1,17},{... | collective-permute-start | bytes 393224 | tf_op jit(solution)/shard_map/ppermute | solution.py:746
  37.2 7.3 %collective-permute-start.7 = (f32[2,128,128]{2,1,0:T(8,128)S(1)}, f32[2,128,128]{2,1,0:T(8,128)S(1)}, u32[]{:S(2)}, u32[]{:S(2)}) collective-permute-start(f32[2,128,128]{2,1,0:T(8,128)S(1)} %get-tuple-element.170), channel_id=1, source_target_pairs={{0,12},{4,8},{8,4},{12,0},{16,28},{20,24},{24,20},{28,16},{1,13},{... | collective-permute-start | bytes 393224 | tf_op jit(solution)/shard_map/ppermute | solution.py:756
  38.5 6.8 %collective-permute-start.8 = (f32[2,128,128]{2,1,0:T(8,128)S(1)}, f32[2,128,128]{2,1,0:T(8,128)S(1)}, u32[]{:S(2)}, u32[]{:S(2)}) collective-permute-start(f32[2,128,128]{2,1,0:T(8,128)S(1)} %get-tuple-element.171), channel_id=1, source_target_pairs={{0,4},{4,0},{8,12},{12,8},{16,20},{20,16},{24,28},{28,24},{1,5},{5... | collective-permute-start | bytes 393224 | tf_op jit(solution)/shard_map/ppermute | solution.py:756
  39.2 6.2 %collective-permute-start.9 = (f32[2,128,128]{2,1,0:T(8,128)S(1)}, f32[2,128,128]{2,1,0:T(8,128)S(1)}, u32[]{:S(2)}, u32[]{:S(2)}) collective-permute-start(f32[2,128,128]{2,1,0:T(8,128)S(1)} %get-tuple-element.172), channel_id=1, source_target_pairs={{0,8},{4,12},{8,0},{12,4},{16,24},{20,28},{24,16},{28,20},{1,9},{5... | collective-permute-start | bytes 393224 | tf_op jit(solution)/shard_map/ppermute | solution.py:756
